TPU v7x, 32 devices: a whole 2x2x4 slice. The times are simulated.
32 devices in a mesh: groups: 2 (over x), pb: 16 (over z, y, core).
Axes of the slice: x: 2, y: 2, z: 4, core: 2. Of those that a mesh axis runs over, the one named last changes fastest.
Arguments:
- hidden: bfloat16 [8192, 4096], P(('groups', 'pb')), parts along dimension 0, may hold values from -6 to 6
- final_gain: bfloat16 [4096], replicated, may hold values from 0.099609375 to 1.8984375
- last_row: int32 [32, 256], P(('groups', 'pb')), parts along dimension 0, may hold values from 0 to 255, each once within a row
- pair_owner: int32 [4096, 2], P(('groups', 'pb')), parts along dimension 0, may hold values from 0 to 4095, as said below
- hard_negatives: int32 [32, 4], P(('groups', 'pb')), parts along dimension 0, may hold values from -1 to 15, as said below
Outputs:
- pooled_grad: float32 [8192, 4096], P(('groups', 'pb')), parts along dimension 0
- block_loss: float32 [32], P(('groups', 'pb')), parts along dimension 0
There are 2 independent parts, one for each index of `groups`. A program takes and returns all parts, laid end to end along the dimension named above; an argument that names none is the same for every part. Nothing has to cross between parts.
Inputs may be any that keep to these rules, and one draw needn't show every extreme that they name: `last_row`: each device's row names each of its 256 rows once. `pair_owner`: every global sequence index is named exactly once. The 128 pairs of one query block name at most 32 sequences of any one device, and exactly 32 of some device. `hard_negatives`: entry r of query block j is -1 or block (j + r + 1) mod 16. Every row names at least one block, and some row names all 4.
All inputs are finite; a program needn't handle non-finite values.
Results may differ from a plain program's by a relative error of at most 0.006.
Values may be sent and summed in bfloat16 or wider, within the bound.
No kernel may reach another device: no remote copies, remote signals or barrier semaphores. Data moves between devices by JAX's collectives and lax.ppermute only.
A program may use at most 128 MiB of HBM per device.

v0:
```python
import functools

import jax
import jax.numpy as jnp
from jax import lax
from jax.experimental import pallas as pl
from jax.experimental.pallas import tpu as pltpu
from jax.sharding import PartitionSpec as P

inverse_temp = 50.0
token_eps = 1e-05
unit_eps = 1e-06
lanes = 128
bound_steps = 256.0
code_steps = 32000.0
mebibyte = 1024 * 1024


def spread(target, at, value):
    count = value.shape[0]
    for half in range(2):
        target[pl.ds(2 * at + half, count, stride=2), :] = value[:, half * lanes : (half + 1) * lanes]


def gathered(source, at, count):
    halves = [source[pl.ds(2 * at + half, count, stride=2), :] for half in range(2)]
    return jnp.concatenate(halves, axis=1)


def row_pair(index):
    return pl.ds(pl.multiple_of(2 * index, 2), 2)


def norm_kernel(
    last_ref, hidden_ref, gain_ref, owner_ref, negative_ref, normed_ref, inv_ref, emb_ref
):
    seqs, width = normed_ref.shape
    parts, _, piece = emb_ref.shape
    pairs = owner_ref.shape[1]
    cuts = [slice(part * piece, (part + 1) * piece) for part in range(parts)]
    sources = lax.broadcasted_iota(jnp.int32, (seqs, seqs), 0)
    pick = jnp.where(sources == last_ref[...], 1.0, 0.0).astype(jnp.bfloat16)

    def folded(squares):
        return functools.reduce(
            jnp.add, [squares[:, at : at + lanes] for at in range(0, piece, lanes)]
        )

    total = jnp.zeros((seqs, lanes), jnp.float32)
    for cut in cuts:
        values = lax.dot_general(
            pick, hidden_ref[:, cut], (((0,), (0,)), ((), ())), preferred_element_type=jnp.float32
        )
        normed_ref[:, cut] = values.astype(jnp.bfloat16)
        total = total + folded(values * values)
    scale = lax.rsqrt(jnp.sum(total, axis=-1, keepdims=True) / width + token_eps)
    total = jnp.zeros((seqs, lanes), jnp.float32)
    for cut in cuts:
        values = normed_ref[:, cut].astype(jnp.float32)
        gain = gain_ref[cut].astype(jnp.float32).reshape(1, piece)
        normed = (values * scale * gain).astype(jnp.bfloat16)
        normed_ref[:, cut] = normed
        pooled = normed.astype(jnp.float32)
        total = total + folded(pooled * pooled)
    inverse = lax.rsqrt(jnp.sum(total, axis=-1, keepdims=True) + unit_eps)
    inv_ref[...] = jnp.broadcast_to(inverse, inv_ref.shape)

    owners = owner_ref[...].astype(jnp.float32)
    high = jnp.floor(owners * (1.0 / 256.0))
    low = owners - 256.0 * high
    row = lax.broadcasted_iota(jnp.int32, (16, pairs), 0)
    spot = lax.broadcasted_iota(jnp.int32, (16, pairs), 1)
    left = jnp.where(row == 0, low[:1], jnp.where(row == 1, high[:1], 0.0))
    right = jnp.where(row == 0, low[1:2], jnp.where(row == 1, high[1:2], 0.0))
    for offset in range(negative_ref.shape[1]):
        named = (negative_ref[0, offset] >= 0).astype(jnp.float32)
        left = jnp.where((row == 2) & (spot == offset), named, left)
    facts = jnp.concatenate([left, right], axis=1).astype(jnp.bfloat16)

    for part, cut in enumerate(cuts):
        emb_ref[part, :seqs] = (normed_ref[:, cut].astype(jnp.float32) * inverse).astype(jnp.bfloat16)
        emb_ref[part, seqs:] = facts


def norm_call(last_row, hidden, gain, owners, hard_negatives, parts):
    seqs, width = hidden.shape
    piece = width // parts
    whole = pl.BlockSpec(memory_space=pltpu.VMEM)
    return pl.pallas_call(
        norm_kernel,
        in_specs=[whole, whole, whole, whole, pl.BlockSpec(memory_space=pltpu.SMEM)],
        out_specs=[whole] * 3,
        out_shape=[
            jax.ShapeDtypeStruct((seqs, width), jnp.bfloat16),
            jax.ShapeDtypeStruct((seqs, lanes), jnp.float32),
            jax.ShapeDtypeStruct((parts, seqs + 16, piece), jnp.bfloat16),
        ],
        compiler_params=pltpu.CompilerParams(vmem_limit_bytes=56 * mebibyte),
        name="norm_rows",
    )(last_row, hidden, gain, owners, hard_negatives)


def score_kernel(
    blocks,
    pairs,
    window,
    *refs,
):
    emb_ref, q_ref, d_ref, mine_ref, other_ref, top_ref, own_ref, place_ref = refs[:-7]
    wide, picked, picked_too, facts, own, named, sems = refs[-7:]
    seqs = emb_ref.shape[1] - 16
    sent = emb_ref[:, seqs:, :].astype(jnp.float32)
    own_ref[...] = (sent[:, 0, :] + 256.0 * sent[:, 1, :]).astype(jnp.int32)
    facts[...] = sent[:, 2, :lanes].astype(jnp.int32)
    fetches = [
        pltpu.make_async_copy(own_ref, own, sems.at[0]),
        pltpu.make_async_copy(facts, named, sems.at[1]),
    ]
    for fetch in fetches:
        fetch.start()

    for part in range(blocks):
        spread(wide, part * seqs, emb_ref[part, :seqs, :].astype(jnp.float32))
    for fetch in fetches:
        fetch.wait()

    def place(block, count):
        place_ref[0, block] = block
        for offset in range(window):
            present = named[block, offset] > 0
            place_ref[offset + 1, block] = jnp.where(present, count, -1)
            count = count + present.astype(jnp.int32)
        return count

    used = lax.fori_loop(0, blocks, place, blocks)
    fine = pairs // blocks

    def clear(spot, carry):
        empty = jnp.zeros((blocks // 2, fine, pairs), jnp.float32)
        at = pl.ds(pl.multiple_of(spot * fine, fine), fine)
        mine_ref[:, at, :] = empty
        other_ref[:, at, :] = empty
        return carry

    lax.fori_loop(used, mine_ref.shape[1] // fine, clear, 0)
    group = 32

    def pick_block(block, rows_at):
        for base in range(0, 2 * pairs, group):
            rows = [wide[row_pair(own[block, base + k]), :] for k in range(group)]
            for k in range(group):
                rows_at[2 * (base + k) : 2 * (base + k + 1), :] = rows[k]
        at = pl.multiple_of(block * pairs, pairs)
        q_ref[pl.ds(at, pairs), :] = gathered(rows_at, 0, pairs).astype(jnp.bfloat16)
        d_ref[pl.ds(at, pairs), :] = gathered(rows_at, pairs, pairs).astype(jnp.bfloat16)

    ahead = -(-(window + 2) // 2)

    def pick_one(block, carry):
        pick_block(block, picked)
        return carry

    lax.fori_loop(0, 2 * ahead, pick_one, 0)
    even = lax.axis_index("pb") % 2 == 0
    spare = mine_ref.shape[1] // fine - 1

    def score_blocks(step, carry):
        at = pl.multiple_of(step * 2 * pairs, 2 * pairs)
        tiles = inverse_temp * lax.dot_general(
            q_ref[pl.ds(at, 2 * pairs), :],
            d_ref[pl.ds(at, (window + 2) * pairs), :],
            (((1,), (1,)), ((), ())),
            preferred_element_type=jnp.float32,
        )
        top = carry
        for half in range(2):
            for column in range(window + 1):
                spot = place_ref[column, 2 * step + half]
                row = pl.multiple_of(jnp.where(spot >= 0, spot, spare) * fine, fine)
                tile = tiles[
                    half * pairs : (half + 1) * pairs,
                    (half + column) * pairs : (half + column + 1) * pairs,
                ]
                parted = tile.reshape(blocks // 2, 2, fine, pairs)
                first, second = parted[:, 0], parted[:, 1]
                mine_ref[:, pl.ds(row, fine), :] = jnp.where(even, first, second)
                other_ref[:, pl.ds(row, fine), :] = jnp.where(even, second, first)
                size = jnp.maximum(jnp.abs(first), jnp.abs(second))
                top = jnp.maximum(top, jnp.max(size, axis=0))
        return top

    def score_and_pick(step, top):
        top = score_blocks(step - ahead, top)
        pick_block(2 * step, picked)
        pick_block(2 * step + 1, picked_too)
        return top

    top = jnp.zeros((fine, pairs), jnp.float32)
    top = lax.fori_loop(ahead, blocks // 2, score_and_pick, top)
    d_ref[blocks * pairs :, :] = d_ref[: window * pairs, :]
    top_ref[...] = lax.fori_loop(blocks // 2 - ahead, blocks // 2, score_blocks, top)


def score_call(embedded, room, blocks, pairs, window):
    _, rows, piece = embedded.shape
    fine = pairs // blocks
    whole = pl.BlockSpec(memory_space=pltpu.VMEM)
    scalars = pl.BlockSpec(memory_space=pltpu.SMEM)
    return pl.pallas_call(
        functools.partial(score_kernel, blocks, pairs, window),
        in_specs=[whole],
        out_specs=[whole, whole, whole, whole, whole, whole, scalars],
        out_shape=[
            jax.ShapeDtypeStruct((blocks * pairs, piece), jnp.bfloat16),
            jax.ShapeDtypeStruct(((blocks + window) * pairs, piece), jnp.bfloat16),
            jax.ShapeDtypeStruct((blocks // 2, (room + 1) * fine, pairs), jnp.float32),
            jax.ShapeDtypeStruct((blocks // 2, (room + 1) * fine, pairs), jnp.float32),
            jax.ShapeDtypeStruct((fine, pairs), jnp.float32),
            jax.ShapeDtypeStruct((blocks, 2 * pairs), jnp.int32),
            jax.ShapeDtypeStruct((window + 1, blocks), jnp.int32),
        ],
        scratch_shapes=[
            pltpu.VMEM((2 * blocks * (rows - 16), lanes), jnp.float32),
            pltpu.VMEM((4 * pairs, lanes), jnp.float32),
            pltpu.VMEM((4 * pairs, lanes), jnp.float32),
            pltpu.VMEM((blocks, lanes), jnp.int32),
            pltpu.SMEM((blocks, 2 * pairs), jnp.int32),
            pltpu.SMEM((blocks, lanes), jnp.int32),
            pltpu.SemaphoreType.DMA((2,)),
        ],
        compiler_params=pltpu.CompilerParams(vmem_limit_bytes=22 * mebibyte),
        name="partial_scores",
    )(embedded)


def merge_kernel(mine_ref, other_ref, top_ref, other_top_ref, own_ref, *code_refs):
    rows, pairs = own_ref.shape
    steps = code_refs[0].shape[0] - 1
    fine = rows // steps // 2
    chip = lax.axis_index("pb") // 2

    def highest(ref):
        return jnp.max(jnp.max(ref[...], axis=1, keepdims=True), axis=0, keepdims=True)

    top = highest(top_ref) + highest(other_top_ref)
    bound = jnp.ceil(top * bound_steps) + 1.0
    scale = code_steps * bound_steps / bound
    own_ref[...] = mine_ref[chip, :rows] + other_ref[chip, :rows]
    for hop, code_ref in enumerate(code_refs):
        target = chip ^ (hop + 1)

        def encode(step, carry):
            at = pl.multiple_of(step * 2 * fine, 2 * fine)
            there = pl.ds(at, 2 * fine)
            codes = jnp.round((mine_ref[target, there, :] + other_ref[target, there, :]) * scale)
            code_ref[step] = codes.astype(jnp.int32).astype(jnp.int16)
            return carry

        lax.fori_loop(0, steps, encode, 0)
        code_ref[steps] = jnp.broadcast_to(bound, (2 * fine, pairs)).astype(jnp.int32).astype(jnp.int16)


def merge_call(mine, other, top, other_top, blocks):
    chips, rows, pairs = mine.shape
    fine = pairs // blocks
    rows = rows - fine
    whole = pl.BlockSpec(memory_space=pltpu.VMEM)
    coded = jax.ShapeDtypeStruct((rows // (2 * fine) + 1, 2 * fine, pairs), jnp.int16)
    return pl.pallas_call(
        merge_kernel,
        in_specs=[whole] * 4,
        out_specs=[whole] * chips,
        out_shape=[jax.ShapeDtypeStruct((rows, pairs), jnp.float32)] + [coded] * (chips - 1),
        compiler_params=pltpu.CompilerParams(vmem_limit_bytes=12 * mebibyte),
        name="merge_scores",
    )(mine, other, top, other_top)


def softmax_kernel(blocks, window, place_ref, own_ref, *refs):
    code_refs, (c_ref, packed, masked) = refs[:-3], refs[-3:]
    room, fine, pairs = packed.shape
    count = blocks * fine
    unit = 1.0 / (code_steps * bound_steps)
    scales = [ref[room // 2].astype(jnp.int32).astype(jnp.float32) * unit for ref in code_refs]

    def decode(step, carry):
        both = own_ref[pl.ds(pl.multiple_of(step * 2 * fine, 2 * fine), 2 * fine), :]
        for ref, scale in zip(code_refs, scales):
            both = both + ref[step].astype(jnp.int32).astype(jnp.float32) * scale
        packed[2 * step] = both[:fine]
        packed[2 * step + 1] = both[fine:]
        return carry

    lax.fori_loop(0, room // 2, decode, 0)
    for block in range(blocks):
        for column in range(window + 1):
            spot = place_ref[column, block]
            tile = packed[jnp.maximum(spot, 0)]
            masked[block * fine : (block + 1) * fine, column * pairs : (column + 1) * pairs] = (
                jnp.where(spot >= 0, tile, -jnp.inf)
            )
    row = lax.broadcasted_iota(jnp.int32, (count, pairs), 0)
    lane = lax.broadcasted_iota(jnp.int32, (count, pairs), 1)
    target = lane == lax.axis_index("pb") * fine + row % fine
    pieces = [masked[:, column * pairs : (column + 1) * pairs] for column in range(window + 1)]
    row_max = jnp.max(functools.reduce(jnp.maximum, pieces), axis=1, keepdims=True)
    total = functools.reduce(jnp.add, [jnp.exp(piece - row_max) for piece in pieces])
    log_total = row_max + jnp.log(jnp.sum(total, axis=1, keepdims=True))
    positive = jnp.sum(jnp.where(target, pieces[0], 0.0), axis=1, keepdims=True)
    for column, piece in enumerate(pieces):
        share = jnp.exp(piece - log_total)
        if column == 0:
            share = share - jnp.where(target, 1.0, 0.0)
        masked[:, column * pairs : (column + 1) * pairs] = inverse_temp * share
    for block in range(blocks):
        for column in range(window + 1):
            spot = place_ref[column, block]

            @pl.when(spot >= 0)
            def _():
                packed[spot] = masked[
                    block * fine : (block + 1) * fine, column * pairs : (column + 1) * pairs
                ]

    for step in range(room // 2):
        both = jnp.concatenate([packed[2 * step], packed[2 * step + 1]], axis=0)
        c_ref[step] = both.astype(jnp.bfloat16)
    losses = jnp.sum(
        jnp.where(lane == row // fine, log_total - positive, 0.0), axis=0, keepdims=True
    )
    coarse = losses.astype(jnp.bfloat16).astype(jnp.float32)
    rank = lax.broadcasted_iota(jnp.int32, (2 * fine, pairs), 0)
    both = jnp.where(rank == 0, coarse, jnp.where(rank == 1, losses - coarse, 0.0))
    c_ref[room // 2] = both.astype(jnp.bfloat16)


def softmax_call(place, own_scores, codes, blocks, window):
    steps, fine, pairs = codes[0].shape
    room, fine = 2 * (steps - 1), fine // 2
    whole = pl.BlockSpec(memory_space=pltpu.VMEM)
    return pl.pallas_call(
        functools.partial(softmax_kernel, blocks, window),
        in_specs=[pl.BlockSpec(memory_space=pltpu.SMEM), whole] + [whole] * len(codes),
        out_specs=whole,
        out_shape=jax.ShapeDtypeStruct((room // 2 + 1, 2 * fine, pairs), jnp.bfloat16),
        scratch_shapes=[
            pltpu.VMEM((room, fine, pairs), jnp.float32),
            pltpu.VMEM((blocks * fine, (window + 1) * pairs), jnp.float32),
        ],
        compiler_params=pltpu.CompilerParams(vmem_limit_bytes=8 * mebibyte),
        name="softmax_rows",
    )(place, own_scores, *codes)


def grad_kernel(
    blocks,
    pairs,
    window,
    own_ref,
    place_ref,
    q_ref,
    d_ref,
    *refs,
):
    part_refs = refs[:-7]
    out_ref, loss_ref, wide, dsum, picked, packed, square = refs[-7:]
    fine = pairs // blocks
    room = packed.shape[1]
    me = lax.axis_index("pb")
    masks = swap_masks(blocks)
    group = 32
    losses = 0.0
    for part in part_refs:
        sent = part[:, room // 2].astype(jnp.float32)
        losses = losses + jnp.sum(sent[:, 0, :] + sent[:, 1, :], axis=0, keepdims=True) / pairs
    lane = lax.broadcasted_iota(jnp.int32, losses.shape, 1)
    mine = jnp.where(lane == me, losses, 0.0)
    loss_ref[...] = jnp.broadcast_to(jnp.sum(mine, axis=1, keepdims=True), loss_ref.shape)
    dsum[...] = jnp.zeros_like(dsum)
    square[...] = jnp.zeros_like(square)

    def unpack(step, carry):
        for part, mask in zip(part_refs, masks):
            both = part[:, step].astype(jnp.float32)
            for at, apart in enumerate(mask):
                packed[me ^ apart, 2 * step] = both[at, :fine]
                packed[me ^ apart, 2 * step + 1] = both[at, fine:]
        return carry

    lax.fori_loop(0, room // 2, unpack, 0)

    def scatter_rows(block, offset, start):
        for base in range(0, pairs, group):
            rows = [
                picked[2 * (start + base + k) : 2 * (start + base + k + 1), :] for k in range(group)
            ]
            for k in range(group):
                wide[row_pair(own_ref[block, offset + base + k]), :] = rows[k]

    def two_blocks(step, carry):
        for half in range(2):
            for column in range(window + 1):
                spot = place_ref[column, 2 * step + half]
                tile = packed[:, jnp.maximum(spot, 0)].reshape(pairs, pairs)
                square[
                    half * pairs : (half + 1) * pairs,
                    (half + column) * pairs : (half + column + 1) * pairs,
                ] = jnp.where(spot >= 0, tile, 0.0).astype(jnp.bfloat16)
        at = pl.multiple_of(step * 2 * pairs, 2 * pairs)
        there = pl.ds(at, (window + 2) * pairs)
        coefficients = square[...]
        summed = jnp.dot(coefficients, d_ref[there, :], preferred_element_type=jnp.float32)
        spread(picked, 0, summed)
        dsum[there, :] += lax.dot_general(
            coefficients,
            q_ref[pl.ds(at, 2 * pairs), :],
            (((0,), (0,)), ((), ())),
            preferred_element_type=jnp.float32,
        )
        for half in range(2):
            scatter_rows(2 * step + half, 0, half * pairs)
        return carry

    lax.fori_loop(0, blocks // 2, two_blocks, 0)
    dsum[: window * pairs, :] += dsum[blocks * pairs :, :]

    def doc_block(block, carry):
        at = pl.multiple_of(block * pairs, pairs)
        spread(picked, 0, dsum[pl.ds(at, pairs), :])
        scatter_rows(block, pairs, 0)
        return carry

    lax.fori_loop(0, blocks, doc_block, 0)
    slots = out_ref.shape[1]
    for part in range(blocks):
        out_ref[part] = gathered(wide, part * slots, slots).astype(jnp.bfloat16)


def grad_call(own, place, parts, queries, documents, blocks, pairs, window):
    count, piece = queries.shape
    seqs = 2 * count
    room = 2 * (parts[0].shape[1] - 1)
    whole = pl.BlockSpec(memory_space=pltpu.VMEM)
    scalars = pl.BlockSpec(memory_space=pltpu.SMEM)
    return pl.pallas_call(
        functools.partial(grad_kernel, blocks, pairs, window),
        in_specs=[scalars, scalars, whole, whole] + [whole] * len(parts),
        out_specs=[whole, whole],
        out_shape=[
            jax.ShapeDtypeStruct((blocks, seqs // blocks, piece), jnp.bfloat16),
            jax.ShapeDtypeStruct((1, lanes), jnp.float32),
        ],
        scratch_shapes=[
            pltpu.VMEM((2 * seqs, lanes), jnp.float32),
            pltpu.VMEM(((blocks + window) * pairs, piece), jnp.float32),
            pltpu.VMEM((4 * pairs, lanes), jnp.float32),
            pltpu.VMEM((blocks, room, pairs // blocks, pairs), jnp.float32),
            pltpu.VMEM((2 * pairs, (window + 2) * pairs), jnp.bfloat16),
        ],
        compiler_params=pltpu.CompilerParams(vmem_limit_bytes=26 * mebibyte),
        name="slice_grads",
    )(own, place, queries, documents, *parts)


def project_kernel(grad_ref, normed_ref, inv_ref, out_ref):
    parts, _, piece = grad_ref.shape
    cuts = [slice(part * piece, (part + 1) * piece) for part in range(parts)]
    inverse = inv_ref[:, :1]
    total = 0.0
    for part, cut in enumerate(cuts):
        unit = normed_ref[:, cut].astype(jnp.float32) * inverse
        total = total + unit * grad_ref[part].astype(jnp.float32)
    along = jnp.sum(total, axis=-1, keepdims=True)
    for part, cut in enumerate(cuts):
        unit = normed_ref[:, cut].astype(jnp.float32) * inverse
        out_ref[:, cut] = grad_ref[part].astype(jnp.float32) - unit * along


def project_call(returned, normed, inverse):
    parts, seqs, piece = returned.shape
    width = normed.shape[1]
    rows = 64
    return pl.pallas_call(
        project_kernel,
        grid=(seqs // rows,),
        in_specs=[
            pl.BlockSpec((parts, rows, piece), lambda i: (0, i, 0)),
            pl.BlockSpec((rows, width), lambda i: (i, 0)),
            pl.BlockSpec((rows, lanes), lambda i: (i, 0)),
        ],
        out_specs=pl.BlockSpec((rows, width), lambda i: (i, 0)),
        out_shape=jax.ShapeDtypeStruct((seqs, width), jnp.float32),
        compiler_params=pltpu.CompilerParams(vmem_limit_bytes=10 * mebibyte),
        name="project_out",
    )(returned, normed, inverse)


def swapped(value, apart):
    pairs = [(at, at ^ apart) for at in range(lax.axis_size("pb"))]
    return lax.ppermute(value, "pb", pairs)


def swap_bits(devices):
    bits = [1 << bit for bit in reversed(range(devices.bit_length() - 1))]
    return bits[:-2], bits[-2], bits[-1]


def swap_masks(devices):
    far, side, last = swap_bits(devices)
    held = [0]
    for apart in far:
        held = held + [mask ^ apart for mask in held]
    held = held + [mask ^ side for mask in held]
    return [held, [mask ^ last for mask in held]]


def gather_all(value):
    far, side, last = swap_bits(lax.axis_size("pb"))
    held = value[None]
    beside = [swapped(held, side)]
    for apart in far:
        arrived = swapped(held, apart)
        beside.append(swapped(arrived, side))
        held = jnp.concatenate([held, arrived], axis=0)
    held = jnp.concatenate([held] + beside, axis=0)
    return [held, swapped(held, last)]


def middle(embedded, room, devices, pairs, window):
    queries, documents, mine, other, top, own, place = score_call(
        embedded, room, devices, pairs, window
    )
    own_scores, *codes = merge_call(mine, swapped(other, 1), top, swapped(top, 1), devices)
    codes = [swapped(code, 2 * (hop + 1)) for hop, code in enumerate(codes)]
    parts = gather_all(softmax_call(place, own_scores, codes, devices, window))
    grads, loss = grad_call(own, place, parts, queries, documents, devices, pairs, window)
    return grads, loss[0, :1]


def feature_plan(hidden, final_gain, last_row, pair_owner, hard_negatives):
    devices = lax.axis_size("pb")
    seqs, width = hidden.shape
    pairs = pair_owner.shape[0]
    window = hard_negatives.shape[1]
    normed, inverse, embedding = norm_call(
        last_row, hidden, final_gain, pair_owner.T, hard_negatives, devices
    )
    embedded = lax.all_to_all(embedding, "pb", split_axis=0, concat_axis=0, tiled=True)
    most = devices * (window + 1)
    rooms = [most * part // 20 for part in (11, 12, 13, 15, 20)]
    used = devices + jnp.sum(embedded[:, seqs + 2, :window].astype(jnp.float32))
    level = sum((used > room).astype(jnp.int32) for room in rooms[:-1])
    grads, loss = lax.switch(
        level,
        [
            functools.partial(middle, room=room, devices=devices, pairs=pairs, window=window)
            for room in rooms
        ],
        embedded,
    )
    returned = lax.all_to_all(grads, "pb", split_axis=0, concat_axis=0, tiled=True)
    return project_call(returned, normed, inverse), loss


def from_behind(value, axis, steps):
    count = lax.axis_size(axis)
    pairs = [(source, (source + steps) % count) for source in range(count)]
    return lax.ppermute(value, axis, pairs)


def similarity(queries, documents):
    return inverse_temp * lax.dot_general(
        queries, documents, (((1,), (1,)), ((), ())), preferred_element_type=jnp.float32
    )


def transposed(weights, queries):
    return lax.dot_general(
        weights, queries, (((0,), (0,)), ((), ())), preferred_element_type=jnp.float32
    )


def combine_docs(weights, documents):
    return jnp.dot(weights, documents, preferred_element_type=jnp.float32)


def skipped(listed, function, operands, out_shape):
    return lax.cond(
        listed,
        lambda inputs: function(*inputs),
        lambda inputs: jnp.zeros(out_shape, jnp.float32),
        operands,
    )


def row_plan(hidden, final_gain, last_row, pair_owner, hard_negatives):
    values = hidden.astype(jnp.float32)
    scale_row = lax.rsqrt(jnp.mean(values * values, axis=-1, keepdims=True) + token_eps)
    normed = (values * scale_row * final_gain.astype(jnp.float32)).astype(jnp.bfloat16)
    seq_count = last_row.shape[1]
    model_width = hidden.shape[1]
    pooled = normed[last_row[0]].astype(jnp.float32)
    inverse_norm = lax.rsqrt(jnp.sum(pooled * pooled, axis=-1, keepdims=True) + 1e-06)
    unit_vec = pooled * inverse_norm
    embedding = unit_vec.astype(jnp.bfloat16)
    devices = lax.axis_size("pb")
    capacity = 2 * seq_count // devices
    pair_count = pair_owner.shape[0]
    wanted = jnp.concatenate([pair_owner[:, 0], pair_owner[:, 1]])
    holder = wanted // seq_count
    within = wanted % seq_count
    entry_ids = jnp.arange(2 * pair_count, dtype=jnp.int32)
    earlier = (holder[None, :] == holder[:, None]) & (entry_ids[None, :] < entry_ids[:, None])
    position = jnp.sum(earlier.astype(jnp.int32), axis=1)
    request = jnp.full((devices, capacity), -1, jnp.int32).at[holder, position].set(within)
    served = lax.all_to_all(request, "pb", split_axis=0, concat_axis=0, tiled=True)
    outgoing = jnp.where(
        served[:, :, None] >= 0, embedding[jnp.maximum(served, 0)], jnp.zeros((), jnp.bfloat16)
    )
    received = lax.all_to_all(outgoing, "pb", split_axis=0, concat_axis=0, tiled=True)
    gathered = received[holder, position]
    queries = gathered[:pair_count]
    own_docs = gathered[pair_count:]
    listed_ids = hard_negatives[0]
    window = hard_negatives.shape[1]
    listed = [listed_ids[offset] >= 0 for offset in range(window)]
    neighbours = []
    moving = own_docs
    for offset in range(window):
        moving = from_behind(moving, "pb", -1)
        neighbours.append(moving)
    tile_shape = (pair_count, pair_count)
    score_blocks = [similarity(queries, own_docs)]
    for offset in range(window):
        score_blocks.append(
            skipped(listed[offset], similarity, (queries, neighbours[offset]), tile_shape)
        )
    all_scores = jnp.concatenate(score_blocks, axis=1)
    usable = jnp.concatenate(
        [jnp.ones((pair_count,), jnp.bool_)]
        + [jnp.broadcast_to(listed[offset], (pair_count,)) for offset in range(window)]
    )
    masked = jnp.where(usable[None, :], all_scores, -jnp.inf)
    row_max = jnp.max(masked, axis=1, keepdims=True)
    log_total = row_max + jnp.log(jnp.sum(jnp.exp(masked - row_max), axis=1, keepdims=True))
    diagonal = jnp.arange(pair_count, dtype=jnp.int32)
    positive = all_scores[diagonal, diagonal]
    block_loss = jnp.mean(log_total[:, 0] - positive).reshape(1)
    columns = jnp.arange((window + 1) * pair_count, dtype=jnp.int32)
    target = (columns[None, :] == diagonal[:, None]).astype(jnp.float32)
    coefficients = (inverse_temp * (jnp.exp(masked - log_total) - target)).astype(jnp.bfloat16)
    pieces = [
        coefficients[:, offset * pair_count : (offset + 1) * pair_count]
        for offset in range(window + 1)
    ]
    grad_shape = (pair_count, model_width)
    query_sum = combine_docs(pieces[0], own_docs)
    for offset in range(window):
        query_sum = query_sum + skipped(
            listed[offset], combine_docs, (pieces[offset + 1], neighbours[offset]), grad_shape
        )
    query_grad = query_sum.astype(jnp.bfloat16)
    own_part = transposed(pieces[0], queries).astype(jnp.bfloat16)
    partial_value = [
        skipped(listed[offset], transposed, (pieces[offset + 1], queries), grad_shape).astype(
            jnp.bfloat16
        )
        for offset in range(window)
    ]
    running = partial_value[window - 1].astype(jnp.float32)
    for offset in range(window):
        running = from_behind(running, "pb", 1)
        if offset + 1 < window:
            running = running + partial_value[window - 2 - offset].astype(jnp.float32)
    doc_grad = (own_part.astype(jnp.float32) + running).astype(jnp.bfloat16)
    answers = jnp.concatenate([query_grad, doc_grad], axis=0)
    returning = (
        jnp.zeros((devices, capacity, model_width), jnp.bfloat16).at[holder, position].set(answers)
    )
    returned = lax.all_to_all(returning, "pb", split_axis=0, concat_axis=0, tiled=True)
    slot_ids = jnp.where(served >= 0, served, seq_count).reshape(-1)
    emb_grad = (
        jnp.zeros((seq_count, model_width), jnp.bfloat16)
        .at[slot_ids]
        .set(returned.reshape(-1, model_width), mode="drop")
    )
    gradient = emb_grad.astype(jnp.float32)
    pooled_grad = gradient - unit_vec * jnp.sum(unit_vec * gradient, axis=-1, keepdims=True)
    return (pooled_grad, block_loss)


def solution(mesh):
    def local(hidden, final_gain, last_row, pair_owner, hard_negatives):
        plan = feature_plan if hidden.shape[1] >= lanes * mesh.shape["pb"] else row_plan
        return plan(hidden, final_gain, last_row, pair_owner, hard_negatives)

    return jax.shard_map(
        local,
        mesh=mesh,
        in_specs=(
            P(("groups", "pb"), None),
            P(),
            P(("groups", "pb"), None),
            P(("groups", "pb"), None),
            P(("groups", "pb"), None),
        ),
        out_specs=(P(("groups", "pb"), None), P(("groups", "pb"))),
        check_vma=False,
    )
```

profile of v0, /device:TPU:1, one launch (start us, length us, event | category | flops | bytes accessed | tf_op | source)
XLA Modules:
  0.0 195.0 jit_solution(15875968308687688497)
XLA Ops:
  0.6 5.7 %norm_rows.1 = (bf16[256,4096]{1,0:T(8,128)(2,1)}, f32[256,128]{1,0:T(8,128)}, bf16[16,272,256]{2,1,0:T(8,128)(2,1)}) custom-call(s32[1,256]{1,0:T(1,128)} %last_ref.1, bf16[256,4096]{1,0:T(8,128)(2,1)} %hidden_ref.1, bf16[4096]{0:T(1024)(128)(2,1)} %gain_ref.1, s32[2,128]{1,0:T(2,128)} %bitcast.36, s32[1,4]{1,0:T(1,128)} %negative_ref.1), custom_call_target="tpu_custom_call" | custom-call | tf_op jit(solution)/shard_map/norm_rows/pallas_call | solution.py:89
  6.3 59.2 %all_to_all.25 = bf16[16,272,256]{2,1,0:T(8,128)(2,1)S(1)} all-to-all(bf16[16,272,256]{2,1,0:T(8,128)(2,1)} %get-tuple-element.97), channel_id=1, replica_groups=mesh['groups'=2,'pb'=16] {'pb'}, dimensions={0} | all-to-all | bytes 4456448 | tf_op jit(solution)/shard_map/all_to_all | solution.py:548
  65.5 0.6 fusion
  66.8 73.7 %conditional.1 = (bf16[16,256,256]{2,1,0:T(8,128)(2,1)S(1)}, f32[1]{0:T(128)}) conditional(s32[]{:T(128)} %clamp.3, bf16[16,272,256]{2,1,0:T(8,128)(2,1)S(1)} %all_to_all.25, bf16[16,272,256]{2,1,0:T(8,128)(2,1)S(1)} %all_to_all.25, bf16[16,272,256]{2,1,0:T(8,128)(2,1)S(1)} %all_to_all.25, ...), branch_computations={%region_1.0_spmd, %region_2.0_spmd, %region_3.0_spmd, %region_4.0_... | conditional | flops 167936 | bytes 28770920 | solution.py:553
  67.0 9.7 %partial_scores.7 = (bf16[2048,256]{1,0:T(8,128)(2,1)S(1)}, bf16[2560,256]{1,0:T(8,128)(2,1)S(1)}, f32[8,424,128]{2,1,0:T(8,128)S(1)}, f32[8,424,128]{2,1,0:T(8,...) custom-call(bf16[16,272,256]{2,1,0:T(8,128)(2,1)S(1)} %refs_0_.2), custom_call_target="tpu_custom_call" | custom-call | tf_op jit(solution)/shard_map/cond/branch_2_fun/partial_scores/pallas_call | solution.py:209
  76.7 0.3 collective-permute-start.30
  77.0 0.3 collective-permute-start.31
  77.3 3.1 %collective-permute-done.31.other_top_ref = f32[8,128]{1,0:T(8,128)S(1)} collective-permute-done((f32[8,128]{1,0:T(8,128)S(1)}, f32[8,128]{1,0:T(8,128)S(1)}, u32[]{:S(2)}, u32[]{:S(2)}) %collective-permute-start.31) | collective-permute-done | bytes 4128 | tf_op jit(solution)/shard_map/cond/branch_2_fun/ppermute | solution.py:500
  80.4 1.5 merge_scores.7
  81.9 0.4 collective-permute-start.32
  82.4 0.5 collective-permute-start.33
  82.8 1.8 collective-permute-start.34
  84.7 0.8 collective-permute-start.35
  85.5 1.6 collective-permute-start.36
  87.1 1.5 collective-permute-start.37
  88.6 2.5 %collective-permute-start.38 = (s16[27,16,128]{2,1,0:T(8,128)(2,1)S(1)}, s16[27,16,128]{2,1,0:T(8,128)(2,1)S(1)}, u32[]{:S(2)}, u32[]{:S(2)}) collective-permute-start(s16[27,16,128]{2,1,0:T(8,128)(2,1)S(1)} %get-tuple-element.53), channel_id=1, source_target_pairs={{0,14},{1,15},{2,12},{3,13},{4,10},{5,11},{6,8},{7,9},{8,6},{9,7},... | collective-permute-start | bytes 331784 | tf_op jit(solution)/shard_map/cond/branch_2_fun/ppermute | solution.py:500
  91.2 0.8 collective-permute-done.34.refs_2_
  92.0 9.9 %collective-permute-done.36.refs_4_ = s16[27,16,128]{2,1,0:T(8,128)(2,1)S(1)} collective-permute-done((s16[27,16,128]{2,1,0:T(8,128)(2,1)S(1)}, s16[27,16,128]{2,1,0:T(8,128)(2,1)S(1)}, u32[]{:S(2)}, u32[]{:S(2)}) %collective-permute-start.36) | collective-permute-done | bytes 110624 | tf_op jit(solution)/shard_map/cond/branch_2_fun/ppermute | solution.py:500
  101.9 1.9 softmax_rows.7
  103.8 5.6 %collective-permute-start.39 = (bf16[1,27,16,128]{3,2,1,0:T(8,128)(2,1)S(1)}, bf16[1,27,16,128]{3,2,1,0:T(8,128)(2,1)S(1)}, u32[]{:S(2)}, u32[]{:S(2)}) collective-permute-start(bf16[1,27,16,128]{3,2,1,0:T(8,128)(2,1)S(1)} %bitcast.27), channel_id=1, source_target_pairs={{0,8},{1,9},{2,10},{3,11},{4,12},{5,13},{6,14},{7,15},{8,0},{9,1},... | collective-permute-start | bytes 331784 | tf_op jit(solution)/shard_map/cond/branch_2_fun/ppermute | solution.py:500
  109.4 2.1 %collective-permute-done.39 = bf16[1,27,16,128]{3,2,1,0:T(8,128)(2,1)S(1)} collective-permute-done((bf16[1,27,16,128]{3,2,1,0:T(8,128)(2,1)S(1)}, bf16[1,27,16,128]{3,2,1,0:T(8,128)(2,1)S(1)}, u32[]{:S(2)}, u32[]{:S(2)}) %collective-permute-start.39) | collective-permute-done | bytes 110624 | tf_op jit(solution)/shard_map/cond/branch_2_fun/ppermute | solution.py:500
  111.5 2.0 %collective-permute-start.40 = (bf16[2,27,16,128]{3,2,1,0:T(8,128)(2,1)S(1)}, bf16[2,27,16,128]{3,2,1,0:T(8,128)(2,1)S(1)}, u32[]{:S(2)}, u32[]{:S(2)}) collective-permute-start(bf16[2,27,16,128]{3,2,1,0:T(8,128)(2,1)S(1)} %pad_maximum_fusion.2), channel_id=1, source_target_pairs={{0,4},{1,5},{2,6},{3,7},{4,0},{5,1},{6,2},{7,3},{8,12},{9,13},{10,... | collective-permute-start | bytes 663560 | tf_op jit(solution)/shard_map/cond/branch_2_fun/ppermute | solution.py:500
  113.6 0.3 collective-permute-start.41
  113.8 1.3 collective-permute-start.42
  115.1 2.0 %collective-permute-done.40 = bf16[2,27,16,128]{3,2,1,0:T(8,128)(2,1)S(1)} collective-permute-done((bf16[2,27,16,128]{3,2,1,0:T(8,128)(2,1)S(1)}, bf16[2,27,16,128]{3,2,1,0:T(8,128)(2,1)S(1)}, u32[]{:S(2)}, u32[]{:S(2)}) %collective-permute-start.40) | collective-permute-done | bytes 221216 | tf_op jit(solution)/shard_map/cond/branch_2_fun/ppermute | solution.py:500
  117.2 1.2 collective-permute-done.42
  118.4 5.9 %collective-permute-done.43 = bf16[2,27,16,128]{3,2,1,0:T(8,128)(2,1)S(1)} collective-permute-done((bf16[2,27,16,128]{3,2,1,0:T(8,128)(2,1)S(1)}, bf16[2,27,16,128]{3,2,1,0:T(8,128)(2,1)S(1)}, u32[]{:S(2)}, u32[]{:S(2)}) %collective-permute-start.43) | collective-permute-done | bytes 221216 | tf_op jit(solution)/shard_map/cond/branch_2_fun/ppermute | solution.py:500
  124.4 3.9 %collective-permute-start.44 = (bf16[8,27,16,128]{3,2,1,0:T(8,128)(2,1)S(1)}, bf16[8,27,16,128]{3,2,1,0:T(8,128)(2,1)S(1)}, u32[]{:S(2)}, u32[]{:S(2)}) collective-permute-start(bf16[8,27,16,128]{3,2,1,0:T(8,128)(2,1)S(1)} %constant_dynamic-update-slice_fusion.12.refs_0_), channel_id=1, source_target_pairs={{0,1},{1,0},{2,3},{3,2},{4,5},{5,4},{6,7},{7,6},{8,9},{9,8},{10,11... | collective-permute-start | bytes 2654216 | tf_op jit(solution)/shard_map/cond/branch_2_fun/ppermute | solution.py:500
  128.3 2.1 %collective-permute-done.44.refs_1_ = bf16[8,27,16,128]{3,2,1,0:T(8,128)(2,1)S(1)} collective-permute-done((bf16[8,27,16,128]{3,2,1,0:T(8,128)(2,1)S(1)}, bf16[8,27,16,128]{3,2,1,0:T(8,128)(2,1)S(1)}, u32[]{:S(2)}, u32[]{:S(2)}) %collective-permute-start.44) | collective-permute-done | bytes 884768 | tf_op jit(solution)/shard_map/cond/branch_2_fun/ppermute | solution.py:500
  130.3 10.1 %slice_grads.7 = (bf16[16,256,256]{2,1,0:T(8,128)(2,1)S(1)}, f32[1,128]{1,0:T(1,128)}) custom-call(s32[16,256]{1,0:T(8,128)S(1)} %get-tuple-element.39.own_ref, s32[5,16]{1,0:T(8,128)S(1)} %get-tuple-element.40.place_ref, bf16[2048,256]{1,0:T(8,128)(2,1)S(1)} %get-tuple-element.41.q_ref, bf16[2560,256]{1,0:T(8,128)(2,1)S(1)} %get-tuple-element.42.d_ref, ...), custom_call_target="tpu_custom_call" | custom-call | tf_op jit(solution)/shard_map/cond/branch_2_fun/slice_grads/pallas_call | solution.py:445
  140.5 51.2 %all_to_all.26.grad_ref = bf16[16,256,256]{2,1,0:T(8,128)(2,1)S(1)} all-to-all(bf16[16,256,256]{2,1,0:T(8,128)(2,1)S(1)} %get-tuple-element.98), channel_id=1, replica_groups=mesh['groups'=2,'pb'=16] {'pb'}, dimensions={0} | all-to-all | bytes 4194304 | tf_op jit(solution)/shard_map/all_to_all | solution.py:561
  191.7 3.3 %project_out.1 = f32[256,4096]{1,0:T(8,128)} custom-call(bf16[16,256,256]{2,1,0:T(8,128)(2,1)S(1)} %all_to_all.26.grad_ref, bf16[256,4096]{1,0:T(8,128)(2,1)S(1)} %copy-done, f32[256,128]{1,0:T(8,128)S(1)} %copy-done.1), custom_call_target="tpu_custom_call" | custom-call | tf_op jit(solution)/shard_map/project_out/pallas_call | solution.py:483
  (19 shorter events, 0.2 us)
Async XLA Ops:
  76.7 3.7 %collective-permute-start.30 = (f32[8,424,128]{2,1,0:T(8,128)S(1)}, f32[8,424,128]{2,1,0:T(8,128)S(1)}, u32[]{:S(2)}, u32[]{:S(2)}) collective-permute-start(f32[8,424,128]{2,1,0:T(8,128)S(1)} %get-tuple-element.44), channel_id=1, source_target_pairs={{0,1},{1,0},{2,3},{3,2},{4,5},{5,4},{6,7},{7,6},{8,9},{9,8},{10,11... | collective-permute-start | bytes 5210120 | tf_op jit(solution)/shard_map/cond/branch_2_fun/ppermute | solution.py:500
  77.0 3.4 %collective-permute-start.31 = (f32[8,128]{1,0:T(8,128)S(1)}, f32[8,128]{1,0:T(8,128)S(1)}, u32[]{:S(2)}, u32[]{:S(2)}) collective-permute-start(f32[8,128]{1,0:T(8,128)S(1)} %get-tuple-element.45.top_ref), channel_id=1, source_target_pairs={{0,1},{1,0},{2,3},{3,2},{4,5},{5,4},{6,7},{7,6},{8,9},{9,8},{10,11... | collective-permute-start | bytes 12296 | tf_op jit(solution)/shard_map/cond/branch_2_fun/ppermute | solution.py:500
  81.9 5.2 %collective-permute-start.32 = (s16[27,16,128]{2,1,0:T(8,128)(2,1)S(1)}, s16[27,16,128]{2,1,0:T(8,128)(2,1)S(1)}, u32[]{:S(2)}, u32[]{:S(2)}) collective-permute-start(s16[27,16,128]{2,1,0:T(8,128)(2,1)S(1)} %get-tuple-element.47), channel_id=1, source_target_pairs={{0,2},{1,3},{2,0},{3,1},{4,6},{5,7},{6,4},{7,5},{8,10},{9,11},{10,... | collective-permute-start | bytes 331784 | tf_op jit(solution)/shard_map/cond/branch_2_fun/ppermute | solution.py:500
  82.4 6.3 %collective-permute-start.33 = (s16[27,16,128]{2,1,0:T(8,128)(2,1)S(1)}, s16[27,16,128]{2,1,0:T(8,128)(2,1)S(1)}, u32[]{:S(2)}, u32[]{:S(2)}) collective-permute-start(s16[27,16,128]{2,1,0:T(8,128)(2,1)S(1)} %get-tuple-element.48), channel_id=1, source_target_pairs={{0,4},{1,5},{2,6},{3,7},{4,0},{5,1},{6,2},{7,3},{8,12},{9,13},{10,... | collective-permute-start | bytes 331784 | tf_op jit(solution)/shard_map/cond/branch_2_fun/ppermute | solution.py:500
  82.8 9.1 %collective-permute-start.34 = (s16[27,16,128]{2,1,0:T(8,128)(2,1)S(1)}, s16[27,16,128]{2,1,0:T(8,128)(2,1)S(1)}, u32[]{:S(2)}, u32[]{:S(2)}) collective-permute-start(s16[27,16,128]{2,1,0:T(8,128)(2,1)S(1)} %get-tuple-element.49), channel_id=1, source_target_pairs={{0,6},{1,7},{2,4},{3,5},{4,2},{5,3},{6,0},{7,1},{8,14},{9,15},{10,... | collective-permute-start | bytes 331784 | tf_op jit(solution)/shard_map/cond/branch_2_fun/ppermute | solution.py:500
  84.7 7.3 %collective-permute-start.35 = (s16[27,16,128]{2,1,0:T(8,128)(2,1)S(1)}, s16[27,16,128]{2,1,0:T(8,128)(2,1)S(1)}, u32[]{:S(2)}, u32[]{:S(2)}) collective-permute-start(s16[27,16,128]{2,1,0:T(8,128)(2,1)S(1)} %get-tuple-element.50), channel_id=1, source_target_pairs={{0,8},{1,9},{2,10},{3,11},{4,12},{5,13},{6,14},{7,15},{8,0},{9,1},... | collective-permute-start | bytes 331784 | tf_op jit(solution)/shard_map/cond/branch_2_fun/ppermute | solution.py:500
  85.5 16.4 %collective-permute-start.36 = (s16[27,16,128]{2,1,0:T(8,128)(2,1)S(1)}, s16[27,16,128]{2,1,0:T(8,128)(2,1)S(1)}, u32[]{:S(2)}, u32[]{:S(2)}) collective-permute-start(s16[27,16,128]{2,1,0:T(8,128)(2,1)S(1)} %get-tuple-element.51), channel_id=1, source_target_pairs={{0,10},{1,11},{2,8},{3,9},{4,14},{5,15},{6,12},{7,13},{8,2},{9,3},... | collective-permute-start | bytes 331784 | tf_op jit(solution)/shard_map/cond/branch_2_fun/ppermute | solution.py:500
  87.1 14.7 %collective-permute-start.37 = (s16[27,16,128]{2,1,0:T(8,128)(2,1)S(1)}, s16[27,16,128]{2,1,0:T(8,128)(2,1)S(1)}, u32[]{:S(2)}, u32[]{:S(2)}) collective-permute-start(s16[27,16,128]{2,1,0:T(8,128)(2,1)S(1)} %get-tuple-element.52), channel_id=1, source_target_pairs={{0,12},{1,13},{2,14},{3,15},{4,8},{5,9},{6,10},{7,11},{8,4},{9,5},... | collective-permute-start | bytes 331784 | tf_op jit(solution)/shard_map/cond/branch_2_fun/ppermute | solution.py:500
  88.6 13.2 %collective-permute-start.38 = (s16[27,16,128]{2,1,0:T(8,128)(2,1)S(1)}, s16[27,16,128]{2,1,0:T(8,128)(2,1)S(1)}, u32[]{:S(2)}, u32[]{:S(2)}) collective-permute-start(s16[27,16,128]{2,1,0:T(8,128)(2,1)S(1)} %get-tuple-element.53), channel_id=1, source_target_pairs={{0,14},{1,15},{2,12},{3,13},{4,10},{5,11},{6,8},{7,9},{8,6},{9,7},... | collective-permute-start | bytes 331784 | tf_op jit(solution)/shard_map/cond/branch_2_fun/ppermute | solution.py:500
  103.8 7.7 %collective-permute-start.39 = (bf16[1,27,16,128]{3,2,1,0:T(8,128)(2,1)S(1)}, bf16[1,27,16,128]{3,2,1,0:T(8,128)(2,1)S(1)}, u32[]{:S(2)}, u32[]{:S(2)}) collective-permute-start(bf16[1,27,16,128]{3,2,1,0:T(8,128)(2,1)S(1)} %bitcast.27), channel_id=1, source_target_pairs={{0,8},{1,9},{2,10},{3,11},{4,12},{5,13},{6,14},{7,15},{8,0},{9,1},... | collective-permute-start | bytes 331784 | tf_op jit(solution)/shard_map/cond/branch_2_fun/ppermute | solution.py:500
  111.5 5.6 %collective-permute-start.40 = (bf16[2,27,16,128]{3,2,1,0:T(8,128)(2,1)S(1)}, bf16[2,27,16,128]{3,2,1,0:T(8,128)(2,1)S(1)}, u32[]{:S(2)}, u32[]{:S(2)}) collective-permute-start(bf16[2,27,16,128]{3,2,1,0:T(8,128)(2,1)S(1)} %pad_maximum_fusion.2), channel_id=1, source_target_pairs={{0,4},{1,5},{2,6},{3,7},{4,0},{5,1},{6,2},{7,3},{8,12},{9,13},{10,... | collective-permute-start | bytes 663560 | tf_op jit(solution)/shard_map/cond/branch_2_fun/ppermute | solution.py:500
  113.6 3.7 %collective-permute-start.41 = (bf16[1,27,16,128]{3,2,1,0:T(8,128)(2,1)S(1)}, bf16[1,27,16,128]{3,2,1,0:T(8,128)(2,1)S(1)}, u32[]{:S(2)}, u32[]{:S(2)}) collective-permute-start(bf16[1,27,16,128]{3,2,1,0:T(8,128)(2,1)S(1)} %bitcast.29), channel_id=1, source_target_pairs={{0,2},{1,3},{2,0},{3,1},{4,6},{5,7},{6,4},{7,5},{8,10},{9,11},{10,... | collective-permute-start | bytes 331784 | tf_op jit(solution)/shard_map/cond/branch_2_fun/ppermute | solution.py:500
  113.8 4.6 %collective-permute-start.42 = (bf16[1,27,16,128]{3,2,1,0:T(8,128)(2,1)S(1)}, bf16[1,27,16,128]{3,2,1,0:T(8,128)(2,1)S(1)}, u32[]{:S(2)}, u32[]{:S(2)}) collective-permute-start(bf16[1,27,16,128]{3,2,1,0:T(8,128)(2,1)S(1)} %collective-permute-done.39), channel_id=1, source_target_pairs={{0,2},{1,3},{2,0},{3,1},{4,6},{5,7},{6,4},{7,5},{8,10},{9,11},{10,... | collective-permute-start | bytes 331784 | tf_op jit(solution)/shard_map/cond/branch_2_fun/ppermute | solution.py:500
  117.2 7.2 %collective-permute-start.43 = (bf16[2,27,16,128]{3,2,1,0:T(8,128)(2,1)S(1)}, bf16[2,27,16,128]{3,2,1,0:T(8,128)(2,1)S(1)}, u32[]{:S(2)}, u32[]{:S(2)}) collective-permute-start(bf16[2,27,16,128]{3,2,1,0:T(8,128)(2,1)S(1)} %collective-permute-done.40), channel_id=1, source_target_pairs={{0,2},{1,3},{2,0},{3,1},{4,6},{5,7},{6,4},{7,5},{8,10},{9,11},{10,... | collective-permute-start | bytes 663560 | tf_op jit(solution)/shard_map/cond/branch_2_fun/ppermute | solution.py:500
  124.4 5.9 %collective-permute-start.44 = (bf16[8,27,16,128]{3,2,1,0:T(8,128)(2,1)S(1)}, bf16[8,27,16,128]{3,2,1,0:T(8,128)(2,1)S(1)}, u32[]{:S(2)}, u32[]{:S(2)}) collective-permute-start(bf16[8,27,16,128]{3,2,1,0:T(8,128)(2,1)S(1)} %constant_dynamic-update-slice_fusion.12.refs_0_), channel_id=1, source_target_pairs={{0,1},{1,0},{2,3},{3,2},{4,5},{5,4},{6,7},{7,6},{8,9},{9,8},{10,11... | collective-permute-start | bytes 2654216 | tf_op jit(solution)/shard_map/cond/branch_2_fun/ppermute | solution.py:500
  140.5 51.3 %copy-start = (bf16[256,4096]{1,0:T(8,128)(2,1)S(1)}, bf16[256,4096]{1,0:T(8,128)(2,1)}, u32[]{:S(2)}) copy-start(bf16[256,4096]{1,0:T(8,128)(2,1)} %get-tuple-element.99.normed_ref) | copy-start | bytes 6291460
  140.5 51.3 %copy-start.1 = (f32[256,128]{1,0:T(8,128)S(1)}, f32[256,128]{1,0:T(8,128)}, u32[]{:S(2)}) copy-start(f32[256,128]{1,0:T(8,128)} %get-tuple-element.100.inv_ref) | copy-start | bytes 393220
where the time goes:
time: 194 us; the launch traced here: 195 us
  blocking collectives  110 us (57%)
  Pallas kernels  32.2 us (17%)
  waiting for transfers between devices  27.2 us (14%)
  starting transfers between devices  22.8 us (12%)
    all_to_all x1, blocking collectives, feature_plan(): lax.all_to_all(embedding, 'pb', split_axis=0, concat_axis=0, tiled=True)  59.2 us
    all_to_all x1, blocking collectives, feature_plan(): lax.all_to_all(grads, 'pb', split_axis=0, concat_axis=0, tiled=True)  51.2 us
    ppermute x15, waiting for transfers between devices, swapped(): return lax.ppermute(value, 'pb', pairs)  27.2 us
    ppermute x15, starting transfers between devices, swapped(): return lax.ppermute(value, 'pb', pairs)  22.8 us
    pallas_call x1, Pallas kernels, grad_call(): pl.pallas_call(functools.partial(grad_kernel, blocks, pairs, window), in_...  10.1 us
    pallas_call x1, Pallas kernels, score_call(): pl.pallas_call(functools.partial(score_kernel, blocks, pairs, window), in...  9.72 us
    pallas_call x1, Pallas kernels, norm_call(): pl.pallas_call(norm_kernel, in_specs=[whole, whole, whole, whole, pl.Bloc...  5.66 us
  transfers between devices with their start and end apart: 15, of which 8 were waited for; matrix products, arithmetic and copies ran while one was open for 0% of the time, Pallas kernels for 0%

commit v1 on v0

--- a/solution.py
+++ b/solution.py
@@ -27,8 +27,8 @@
     return jnp.concatenate(halves, axis=1)
 
 
-def row_pair(index):
-    return pl.ds(pl.multiple_of(2 * index, 2), 2)
+def row_pair(place):
+    return pl.ds(pl.multiple_of(place, 2), 2)
 
 
 def norm_kernel(
@@ -110,7 +110,7 @@
     wide, picked, picked_too, facts, own, named, sems = refs[-7:]
     seqs = emb_ref.shape[1] - 16
     sent = emb_ref[:, seqs:, :].astype(jnp.float32)
-    own_ref[...] = (sent[:, 0, :] + 256.0 * sent[:, 1, :]).astype(jnp.int32)
+    own_ref[...] = (2.0 * sent[:, 0, :] + 512.0 * sent[:, 1, :]).astype(jnp.int32)
     facts[...] = sent[:, 2, :lanes].astype(jnp.int32)
     fetches = [
         pltpu.make_async_copy(own_ref, own, sems.at[0]),
@@ -517,11 +517,13 @@
 def gather_all(value):
     far, side, last = swap_bits(lax.axis_size("pb"))
     held = value[None]
-    beside = [swapped(held, side)]
+    beside, latest = [], held
     for apart in far:
         arrived = swapped(held, apart)
-        beside.append(swapped(arrived, side))
+        beside.append(swapped(latest, side))
         held = jnp.concatenate([held, arrived], axis=0)
+        latest = arrived
+    beside.append(swapped(latest, side))
     held = jnp.concatenate([held] + beside, axis=0)
     return [held, swapped(held, last)]
 
@@ -531,7 +533,7 @@
         embedded, room, devices, pairs, window
     )
     own_scores, *codes = merge_call(mine, swapped(other, 1), top, swapped(top, 1), devices)
-    codes = [swapped(code, 2 * (hop + 1)) for hop, code in enumerate(codes)]
+    codes = [swapped(codes[hop], 2 * (hop + 1)) for hop in reversed(range(len(codes)))]
     parts = gather_all(softmax_call(place, own_scores, codes, devices, window))
     grads, loss = grad_call(own, place, parts, queries, documents, devices, pairs, window)
     return grads, loss[0, :1]

time: 194 us -> 190 us (0.979); the launches traced: 195 us -> 186 us
  starting transfers between devices: 22.8 us -> 16.6 us
  Pallas kernels: 32.2 us -> 29.3 us
    ppermute x15, starting transfers between devices: 22.8 us -> 16.6 us  [swapped(): return lax.ppermute(value, 'pb', pairs)]
where the time goes in v1:
time: 190 us; the launch traced here: 186 us
  blocking collectives  111 us (58%)
  Pallas kernels  29.3 us (15%)
  waiting for transfers between devices  27 us (14%)
  starting transfers between devices  16.6 us (9%)
    all_to_all x1, blocking collectives, feature_plan(): lax.all_to_all(embedding, 'pb', split_axis=0, concat_axis=0, tiled=True)  59.2 us
    all_to_all x1, blocking collectives, feature_plan(): lax.all_to_all(grads, 'pb', split_axis=0, concat_axis=0, tiled=True)  51.7 us
    ppermute x15, waiting for transfers between devices, swapped(): return lax.ppermute(value, 'pb', pairs)  27 us
    ppermute x15, starting transfers between devices, swapped(): return lax.ppermute(value, 'pb', pairs)  16.6 us
    pallas_call x1, Pallas kernels, grad_call(): pl.pallas_call(functools.partial(grad_kernel, blocks, pairs, window), in_...  9.05 us
    pallas_call x1, Pallas kernels, score_call(): pl.pallas_call(functools.partial(score_kernel, blocks, pairs, window), in...  8.14 us
    pallas_call x1, Pallas kernels, norm_call(): pl.pallas_call(norm_kernel, in_specs=[whole, whole, whole, whole, pl.Bloc...  5.66 us
  transfers between devices with their start and end apart: 15, of which 8 were waited for; matrix products, arithmetic and copies ran while one was open for 0% of the time, Pallas kernels for 0%

profile of v1, /device:TPU:1, one launch (start us, length us, event | category | flops | bytes accessed | tf_op | source)
XLA Modules:
  0.0 186.2 jit_solution(8848960139806101882)
XLA Ops:
  0.6 5.7 %norm_rows.1 = (bf16[256,4096]{1,0:T(8,128)(2,1)}, f32[256,128]{1,0:T(8,128)}, bf16[16,272,256]{2,1,0:T(8,128)(2,1)}) custom-call(s32[1,256]{1,0:T(1,128)} %last_ref.1, bf16[256,4096]{1,0:T(8,128)(2,1)} %hidden_ref.1, bf16[4096]{0:T(1024)(128)(2,1)} %gain_ref.1, s32[2,128]{1,0:T(2,128)} %bitcast.36, s32[1,4]{1,0:T(1,128)} %negative_ref.1), custom_call_target="tpu_custom_call" | custom-call | tf_op jit(solution)/shard_map/norm_rows/pallas_call | solution.py:89
  6.3 59.2 %all_to_all.25 = bf16[16,272,256]{2,1,0:T(8,128)(2,1)S(1)} all-to-all(bf16[16,272,256]{2,1,0:T(8,128)(2,1)} %get-tuple-element.97), channel_id=1, replica_groups=mesh['groups'=2,'pb'=16] {'pb'}, dimensions={0} | all-to-all | bytes 4456448 | tf_op jit(solution)/shard_map/all_to_all | solution.py:550
  65.5 0.6 fusion
  66.8 64.4 %conditional.1 = (bf16[16,256,256]{2,1,0:T(8,128)(2,1)S(1)}, f32[1]{0:T(128)}) conditional(s32[]{:T(128)} %clamp.3, bf16[16,272,256]{2,1,0:T(8,128)(2,1)S(1)} %all_to_all.25, bf16[16,272,256]{2,1,0:T(8,128)(2,1)S(1)} %all_to_all.25, bf16[16,272,256]{2,1,0:T(8,128)(2,1)S(1)} %all_to_all.25, ...), branch_computations={%region_1.0_spmd, %region_2.0_spmd, %region_3.0_spmd, %region_4.0_... | conditional | flops 167936 | bytes 28770920 | solution.py:555
  66.8 8.1 %partial_scores.5 = (bf16[2048,256]{1,0:T(8,128)(2,1)S(1)}, bf16[2560,256]{1,0:T(8,128)(2,1)S(1)}, f32[8,360,128]{2,1,0:T(8,128)S(1)}, f32[8,360,128]{2,1,0:T(8,...) custom-call(bf16[16,272,256]{2,1,0:T(8,128)(2,1)S(1)} %refs_0_), custom_call_target="tpu_custom_call" | custom-call | tf_op jit(solution)/shard_map/cond/branch_0_fun/partial_scores/pallas_call | solution.py:209
  74.9 0.3 collective-permute-start
  75.2 0.3 collective-permute-start.1
  75.5 2.8 %collective-permute-done.1.other_top_ref = f32[8,128]{1,0:T(8,128)S(1)} collective-permute-done((f32[8,128]{1,0:T(8,128)S(1)}, f32[8,128]{1,0:T(8,128)S(1)}, u32[]{:S(2)}, u32[]{:S(2)}) %collective-permute-start.1) | collective-permute-done | bytes 4128 | tf_op jit(solution)/shard_map/cond/branch_0_fun/ppermute | solution.py:500
  78.3 1.3 merge_scores.5
  79.6 1.7 collective-permute-start.2
  81.3 1.7 collective-permute-start.3
  83.0 3.2 %collective-permute-start.5 = (s16[23,16,128]{2,1,0:T(8,128)(2,1)S(1)}, s16[23,16,128]{2,1,0:T(8,128)(2,1)S(1)}, u32[]{:S(2)}, u32[]{:S(2)}) collective-permute-start(s16[23,16,128]{2,1,0:T(8,128)(2,1)S(1)} %get-tuple-element.16), channel_id=1, source_target_pairs={{0,8},{1,9},{2,10},{3,11},{4,12},{5,13},{6,14},{7,15},{8,0},{9,1},... | collective-permute-start | bytes 282632 | tf_op jit(solution)/shard_map/cond/branch_0_fun/ppermute | solution.py:500
  86.2 0.3 collective-permute-done.2.refs_0_
  86.5 1.2 collective-permute-start.7
  87.7 0.0 collective-permute-done.3.refs_1_
  87.7 1.1 collective-permute-start.8
  88.8 7.9 %collective-permute-done.4.refs_2_ = s16[23,16,128]{2,1,0:T(8,128)(2,1)S(1)} collective-permute-done((s16[23,16,128]{2,1,0:T(8,128)(2,1)S(1)}, s16[23,16,128]{2,1,0:T(8,128)(2,1)S(1)}, u32[]{:S(2)}, u32[]{:S(2)}) %collective-permute-start.4) | collective-permute-done | bytes 94240 | tf_op jit(solution)/shard_map/cond/branch_0_fun/ppermute | solution.py:500
  96.8 1.2 collective-permute-done.5.refs_3_
  98.0 1.9 %softmax_rows.5 = bf16[23,16,128]{2,1,0:T(8,128)(2,1)S(1)} custom-call(s32[5,16]{1,0:T(8,128)S(1)} %get-tuple-element.6.place_ref, f32[352,128]{1,0:T(8,128)S(1)} %get-tuple-element.12.own_ref, s16[23,16,128]{2,1,0:T(8,128)(2,1)S(1)} %collective-permute-done.2.refs_0_, s16[23,16,128]{2,1,0:T(8,128)(2,1)S(1)} %collective-permute-done.3.refs_1_, ...), custom_call_target="tpu_custom_call" | custom-call | tf_op jit(solution)/shard_map/cond/branch_0_fun/softmax_rows/pallas_call | solution.py:341
  99.9 0.1 collective-permute-start.9
  100.0 4.7 %collective-permute-done.9 = bf16[1,23,16,128]{3,2,1,0:T(8,128)(2,1)S(1)} collective-permute-done((bf16[1,23,16,128]{3,2,1,0:T(8,128)(2,1)S(1)}, bf16[1,23,16,128]{3,2,1,0:T(8,128)(2,1)S(1)}, u32[]{:S(2)}, u32[]{:S(2)}) %collective-permute-start.9) | collective-permute-done | bytes 94240 | tf_op jit(solution)/shard_map/cond/branch_0_fun/ppermute | solution.py:500
  104.7 0.1 collective-permute-start.10
  104.8 1.4 collective-permute-start.11
  106.2 0.1 collective-permute-start.12
  106.3 3.5 %collective-permute-done.10 = bf16[2,23,16,128]{3,2,1,0:T(8,128)(2,1)S(1)} collective-permute-done((bf16[2,23,16,128]{3,2,1,0:T(8,128)(2,1)S(1)}, bf16[2,23,16,128]{3,2,1,0:T(8,128)(2,1)S(1)}, u32[]{:S(2)}, u32[]{:S(2)}) %collective-permute-start.10) | collective-permute-done | bytes 188448 | tf_op jit(solution)/shard_map/cond/branch_0_fun/ppermute | solution.py:500
  109.8 1.2 collective-permute-start.13
  111.1 4.7 %collective-permute-done.13 = bf16[2,23,16,128]{3,2,1,0:T(8,128)(2,1)S(1)} collective-permute-done((bf16[2,23,16,128]{3,2,1,0:T(8,128)(2,1)S(1)}, bf16[2,23,16,128]{3,2,1,0:T(8,128)(2,1)S(1)}, u32[]{:S(2)}, u32[]{:S(2)}) %collective-permute-start.13) | collective-permute-done | bytes 188448 | tf_op jit(solution)/shard_map/cond/branch_0_fun/ppermute | solution.py:500
  115.8 4.2 %collective-permute-start.14 = (bf16[8,23,16,128]{3,2,1,0:T(8,128)(2,1)S(1)}, bf16[8,23,16,128]{3,2,1,0:T(8,128)(2,1)S(1)}, u32[]{:S(2)}, u32[]{:S(2)}) collective-permute-start(bf16[8,23,16,128]{3,2,1,0:T(8,128)(2,1)S(1)} %constant_dynamic-update-slice_fusion.refs_0_), channel_id=1, source_target_pairs={{0,1},{1,0},{2,3},{3,2},{4,5},{5,4},{6,7},{7,6},{8,9},{9,8},{10,11... | collective-permute-start | bytes 2261000 | tf_op jit(solution)/shard_map/cond/branch_0_fun/ppermute | solution.py:500
  120.1 1.9 %collective-permute-done.14.refs_1_ = bf16[8,23,16,128]{3,2,1,0:T(8,128)(2,1)S(1)} collective-permute-done((bf16[8,23,16,128]{3,2,1,0:T(8,128)(2,1)S(1)}, bf16[8,23,16,128]{3,2,1,0:T(8,128)(2,1)S(1)}, u32[]{:S(2)}, u32[]{:S(2)}) %collective-permute-start.14) | collective-permute-done | bytes 753696 | tf_op jit(solution)/shard_map/cond/branch_0_fun/ppermute | solution.py:500
  121.9 9.1 %slice_grads.5 = (bf16[16,256,256]{2,1,0:T(8,128)(2,1)S(1)}, f32[1,128]{1,0:T(1,128)}) custom-call(s32[16,256]{1,0:T(8,128)S(1)} %get-tuple-element.5.own_ref, s32[5,16]{1,0:T(8,128)S(1)} %get-tuple-element.6.place_ref, bf16[2048,256]{1,0:T(8,128)(2,1)S(1)} %get-tuple-element.7.q_ref, bf16[2560,256]{1,0:T(8,128)(2,1)S(1)} %get-tuple-element.8.d_ref, ...), custom_call_target="tpu_custom_call" | custom-call | tf_op jit(solution)/shard_map/cond/branch_0_fun/slice_grads/pallas_call | solution.py:445
  131.2 51.7 %all_to_all.26.grad_ref = bf16[16,256,256]{2,1,0:T(8,128)(2,1)S(1)} all-to-all(bf16[16,256,256]{2,1,0:T(8,128)(2,1)S(1)} %get-tuple-element.98), channel_id=1, replica_groups=mesh['groups'=2,'pb'=16] {'pb'}, dimensions={0} | all-to-all | bytes 4194304 | tf_op jit(solution)/shard_map/all_to_all | solution.py:563
  182.9 3.3 %project_out.1 = f32[256,4096]{1,0:T(8,128)} custom-call(bf16[16,256,256]{2,1,0:T(8,128)(2,1)S(1)} %all_to_all.26.grad_ref, bf16[256,4096]{1,0:T(8,128)(2,1)S(1)} %copy-done, f32[256,128]{1,0:T(8,128)S(1)} %copy-done.1), custom_call_target="tpu_custom_call" | custom-call | tf_op jit(solution)/shard_map/project_out/pallas_call | solution.py:483
  (19 shorter events, 0.1 us)
Async XLA Ops:
  74.9 3.3 %collective-permute-start = (f32[8,360,128]{2,1,0:T(8,128)S(1)}, f32[8,360,128]{2,1,0:T(8,128)S(1)}, u32[]{:S(2)}, u32[]{:S(2)}) collective-permute-start(f32[8,360,128]{2,1,0:T(8,128)S(1)} %get-tuple-element.10), channel_id=1, source_target_pairs={{0,1},{1,0},{2,3},{3,2},{4,5},{5,4},{6,7},{7,6},{8,9},{9,8},{10,11... | collective-permute-start | bytes 4423688 | tf_op jit(solution)/shard_map/cond/branch_0_fun/ppermute | solution.py:500
  75.2 3.1 %collective-permute-start.1 = (f32[8,128]{1,0:T(8,128)S(1)}, f32[8,128]{1,0:T(8,128)S(1)}, u32[]{:S(2)}, u32[]{:S(2)}) collective-permute-start(f32[8,128]{1,0:T(8,128)S(1)} %get-tuple-element.11.top_ref), channel_id=1, source_target_pairs={{0,1},{1,0},{2,3},{3,2},{4,5},{5,4},{6,7},{7,6},{8,9},{9,8},{10,11... | collective-permute-start | bytes 12296 | tf_op jit(solution)/shard_map/cond/branch_0_fun/ppermute | solution.py:500
  79.6 6.9 %collective-permute-start.2 = (s16[23,16,128]{2,1,0:T(8,128)(2,1)S(1)}, s16[23,16,128]{2,1,0:T(8,128)(2,1)S(1)}, u32[]{:S(2)}, u32[]{:S(2)}) collective-permute-start(s16[23,16,128]{2,1,0:T(8,128)(2,1)S(1)} %get-tuple-element.13), channel_id=1, source_target_pairs={{0,14},{1,15},{2,12},{3,13},{4,10},{5,11},{6,8},{7,9},{8,6},{9,7},... | collective-permute-start | bytes 282632 | tf_op jit(solution)/shard_map/cond/branch_0_fun/ppermute | solution.py:500
  81.3 6.5 %collective-permute-start.3 = (s16[23,16,128]{2,1,0:T(8,128)(2,1)S(1)}, s16[23,16,128]{2,1,0:T(8,128)(2,1)S(1)}, u32[]{:S(2)}, u32[]{:S(2)}) collective-permute-start(s16[23,16,128]{2,1,0:T(8,128)(2,1)S(1)} %get-tuple-element.14), channel_id=1, source_target_pairs={{0,12},{1,13},{2,14},{3,15},{4,8},{5,9},{6,10},{7,11},{8,4},{9,5},... | collective-permute-start | bytes 282632 | tf_op jit(solution)/shard_map/cond/branch_0_fun/ppermute | solution.py:500
  83.0 13.8 %collective-permute-start.4 = (s16[23,16,128]{2,1,0:T(8,128)(2,1)S(1)}, s16[23,16,128]{2,1,0:T(8,128)(2,1)S(1)}, u32[]{:S(2)}, u32[]{:S(2)}) collective-permute-start(s16[23,16,128]{2,1,0:T(8,128)(2,1)S(1)} %get-tuple-element.15), channel_id=1, source_target_pairs={{0,10},{1,11},{2,8},{3,9},{4,14},{5,15},{6,12},{7,13},{8,2},{9,3},... | collective-permute-start | bytes 282632 | tf_op jit(solution)/shard_map/cond/branch_0_fun/ppermute | solution.py:500
  83.0 15.0 %collective-permute-start.5 = (s16[23,16,128]{2,1,0:T(8,128)(2,1)S(1)}, s16[23,16,128]{2,1,0:T(8,128)(2,1)S(1)}, u32[]{:S(2)}, u32[]{:S(2)}) collective-permute-start(s16[23,16,128]{2,1,0:T(8,128)(2,1)S(1)} %get-tuple-element.16), channel_id=1, source_target_pairs={{0,8},{1,9},{2,10},{3,11},{4,12},{5,13},{6,14},{7,15},{8,0},{9,1},... | collective-permute-start | bytes 282632 | tf_op jit(solution)/shard_map/cond/branch_0_fun/ppermute | solution.py:500
  86.2 11.8 %collective-permute-start.6 = (s16[23,16,128]{2,1,0:T(8,128)(2,1)S(1)}, s16[23,16,128]{2,1,0:T(8,128)(2,1)S(1)}, u32[]{:S(2)}, u32[]{:S(2)}) collective-permute-start(s16[23,16,128]{2,1,0:T(8,128)(2,1)S(1)} %get-tuple-element.17), channel_id=1, source_target_pairs={{0,6},{1,7},{2,4},{3,5},{4,2},{5,3},{6,0},{7,1},{8,14},{9,15},{10,... | collective-permute-start | bytes 282632 | tf_op jit(solution)/shard_map/cond/branch_0_fun/ppermute | solution.py:500
  86.5 11.5 %collective-permute-start.7 = (s16[23,16,128]{2,1,0:T(8,128)(2,1)S(1)}, s16[23,16,128]{2,1,0:T(8,128)(2,1)S(1)}, u32[]{:S(2)}, u32[]{:S(2)}) collective-permute-start(s16[23,16,128]{2,1,0:T(8,128)(2,1)S(1)} %get-tuple-element.18), channel_id=1, source_target_pairs={{0,4},{1,5},{2,6},{3,7},{4,0},{5,1},{6,2},{7,3},{8,12},{9,13},{10,... | collective-permute-start | bytes 282632 | tf_op jit(solution)/shard_map/cond/branch_0_fun/ppermute | solution.py:500
  87.7 10.3 %collective-permute-start.8 = (s16[23,16,128]{2,1,0:T(8,128)(2,1)S(1)}, s16[23,16,128]{2,1,0:T(8,128)(2,1)S(1)}, u32[]{:S(2)}, u32[]{:S(2)}) collective-permute-start(s16[23,16,128]{2,1,0:T(8,128)(2,1)S(1)} %get-tuple-element.19), channel_id=1, source_target_pairs={{0,2},{1,3},{2,0},{3,1},{4,6},{5,7},{6,4},{7,5},{8,10},{9,11},{10,... | collective-permute-start | bytes 282632 | tf_op jit(solution)/shard_map/cond/branch_0_fun/ppermute | solution.py:500
  99.9 4.8 %collective-permute-start.9 = (bf16[1,23,16,128]{3,2,1,0:T(8,128)(2,1)S(1)}, bf16[1,23,16,128]{3,2,1,0:T(8,128)(2,1)S(1)}, u32[]{:S(2)}, u32[]{:S(2)}) collective-permute-start(bf16[1,23,16,128]{3,2,1,0:T(8,128)(2,1)S(1)} %bitcast.33), channel_id=1, source_target_pairs={{0,8},{1,9},{2,10},{3,11},{4,12},{5,13},{6,14},{7,15},{8,0},{9,1},... | collective-permute-start | bytes 282632 | tf_op jit(solution)/shard_map/cond/branch_0_fun/ppermute | solution.py:500
  104.7 5.1 %collective-permute-start.10 = (bf16[2,23,16,128]{3,2,1,0:T(8,128)(2,1)S(1)}, bf16[2,23,16,128]{3,2,1,0:T(8,128)(2,1)S(1)}, u32[]{:S(2)}, u32[]{:S(2)}) collective-permute-start(bf16[2,23,16,128]{3,2,1,0:T(8,128)(2,1)S(1)} %pad_maximum_fusion), channel_id=1, source_target_pairs={{0,4},{1,5},{2,6},{3,7},{4,0},{5,1},{6,2},{7,3},{8,12},{9,13},{10,... | collective-permute-start | bytes 565256 | tf_op jit(solution)/shard_map/cond/branch_0_fun/ppermute | solution.py:500
  104.8 6.3 %collective-permute-start.11 = (bf16[1,23,16,128]{3,2,1,0:T(8,128)(2,1)S(1)}, bf16[1,23,16,128]{3,2,1,0:T(8,128)(2,1)S(1)}, u32[]{:S(2)}, u32[]{:S(2)}) collective-permute-start(bf16[1,23,16,128]{3,2,1,0:T(8,128)(2,1)S(1)} %bitcast.35), channel_id=1, source_target_pairs={{0,2},{1,3},{2,0},{3,1},{4,6},{5,7},{6,4},{7,5},{8,10},{9,11},{10,... | collective-permute-start | bytes 282632 | tf_op jit(solution)/shard_map/cond/branch_0_fun/ppermute | solution.py:500
  106.2 4.9 %collective-permute-start.12 = (bf16[1,23,16,128]{3,2,1,0:T(8,128)(2,1)S(1)}, bf16[1,23,16,128]{3,2,1,0:T(8,128)(2,1)S(1)}, u32[]{:S(2)}, u32[]{:S(2)}) collective-permute-start(bf16[1,23,16,128]{3,2,1,0:T(8,128)(2,1)S(1)} %collective-permute-done.9), channel_id=1, source_target_pairs={{0,2},{1,3},{2,0},{3,1},{4,6},{5,7},{6,4},{7,5},{8,10},{9,11},{10,... | collective-permute-start | bytes 282632 | tf_op jit(solution)/shard_map/cond/branch_0_fun/ppermute | solution.py:500
  109.8 6.0 %collective-permute-start.13 = (bf16[2,23,16,128]{3,2,1,0:T(8,128)(2,1)S(1)}, bf16[2,23,16,128]{3,2,1,0:T(8,128)(2,1)S(1)}, u32[]{:S(2)}, u32[]{:S(2)}) collective-permute-start(bf16[2,23,16,128]{3,2,1,0:T(8,128)(2,1)S(1)} %collective-permute-done.10), channel_id=1, source_target_pairs={{0,2},{1,3},{2,0},{3,1},{4,6},{5,7},{6,4},{7,5},{8,10},{9,11},{10,... | collective-permute-start | bytes 565256 | tf_op jit(solution)/shard_map/cond/branch_0_fun/ppermute | solution.py:500
  115.8 6.1 %collective-permute-start.14 = (bf16[8,23,16,128]{3,2,1,0:T(8,128)(2,1)S(1)}, bf16[8,23,16,128]{3,2,1,0:T(8,128)(2,1)S(1)}, u32[]{:S(2)}, u32[]{:S(2)}) collective-permute-start(bf16[8,23,16,128]{3,2,1,0:T(8,128)(2,1)S(1)} %constant_dynamic-update-slice_fusion.refs_0_), channel_id=1, source_target_pairs={{0,1},{1,0},{2,3},{3,2},{4,5},{5,4},{6,7},{7,6},{8,9},{9,8},{10,11... | collective-permute-start | bytes 2261000 | tf_op jit(solution)/shard_map/cond/branch_0_fun/ppermute | solution.py:500
  131.2 51.8 %copy-start = (bf16[256,4096]{1,0:T(8,128)(2,1)S(1)}, bf16[256,4096]{1,0:T(8,128)(2,1)}, u32[]{:S(2)}) copy-start(bf16[256,4096]{1,0:T(8,128)(2,1)} %get-tuple-element.99.normed_ref) | copy-start | bytes 6291460
  131.2 51.7 %copy-start.1 = (f32[256,128]{1,0:T(8,128)S(1)}, f32[256,128]{1,0:T(8,128)}, u32[]{:S(2)}) copy-start(f32[256,128]{1,0:T(8,128)} %get-tuple-element.100.inv_ref) | copy-start | bytes 393220

commit v2 on v1

--- a/solution.py
+++ b/solution.py
@@ -14,6 +14,17 @@
 bound_steps = 256.0
 code_steps = 32000.0
 mebibyte = 1024 * 1024
+
+
+def peer_order(devices):
+    return [device for pair in zip(range(devices // 2), range(devices // 2, devices)) for device in pair]
+
+
+def exchange(blocks):
+    order = peer_order(blocks.shape[0])
+    return lax.all_to_all(
+        blocks, "pb", split_axis=0, concat_axis=0, axis_index_groups=[order], tiled=True
+    )
 
 
 def spread(target, at, value):
@@ -77,9 +88,10 @@
         left = jnp.where((row == 2) & (spot == offset), named, left)
     facts = jnp.concatenate([left, right], axis=1).astype(jnp.bfloat16)
 
-    for part, cut in enumerate(cuts):
-        emb_ref[part, :seqs] = (normed_ref[:, cut].astype(jnp.float32) * inverse).astype(jnp.bfloat16)
-        emb_ref[part, seqs:] = facts
+    for slot, part in enumerate(peer_order(parts)):
+        values = normed_ref[:, cuts[part]].astype(jnp.float32)
+        emb_ref[slot, :seqs] = (values * inverse).astype(jnp.bfloat16)
+        emb_ref[slot, seqs:] = facts
 
 
 def norm_call(last_row, hidden, gain, owners, hard_negatives, parts):
@@ -110,8 +122,12 @@
     wide, picked, picked_too, facts, own, named, sems = refs[-7:]
     seqs = emb_ref.shape[1] - 16
     sent = emb_ref[:, seqs:, :].astype(jnp.float32)
-    own_ref[...] = (2.0 * sent[:, 0, :] + 512.0 * sent[:, 1, :]).astype(jnp.int32)
-    facts[...] = sent[:, 2, :lanes].astype(jnp.int32)
+    places = (2.0 * sent[:, 0, :] + 512.0 * sent[:, 1, :]).astype(jnp.int32)
+    flags = sent[:, 2, :lanes].astype(jnp.int32)
+    order = peer_order(blocks)
+    for slot, block in enumerate(order):
+        own_ref[block : block + 1, :] = places[slot : slot + 1]
+        facts[block : block + 1, :] = flags[slot : slot + 1]
     fetches = [
         pltpu.make_async_copy(own_ref, own, sems.at[0]),
         pltpu.make_async_copy(facts, named, sems.at[1]),
@@ -119,8 +135,8 @@
     for fetch in fetches:
         fetch.start()
 
-    for part in range(blocks):
-        spread(wide, part * seqs, emb_ref[part, :seqs, :].astype(jnp.float32))
+    for slot, part in enumerate(order):
+        spread(wide, part * seqs, emb_ref[slot, :seqs, :].astype(jnp.float32))
     for fetch in fetches:
         fetch.wait()
 
@@ -432,8 +448,8 @@
 
     lax.fori_loop(0, blocks, doc_block, 0)
     slots = out_ref.shape[1]
-    for part in range(blocks):
-        out_ref[part] = gathered(wide, part * slots, slots).astype(jnp.bfloat16)
+    for slot, part in enumerate(peer_order(blocks)):
+        out_ref[slot] = gathered(wide, part * slots, slots).astype(jnp.bfloat16)
 
 
 def grad_call(own, place, parts, queries, documents, blocks, pairs, window):
@@ -464,7 +480,7 @@
 
 def project_kernel(grad_ref, normed_ref, inv_ref, out_ref):
     parts, _, piece = grad_ref.shape
-    cuts = [slice(part * piece, (part + 1) * piece) for part in range(parts)]
+    cuts = [slice(part * piece, (part + 1) * piece) for part in peer_order(parts)]
     inverse = inv_ref[:, :1]
     total = 0.0
     for part, cut in enumerate(cuts):
@@ -547,7 +563,7 @@
     normed, inverse, embedding = norm_call(
         last_row, hidden, final_gain, pair_owner.T, hard_negatives, devices
     )
-    embedded = lax.all_to_all(embedding, "pb", split_axis=0, concat_axis=0, tiled=True)
+    embedded = exchange(embedding)
     most = devices * (window + 1)
     rooms = [most * part // 20 for part in (11, 12, 13, 15, 20)]
     used = devices + jnp.sum(embedded[:, seqs + 2, :window].astype(jnp.float32))
@@ -560,7 +576,7 @@
         ],
         embedded,
     )
-    returned = lax.all_to_all(grads, "pb", split_axis=0, concat_axis=0, tiled=True)
+    returned = exchange(grads)
     return project_call(returned, normed, inverse), loss
 
 

time: 190 us -> 190 us (level); the launches traced: 186 us -> 190 us
  waiting for transfers between devices: 27 us -> 29.6 us
    ppermute x15, waiting for transfers between devices: 27 us -> 29.6 us  [swapped(): return lax.ppermute(value, 'pb', pairs)]
  transfers between devices with their start and end apart: 15 -> 15, of which waited for: 8 -> 9; matrix products, arithmetic and copies ran while one was open for 0% -> 0% of each run, Pallas kernels for 0% -> 0%
where the time goes in v2:
time: 190 us
  blocking collectives  112 us (59%)
  waiting for transfers between devices  29.6 us (16%)
  Pallas kernels  29.5 us (16%)
  starting transfers between devices  16.1 us (8%)
    all_to_all x2, blocking collectives, exchange(): lax.all_to_all(blocks, 'pb', split_axis=0, concat_axis=0, axis_index_grou...  112 us
    ppermute x15, waiting for transfers between devices, swapped(): return lax.ppermute(value, 'pb', pairs)  29.6 us
    ppermute x15, starting transfers between devices, swapped(): return lax.ppermute(value, 'pb', pairs)  16.1 us
    pallas_call x1, Pallas kernels, grad_call(): pl.pallas_call(functools.partial(grad_kernel, blocks, pairs, window), in_...  9.1 us
    pallas_call x1, Pallas kernels, score_call(): pl.pallas_call(functools.partial(score_kernel, blocks, pairs, window), in...  8.14 us
    pallas_call x1, Pallas kernels, norm_call(): pl.pallas_call(norm_kernel, in_specs=[whole, whole, whole, whole, pl.Bloc...  5.65 us
  transfers between devices with their start and end apart: 15, of which 9 were waited for; matrix products, arithmetic and copies ran while one was open for 0% of the time, Pallas kernels for 0%

profile of v2, /device:TPU:1, one launch (start us, length us, event | category | flops | bytes accessed | tf_op | source)
XLA Modules:
  0.0 189.7 jit_solution(3660689529429115440)
XLA Ops:
  0.6 5.7 %norm_rows.1 = (bf16[256,4096]{1,0:T(8,128)(2,1)}, f32[256,128]{1,0:T(8,128)}, bf16[16,272,256]{2,1,0:T(8,128)(2,1)}) custom-call(s32[1,256]{1,0:T(1,128)} %last_ref.1, bf16[256,4096]{1,0:T(8,128)(2,1)} %hidden_ref.1, bf16[4096]{0:T(1024)(128)(2,1)} %gain_ref.1, s32[2,128]{1,0:T(2,128)} %bitcast.36, s32[1,4]{1,0:T(1,128)} %negative_ref.1), custom_call_target="tpu_custom_call" | custom-call | tf_op jit(solution)/shard_map/norm_rows/pallas_call | solution.py:101
  6.3 59.5 %all_to_all.25 = bf16[16,272,256]{2,1,0:T(8,128)(2,1)S(1)} all-to-all(bf16[16,272,256]{2,1,0:T(8,128)(2,1)} %get-tuple-element.97), channel_id=1, replica_groups={{0,8,1,9,2,10,3,11,4,12,5,13,6,14,7,15},{16,24,17,25,18,26,19,27,20,28,..., dimensions={0} | all-to-all | bytes 4456448 | tf_op jit(solution)/shard_map/all_to_all | solution.py:25
  65.8 0.6 fusion
  67.1 66.7 %conditional.1 = (bf16[16,256,256]{2,1,0:T(8,128)(2,1)S(1)}, f32[1]{0:T(128)}) conditional(s32[]{:T(128)} %clamp.3, bf16[16,272,256]{2,1,0:T(8,128)(2,1)S(1)} %all_to_all.25, bf16[16,272,256]{2,1,0:T(8,128)(2,1)S(1)} %all_to_all.25, bf16[16,272,256]{2,1,0:T(8,128)(2,1)S(1)} %all_to_all.25, ...), branch_computations={%region_1.0_spmd, %region_2.0_spmd, %region_3.0_spmd, %region_4.0_... | conditional | flops 167936 | bytes 28770920 | solution.py:571
  67.1 8.1 %partial_scores.6 = (bf16[2048,256]{1,0:T(8,128)(2,1)S(1)}, bf16[2560,256]{1,0:T(8,128)(2,1)S(1)}, f32[8,392,128]{2,1,0:T(8,128)S(1)}, f32[8,392,128]{2,1,0:T(8,...) custom-call(bf16[16,272,256]{2,1,0:T(8,128)(2,1)S(1)} %refs_0_.1), custom_call_target="tpu_custom_call" | custom-call | tf_op jit(solution)/shard_map/cond/branch_1_fun/partial_scores/pallas_call | solution.py:225
  75.3 0.5 collective-permute-start.15
  75.7 0.1 collective-permute-start.16
  75.9 3.0 %collective-permute-done.16.other_top_ref = f32[8,128]{1,0:T(8,128)S(1)} collective-permute-done((f32[8,128]{1,0:T(8,128)S(1)}, f32[8,128]{1,0:T(8,128)S(1)}, u32[]{:S(2)}, u32[]{:S(2)}) %collective-permute-start.16) | collective-permute-done | bytes 4128 | tf_op jit(solution)/shard_map/cond/branch_1_fun/ppermute | solution.py:516
  78.8 1.4 merge_scores.6
  80.3 1.1 collective-permute-start.17
  81.4 2.4 %collective-permute-start.18 = (s16[25,16,128]{2,1,0:T(8,128)(2,1)S(1)}, s16[25,16,128]{2,1,0:T(8,128)(2,1)S(1)}, u32[]{:S(2)}, u32[]{:S(2)}) collective-permute-start(s16[25,16,128]{2,1,0:T(8,128)(2,1)S(1)} %get-tuple-element.31), channel_id=1, source_target_pairs={{0,12},{1,13},{2,14},{3,15},{4,8},{5,9},{6,10},{7,11},{8,4},{9,5},... | collective-permute-start | bytes 307208 | tf_op jit(solution)/shard_map/cond/branch_1_fun/ppermute | solution.py:516
  83.8 3.1 %collective-permute-start.20 = (s16[25,16,128]{2,1,0:T(8,128)(2,1)S(1)}, s16[25,16,128]{2,1,0:T(8,128)(2,1)S(1)}, u32[]{:S(2)}, u32[]{:S(2)}) collective-permute-start(s16[25,16,128]{2,1,0:T(8,128)(2,1)S(1)} %get-tuple-element.33), channel_id=1, source_target_pairs={{0,8},{1,9},{2,10},{3,11},{4,12},{5,13},{6,14},{7,15},{8,0},{9,1},... | collective-permute-start | bytes 307208 | tf_op jit(solution)/shard_map/cond/branch_1_fun/ppermute | solution.py:516
  86.9 0.3 collective-permute-done.17.refs_0_
  87.2 1.3 collective-permute-start.22
  88.5 0.1 collective-permute-done.18.refs_1_
  88.6 1.0 collective-permute-start.23
  89.6 8.4 %collective-permute-done.19.refs_2_ = s16[25,16,128]{2,1,0:T(8,128)(2,1)S(1)} collective-permute-done((s16[25,16,128]{2,1,0:T(8,128)(2,1)S(1)}, s16[25,16,128]{2,1,0:T(8,128)(2,1)S(1)}, u32[]{:S(2)}, u32[]{:S(2)}) %collective-permute-start.19) | collective-permute-done | bytes 102432 | tf_op jit(solution)/shard_map/cond/branch_1_fun/ppermute | solution.py:516
  98.1 1.8 collective-permute-done.20.refs_3_
  99.9 1.9 %softmax_rows.6 = bf16[25,16,128]{2,1,0:T(8,128)(2,1)S(1)} custom-call(s32[5,16]{1,0:T(8,128)S(1)} %get-tuple-element.23.place_ref, f32[384,128]{1,0:T(8,128)S(1)} %get-tuple-element.29.own_ref, s16[25,16,128]{2,1,0:T(8,128)(2,1)S(1)} %collective-permute-done.17.refs_0_, s16[25,16,128]{2,1,0:T(8,128)(2,1)S(1)} %collective-permute-done.18.refs_1_, ...), custom_call_target="tpu_custom_call" | custom-call | tf_op jit(solution)/shard_map/cond/branch_1_fun/softmax_rows/pallas_call | solution.py:357
  101.8 0.1 collective-permute-start.24
  101.9 4.9 %collective-permute-done.24 = bf16[1,25,16,128]{3,2,1,0:T(8,128)(2,1)S(1)} collective-permute-done((bf16[1,25,16,128]{3,2,1,0:T(8,128)(2,1)S(1)}, bf16[1,25,16,128]{3,2,1,0:T(8,128)(2,1)S(1)}, u32[]{:S(2)}, u32[]{:S(2)}) %collective-permute-start.24) | collective-permute-done | bytes 102432 | tf_op jit(solution)/shard_map/cond/branch_1_fun/ppermute | solution.py:516
  106.8 0.1 collective-permute-start.25
  106.9 0.8 collective-permute-start.26
  107.6 0.8 collective-permute-start.27
  108.4 3.8 %collective-permute-done.25 = bf16[2,25,16,128]{3,2,1,0:T(8,128)(2,1)S(1)} collective-permute-done((bf16[2,25,16,128]{3,2,1,0:T(8,128)(2,1)S(1)}, bf16[2,25,16,128]{3,2,1,0:T(8,128)(2,1)S(1)}, u32[]{:S(2)}, u32[]{:S(2)}) %collective-permute-start.25) | collective-permute-done | bytes 204832 | tf_op jit(solution)/shard_map/cond/branch_1_fun/ppermute | solution.py:516
  112.3 0.7 collective-permute-start.28
  113.0 5.2 %collective-permute-done.28 = bf16[2,25,16,128]{3,2,1,0:T(8,128)(2,1)S(1)} collective-permute-done((bf16[2,25,16,128]{3,2,1,0:T(8,128)(2,1)S(1)}, bf16[2,25,16,128]{3,2,1,0:T(8,128)(2,1)S(1)}, u32[]{:S(2)}, u32[]{:S(2)}) %collective-permute-start.28) | collective-permute-done | bytes 204832 | tf_op jit(solution)/shard_map/cond/branch_1_fun/ppermute | solution.py:516
  118.3 4.2 %collective-permute-start.29 = (bf16[8,25,16,128]{3,2,1,0:T(8,128)(2,1)S(1)}, bf16[8,25,16,128]{3,2,1,0:T(8,128)(2,1)S(1)}, u32[]{:S(2)}, u32[]{:S(2)}) collective-permute-start(bf16[8,25,16,128]{3,2,1,0:T(8,128)(2,1)S(1)} %constant_dynamic-update-slice_fusion.6.refs_0_), channel_id=1, source_target_pairs={{0,1},{1,0},{2,3},{3,2},{4,5},{5,4},{6,7},{7,6},{8,9},{9,8},{10,11... | collective-permute-start | bytes 2457608 | tf_op jit(solution)/shard_map/cond/branch_1_fun/ppermute | solution.py:516
  122.5 2.0 %collective-permute-done.29.refs_1_ = bf16[8,25,16,128]{3,2,1,0:T(8,128)(2,1)S(1)} collective-permute-done((bf16[8,25,16,128]{3,2,1,0:T(8,128)(2,1)S(1)}, bf16[8,25,16,128]{3,2,1,0:T(8,128)(2,1)S(1)}, u32[]{:S(2)}, u32[]{:S(2)}) %collective-permute-start.29) | collective-permute-done | bytes 819232 | tf_op jit(solution)/shard_map/cond/branch_1_fun/ppermute | solution.py:516
  124.5 9.1 %slice_grads.6 = (bf16[16,256,256]{2,1,0:T(8,128)(2,1)S(1)}, f32[1,128]{1,0:T(1,128)}) custom-call(s32[16,256]{1,0:T(8,128)S(1)} %get-tuple-element.22.own_ref, s32[5,16]{1,0:T(8,128)S(1)} %get-tuple-element.23.place_ref, bf16[2048,256]{1,0:T(8,128)(2,1)S(1)} %get-tuple-element.24.q_ref, bf16[2560,256]{1,0:T(8,128)(2,1)S(1)} %get-tuple-element.25.d_ref, ...), custom_call_target="tpu_custom_call" | custom-call | tf_op jit(solution)/shard_map/cond/branch_1_fun/slice_grads/pallas_call | solution.py:461
  133.8 52.6 %all_to_all.26.grad_ref = bf16[16,256,256]{2,1,0:T(8,128)(2,1)S(1)} all-to-all(bf16[16,256,256]{2,1,0:T(8,128)(2,1)S(1)} %get-tuple-element.98), channel_id=1, replica_groups={{0,8,1,9,2,10,3,11,4,12,5,13,6,14,7,15},{16,24,17,25,18,26,19,27,20,28,..., dimensions={0} | all-to-all | bytes 4194304 | tf_op jit(solution)/shard_map/all_to_all | solution.py:25
  186.4 3.3 %project_out.1 = f32[256,4096]{1,0:T(8,128)} custom-call(bf16[16,256,256]{2,1,0:T(8,128)(2,1)S(1)} %all_to_all.26.grad_ref, bf16[256,4096]{1,0:T(8,128)(2,1)S(1)} %copy-done, f32[256,128]{1,0:T(8,128)S(1)} %copy-done.1), custom_call_target="tpu_custom_call" | custom-call | tf_op jit(solution)/shard_map/project_out/pallas_call | solution.py:499
  (19 shorter events, 0.2 us)
Async XLA Ops:
  75.3 3.5 %collective-permute-start.15 = (f32[8,392,128]{2,1,0:T(8,128)S(1)}, f32[8,392,128]{2,1,0:T(8,128)S(1)}, u32[]{:S(2)}, u32[]{:S(2)}) collective-permute-start(f32[8,392,128]{2,1,0:T(8,128)S(1)} %get-tuple-element.27), channel_id=1, source_target_pairs={{0,1},{1,0},{2,3},{3,2},{4,5},{5,4},{6,7},{7,6},{8,9},{9,8},{10,11... | collective-permute-start | bytes 4816904 | tf_op jit(solution)/shard_map/cond/branch_1_fun/ppermute | solution.py:516
  75.7 3.1 %collective-permute-start.16 = (f32[8,128]{1,0:T(8,128)S(1)}, f32[8,128]{1,0:T(8,128)S(1)}, u32[]{:S(2)}, u32[]{:S(2)}) collective-permute-start(f32[8,128]{1,0:T(8,128)S(1)} %get-tuple-element.28.top_ref), channel_id=1, source_target_pairs={{0,1},{1,0},{2,3},{3,2},{4,5},{5,4},{6,7},{7,6},{8,9},{9,8},{10,11... | collective-permute-start | bytes 12296 | tf_op jit(solution)/shard_map/cond/branch_1_fun/ppermute | solution.py:516
  80.3 6.9 %collective-permute-start.17 = (s16[25,16,128]{2,1,0:T(8,128)(2,1)S(1)}, s16[25,16,128]{2,1,0:T(8,128)(2,1)S(1)}, u32[]{:S(2)}, u32[]{:S(2)}) collective-permute-start(s16[25,16,128]{2,1,0:T(8,128)(2,1)S(1)} %get-tuple-element.30), channel_id=1, source_target_pairs={{0,14},{1,15},{2,12},{3,13},{4,10},{5,11},{6,8},{7,9},{8,6},{9,7},... | collective-permute-start | bytes 307208 | tf_op jit(solution)/shard_map/cond/branch_1_fun/ppermute | solution.py:516
  81.4 7.3 %collective-permute-start.18 = (s16[25,16,128]{2,1,0:T(8,128)(2,1)S(1)}, s16[25,16,128]{2,1,0:T(8,128)(2,1)S(1)}, u32[]{:S(2)}, u32[]{:S(2)}) collective-permute-start(s16[25,16,128]{2,1,0:T(8,128)(2,1)S(1)} %get-tuple-element.31), channel_id=1, source_target_pairs={{0,12},{1,13},{2,14},{3,15},{4,8},{5,9},{6,10},{7,11},{8,4},{9,5},... | collective-permute-start | bytes 307208 | tf_op jit(solution)/shard_map/cond/branch_1_fun/ppermute | solution.py:516
  83.8 14.3 %collective-permute-start.19 = (s16[25,16,128]{2,1,0:T(8,128)(2,1)S(1)}, s16[25,16,128]{2,1,0:T(8,128)(2,1)S(1)}, u32[]{:S(2)}, u32[]{:S(2)}) collective-permute-start(s16[25,16,128]{2,1,0:T(8,128)(2,1)S(1)} %get-tuple-element.32), channel_id=1, source_target_pairs={{0,10},{1,11},{2,8},{3,9},{4,14},{5,15},{6,12},{7,13},{8,2},{9,3},... | collective-permute-start | bytes 307208 | tf_op jit(solution)/shard_map/cond/branch_1_fun/ppermute | solution.py:516
  83.8 16.1 %collective-permute-start.20 = (s16[25,16,128]{2,1,0:T(8,128)(2,1)S(1)}, s16[25,16,128]{2,1,0:T(8,128)(2,1)S(1)}, u32[]{:S(2)}, u32[]{:S(2)}) collective-permute-start(s16[25,16,128]{2,1,0:T(8,128)(2,1)S(1)} %get-tuple-element.33), channel_id=1, source_target_pairs={{0,8},{1,9},{2,10},{3,11},{4,12},{5,13},{6,14},{7,15},{8,0},{9,1},... | collective-permute-start | bytes 307208 | tf_op jit(solution)/shard_map/cond/branch_1_fun/ppermute | solution.py:516
  86.8 13.1 %collective-permute-start.21 = (s16[25,16,128]{2,1,0:T(8,128)(2,1)S(1)}, s16[25,16,128]{2,1,0:T(8,128)(2,1)S(1)}, u32[]{:S(2)}, u32[]{:S(2)}) collective-permute-start(s16[25,16,128]{2,1,0:T(8,128)(2,1)S(1)} %get-tuple-element.34), channel_id=1, source_target_pairs={{0,6},{1,7},{2,4},{3,5},{4,2},{5,3},{6,0},{7,1},{8,14},{9,15},{10,... | collective-permute-start | bytes 307208 | tf_op jit(solution)/shard_map/cond/branch_1_fun/ppermute | solution.py:516
  87.2 12.8 %collective-permute-start.22 = (s16[25,16,128]{2,1,0:T(8,128)(2,1)S(1)}, s16[25,16,128]{2,1,0:T(8,128)(2,1)S(1)}, u32[]{:S(2)}, u32[]{:S(2)}) collective-permute-start(s16[25,16,128]{2,1,0:T(8,128)(2,1)S(1)} %get-tuple-element.35), channel_id=1, source_target_pairs={{0,4},{1,5},{2,6},{3,7},{4,0},{5,1},{6,2},{7,3},{8,12},{9,13},{10,... | collective-permute-start | bytes 307208 | tf_op jit(solution)/shard_map/cond/branch_1_fun/ppermute | solution.py:516
  88.6 11.3 %collective-permute-start.23 = (s16[25,16,128]{2,1,0:T(8,128)(2,1)S(1)}, s16[25,16,128]{2,1,0:T(8,128)(2,1)S(1)}, u32[]{:S(2)}, u32[]{:S(2)}) collective-permute-start(s16[25,16,128]{2,1,0:T(8,128)(2,1)S(1)} %get-tuple-element.36), channel_id=1, source_target_pairs={{0,2},{1,3},{2,0},{3,1},{4,6},{5,7},{6,4},{7,5},{8,10},{9,11},{10,... | collective-permute-start | bytes 307208 | tf_op jit(solution)/shard_map/cond/branch_1_fun/ppermute | solution.py:516
  101.8 4.9 %collective-permute-start.24 = (bf16[1,25,16,128]{3,2,1,0:T(8,128)(2,1)S(1)}, bf16[1,25,16,128]{3,2,1,0:T(8,128)(2,1)S(1)}, u32[]{:S(2)}, u32[]{:S(2)}) collective-permute-start(bf16[1,25,16,128]{3,2,1,0:T(8,128)(2,1)S(1)} %bitcast.30), channel_id=1, source_target_pairs={{0,8},{1,9},{2,10},{3,11},{4,12},{5,13},{6,14},{7,15},{8,0},{9,1},... | collective-permute-start | bytes 307208 | tf_op jit(solution)/shard_map/cond/branch_1_fun/ppermute | solution.py:516
  106.8 5.5 %collective-permute-start.25 = (bf16[2,25,16,128]{3,2,1,0:T(8,128)(2,1)S(1)}, bf16[2,25,16,128]{3,2,1,0:T(8,128)(2,1)S(1)}, u32[]{:S(2)}, u32[]{:S(2)}) collective-permute-start(bf16[2,25,16,128]{3,2,1,0:T(8,128)(2,1)S(1)} %pad_maximum_fusion.1), channel_id=1, source_target_pairs={{0,4},{1,5},{2,6},{3,7},{4,0},{5,1},{6,2},{7,3},{8,12},{9,13},{10,... | collective-permute-start | bytes 614408 | tf_op jit(solution)/shard_map/cond/branch_1_fun/ppermute | solution.py:516
  106.9 6.1 %collective-permute-start.26 = (bf16[1,25,16,128]{3,2,1,0:T(8,128)(2,1)S(1)}, bf16[1,25,16,128]{3,2,1,0:T(8,128)(2,1)S(1)}, u32[]{:S(2)}, u32[]{:S(2)}) collective-permute-start(bf16[1,25,16,128]{3,2,1,0:T(8,128)(2,1)S(1)} %bitcast.32), channel_id=1, source_target_pairs={{0,2},{1,3},{2,0},{3,1},{4,6},{5,7},{6,4},{7,5},{8,10},{9,11},{10,... | collective-permute-start | bytes 307208 | tf_op jit(solution)/shard_map/cond/branch_1_fun/ppermute | solution.py:516
  107.6 5.4 %collective-permute-start.27 = (bf16[1,25,16,128]{3,2,1,0:T(8,128)(2,1)S(1)}, bf16[1,25,16,128]{3,2,1,0:T(8,128)(2,1)S(1)}, u32[]{:S(2)}, u32[]{:S(2)}) collective-permute-start(bf16[1,25,16,128]{3,2,1,0:T(8,128)(2,1)S(1)} %collective-permute-done.24), channel_id=1, source_target_pairs={{0,2},{1,3},{2,0},{3,1},{4,6},{5,7},{6,4},{7,5},{8,10},{9,11},{10,... | collective-permute-start | bytes 307208 | tf_op jit(solution)/shard_map/cond/branch_1_fun/ppermute | solution.py:516
  112.3 6.0 %collective-permute-start.28 = (bf16[2,25,16,128]{3,2,1,0:T(8,128)(2,1)S(1)}, bf16[2,25,16,128]{3,2,1,0:T(8,128)(2,1)S(1)}, u32[]{:S(2)}, u32[]{:S(2)}) collective-permute-start(bf16[2,25,16,128]{3,2,1,0:T(8,128)(2,1)S(1)} %collective-permute-done.25), channel_id=1, source_target_pairs={{0,2},{1,3},{2,0},{3,1},{4,6},{5,7},{6,4},{7,5},{8,10},{9,11},{10,... | collective-permute-start | bytes 614408 | tf_op jit(solution)/shard_map/cond/branch_1_fun/ppermute | solution.py:516
  118.3 6.2 %collective-permute-start.29 = (bf16[8,25,16,128]{3,2,1,0:T(8,128)(2,1)S(1)}, bf16[8,25,16,128]{3,2,1,0:T(8,128)(2,1)S(1)}, u32[]{:S(2)}, u32[]{:S(2)}) collective-permute-start(bf16[8,25,16,128]{3,2,1,0:T(8,128)(2,1)S(1)} %constant_dynamic-update-slice_fusion.6.refs_0_), channel_id=1, source_target_pairs={{0,1},{1,0},{2,3},{3,2},{4,5},{5,4},{6,7},{7,6},{8,9},{9,8},{10,11... | collective-permute-start | bytes 2457608 | tf_op jit(solution)/shard_map/cond/branch_1_fun/ppermute | solution.py:516
  133.8 52.6 %copy-start = (bf16[256,4096]{1,0:T(8,128)(2,1)S(1)}, bf16[256,4096]{1,0:T(8,128)(2,1)}, u32[]{:S(2)}) copy-start(bf16[256,4096]{1,0:T(8,128)(2,1)} %get-tuple-element.99.normed_ref) | copy-start | bytes 6291460
  133.8 52.6 %copy-start.1 = (f32[256,128]{1,0:T(8,128)S(1)}, f32[256,128]{1,0:T(8,128)}, u32[]{:S(2)}) copy-start(f32[256,128]{1,0:T(8,128)} %get-tuple-element.100.inv_ref) | copy-start | bytes 393220

commit v3 on v1

--- a/solution.py
+++ b/solution.py
@@ -13,6 +13,7 @@
 lanes = 128
 bound_steps = 256.0
 code_steps = 32000.0
+score_limit = 51.0
 mebibyte = 1024 * 1024
 
 
@@ -68,8 +69,8 @@
     owners = owner_ref[...].astype(jnp.float32)
     high = jnp.floor(owners * (1.0 / 256.0))
     low = owners - 256.0 * high
-    row = lax.broadcasted_iota(jnp.int32, (16, pairs), 0)
-    spot = lax.broadcasted_iota(jnp.int32, (16, pairs), 1)
+    row = lax.broadcasted_iota(jnp.int32, (8, pairs), 0)
+    spot = lax.broadcasted_iota(jnp.int32, (8, pairs), 1)
     left = jnp.where(row == 0, low[:1], jnp.where(row == 1, high[:1], 0.0))
     right = jnp.where(row == 0, low[1:2], jnp.where(row == 1, high[1:2], 0.0))
     for offset in range(negative_ref.shape[1]):
@@ -93,7 +94,7 @@
         out_shape=[
             jax.ShapeDtypeStruct((seqs, width), jnp.bfloat16),
             jax.ShapeDtypeStruct((seqs, lanes), jnp.float32),
-            jax.ShapeDtypeStruct((parts, seqs + 16, piece), jnp.bfloat16),
+            jax.ShapeDtypeStruct((parts, seqs + 8, piece), jnp.bfloat16),
         ],
         compiler_params=pltpu.CompilerParams(vmem_limit_bytes=56 * mebibyte),
         name="norm_rows",
@@ -108,7 +109,7 @@
 ):
     emb_ref, q_ref, d_ref, mine_ref, other_ref, top_ref, own_ref, place_ref = refs[:-7]
     wide, picked, picked_too, facts, own, named, sems = refs[-7:]
-    seqs = emb_ref.shape[1] - 16
+    seqs = emb_ref.shape[1] - 8
     sent = emb_ref[:, seqs:, :].astype(jnp.float32)
     own_ref[...] = (2.0 * sent[:, 0, :] + 512.0 * sent[:, 1, :]).astype(jnp.int32)
     facts[...] = sent[:, 2, :lanes].astype(jnp.int32)
@@ -220,7 +221,7 @@
             jax.ShapeDtypeStruct((window + 1, blocks), jnp.int32),
         ],
         scratch_shapes=[
-            pltpu.VMEM((2 * blocks * (rows - 16), lanes), jnp.float32),
+            pltpu.VMEM((2 * blocks * (rows - 8), lanes), jnp.float32),
             pltpu.VMEM((4 * pairs, lanes), jnp.float32),
             pltpu.VMEM((4 * pairs, lanes), jnp.float32),
             pltpu.VMEM((blocks, lanes), jnp.int32),
@@ -233,31 +234,42 @@
     )(embedded)
 
 
+def coded(values, scale):
+    return jnp.round(values * scale).astype(jnp.int32).astype(jnp.int16)
+
+
+def decoded(codes, scale):
+    return codes.astype(jnp.int32).astype(jnp.float32) * scale
+
+
+def highest(values):
+    return jnp.max(jnp.max(values, axis=1, keepdims=True), axis=0, keepdims=True)
+
+
 def merge_kernel(mine_ref, other_ref, top_ref, other_top_ref, own_ref, *code_refs):
-    rows, pairs = own_ref.shape
-    steps = code_refs[0].shape[0] - 1
+    _, rows, pairs = own_ref.shape
+    steps = code_refs[0].shape[1] - 1
     fine = rows // steps // 2
     chip = lax.axis_index("pb") // 2
-
-    def highest(ref):
-        return jnp.max(jnp.max(ref[...], axis=1, keepdims=True), axis=0, keepdims=True)
-
-    top = highest(top_ref) + highest(other_top_ref)
+    across = mine_ref.shape[0] // 2
+    top = jnp.minimum(highest(top_ref[...]) + highest(other_top_ref[...]), score_limit)
     bound = jnp.ceil(top * bound_steps) + 1.0
     scale = code_steps * bound_steps / bound
-    own_ref[...] = mine_ref[chip, :rows] + other_ref[chip, :rows]
-    for hop, code_ref in enumerate(code_refs):
-        target = chip ^ (hop + 1)
-
-        def encode(step, carry):
-            at = pl.multiple_of(step * 2 * fine, 2 * fine)
-            there = pl.ds(at, 2 * fine)
-            codes = jnp.round((mine_ref[target, there, :] + other_ref[target, there, :]) * scale)
-            code_ref[step] = codes.astype(jnp.int32).astype(jnp.int16)
-            return carry
-
-        lax.fori_loop(0, steps, encode, 0)
-        code_ref[steps] = jnp.broadcast_to(bound, (2 * fine, pairs)).astype(jnp.int32).astype(jnp.int16)
+    sent_bound = jnp.broadcast_to(bound, (2 * fine, pairs)).astype(jnp.int32).astype(jnp.int16)
+    for which in range(2):
+        target = chip ^ (which * across)
+        own_ref[which] = mine_ref[target, :rows] + other_ref[target, :rows]
+        for hop, code_ref in enumerate(code_refs):
+            near = target ^ (hop + 1)
+
+            def encode(step, carry):
+                there = pl.ds(pl.multiple_of(step * 2 * fine, 2 * fine), 2 * fine)
+                values = mine_ref[near, there, :] + other_ref[near, there, :]
+                code_ref[which, step] = coded(values, scale)
+                return carry
+
+            lax.fori_loop(0, steps, encode, 0)
+            code_ref[which, steps] = sent_bound
 
 
 def merge_call(mine, other, top, other_top, blocks):
@@ -265,15 +277,63 @@
     fine = pairs // blocks
     rows = rows - fine
     whole = pl.BlockSpec(memory_space=pltpu.VMEM)
-    coded = jax.ShapeDtypeStruct((rows // (2 * fine) + 1, 2 * fine, pairs), jnp.int16)
+    codes = jax.ShapeDtypeStruct((2, rows // (2 * fine) + 1, 2 * fine, pairs), jnp.int16)
+    near = chips // 2 - 1
     return pl.pallas_call(
         merge_kernel,
         in_specs=[whole] * 4,
-        out_specs=[whole] * chips,
-        out_shape=[jax.ShapeDtypeStruct((rows, pairs), jnp.float32)] + [coded] * (chips - 1),
+        out_specs=[whole] * (near + 1),
+        out_shape=[jax.ShapeDtypeStruct((2, rows, pairs), jnp.float32)] + [codes] * near,
         compiler_params=pltpu.CompilerParams(vmem_limit_bytes=12 * mebibyte),
         name="merge_scores",
     )(mine, other, top, other_top)
+
+
+def half_kernel(own_ref, *refs):
+    near_refs, (sum_ref, code_ref, sums) = refs[:-3], refs[-3:]
+    steps, deep, pairs = code_ref.shape
+    steps = steps - 1
+    unit = 1.0 / (code_steps * bound_steps)
+    scales = [decoded(ref[0, steps], unit) for ref in near_refs]
+
+    def add(step, top):
+        there = pl.ds(pl.multiple_of(step * deep, deep), deep)
+        here, over = own_ref[0, there, :], own_ref[1, there, :]
+        for ref, scale in zip(near_refs, scales):
+            here = here + decoded(ref[0, step], scale)
+            over = over + decoded(ref[1, step], scale)
+        sum_ref[there, :] = here
+        sums[there, :] = over
+        return jnp.maximum(top, jnp.abs(over))
+
+    top = lax.fori_loop(0, steps, add, jnp.zeros((deep, pairs), jnp.float32))
+    bound = jnp.ceil(highest(top) * bound_steps) + 1.0
+    scale = code_steps * bound_steps / bound
+
+    def encode(step, carry):
+        there = pl.ds(pl.multiple_of(step * deep, deep), deep)
+        code_ref[step] = coded(sums[there, :], scale)
+        return carry
+
+    lax.fori_loop(0, steps, encode, 0)
+    code_ref[steps] = jnp.broadcast_to(bound, (deep, pairs)).astype(jnp.int32).astype(jnp.int16)
+
+
+def half_call(own, near):
+    _, rows, pairs = own.shape
+    whole = pl.BlockSpec(memory_space=pltpu.VMEM)
+    return pl.pallas_call(
+        half_kernel,
+        in_specs=[whole] * (1 + len(near)),
+        out_specs=[whole, whole],
+        out_shape=[
+            jax.ShapeDtypeStruct((rows, pairs), jnp.float32),
+            jax.ShapeDtypeStruct(near[0].shape[1:], jnp.int16),
+        ],
+        scratch_shapes=[pltpu.VMEM((rows, pairs), jnp.float32)],
+        compiler_params=pltpu.CompilerParams(vmem_limit_bytes=8 * mebibyte),
+        name="half_scores",
+    )(own, *near)
 
 
 def softmax_kernel(blocks, window, place_ref, own_ref, *refs):
@@ -533,7 +593,9 @@
         embedded, room, devices, pairs, window
     )
     own_scores, *codes = merge_call(mine, swapped(other, 1), top, swapped(top, 1), devices)
-    codes = [swapped(codes[hop], 2 * (hop + 1)) for hop in reversed(range(len(codes)))]
+    near = [swapped(codes[hop], 2 * (hop + 1)) for hop in reversed(range(len(codes)))]
+    own_scores, over = half_call(own_scores, near)
+    codes = [swapped(over, devices // 2)]
     parts = gather_all(softmax_call(place, own_scores, codes, devices, window))
     grads, loss = grad_call(own, place, parts, queries, documents, devices, pairs, window)
     return grads, loss[0, :1]

time: 190 us -> 188 us (0.989); the launches traced: 186 us -> 188 us
  waiting for transfers between devices: 27 us -> 36.8 us
  starting transfers between devices: 16.6 us -> 8.96 us
    ppermute x15 -> x12, waiting for transfers between devices: 27 us -> 36.8 us  [swapped(): return lax.ppermute(value, 'pb', pairs)]
    ppermute x15 -> x12, starting transfers between devices: 16.6 us -> 8.96 us  [swapped(): return lax.ppermute(value, 'pb', pairs)]
  transfers between devices with their start and end apart: 15 -> 12, of which waited for: 8 -> 9; matrix products, arithmetic and copies ran while one was open for 0% -> 0% of each run, Pallas kernels for 0% -> 0%
where the time goes in v3:
time: 188 us
  blocking collectives  110 us (59%)
  waiting for transfers between devices  36.8 us (20%)
  Pallas kernels  29.7 us (16%)
  starting transfers between devices  8.96 us (5%)
    all_to_all x1, blocking collectives, feature_plan(): lax.all_to_all(embedding, 'pb', split_axis=0, concat_axis=0, tiled=True)  58 us
    all_to_all x1, blocking collectives, feature_plan(): lax.all_to_all(grads, 'pb', split_axis=0, concat_axis=0, tiled=True)  52.1 us
    ppermute x12, waiting for transfers between devices, swapped(): return lax.ppermute(value, 'pb', pairs)  36.8 us
    pallas_call x1, Pallas kernels, grad_call(): pl.pallas_call(functools.partial(grad_kernel, blocks, pairs, window), in_...  9.1 us
    ppermute x12, starting transfers between devices, swapped(): return lax.ppermute(value, 'pb', pairs)  8.96 us
    pallas_call x1, Pallas kernels, score_call(): pl.pallas_call(functools.partial(score_kernel, blocks, pairs, window), in...  8.13 us
    pallas_call x1, Pallas kernels, norm_call(): pl.pallas_call(norm_kernel, in_specs=[whole, whole, whole, whole, pl.Bloc...  5.63 us
  transfers between devices with their start and end apart: 12, of which 9 were waited for; matrix products, arithmetic and copies ran while one was open for 0% of the time, Pallas kernels for 0%

profile of v3, /device:TPU:1, one launch (start us, length us, event | category | flops | bytes accessed | tf_op | source)
XLA Modules:
  0.0 187.9 jit_solution(9980997960330280177)
XLA Ops:
  0.6 5.6 %norm_rows.1 = (bf16[256,4096]{1,0:T(8,128)(2,1)}, f32[256,128]{1,0:T(8,128)}, bf16[16,264,256]{2,1,0:T(8,128)(2,1)}) custom-call(s32[1,256]{1,0:T(1,128)} %last_ref.1, bf16[256,4096]{1,0:T(8,128)(2,1)} %hidden_ref.1, bf16[4096]{0:T(1024)(128)(2,1)} %gain_ref.1, s32[2,128]{1,0:T(2,128)} %bitcast.36, s32[1,4]{1,0:T(1,128)} %negative_ref.1), custom_call_target="tpu_custom_call" | custom-call | tf_op jit(solution)/shard_map/norm_rows/pallas_call | solution.py:90
  6.3 58.0 %all_to_all.25 = bf16[16,264,256]{2,1,0:T(8,128)(2,1)S(1)} all-to-all(bf16[16,264,256]{2,1,0:T(8,128)(2,1)} %get-tuple-element.87), channel_id=1, replica_groups=mesh['groups'=2,'pb'=16] {'pb'}, dimensions={0} | all-to-all | bytes 4325376 | tf_op jit(solution)/shard_map/all_to_all | solution.py:612
  64.3 0.6 fusion
  65.6 67.0 %conditional.1 = (bf16[16,256,256]{2,1,0:T(8,128)(2,1)S(1)}, f32[1]{0:T(128)}) conditional(s32[]{:T(128)} %clamp.3, bf16[16,264,256]{2,1,0:T(8,128)(2,1)S(1)} %all_to_all.25, bf16[16,264,256]{2,1,0:T(8,128)(2,1)S(1)} %all_to_all.25, bf16[16,264,256]{2,1,0:T(8,128)(2,1)S(1)} %all_to_all.25, ...), branch_computations={%region_1.0_spmd, %region_2.0_spmd, %region_3.0_spmd, %region_4.0_... | conditional | flops 167936 | bytes 28770800 | solution.py:617
  65.6 8.1 %partial_scores.6 = (bf16[2048,256]{1,0:T(8,128)(2,1)S(1)}, bf16[2560,256]{1,0:T(8,128)(2,1)S(1)}, f32[8,392,128]{2,1,0:T(8,128)S(1)}, f32[8,392,128]{2,1,0:T(8,...) custom-call(bf16[16,264,256]{2,1,0:T(8,128)(2,1)S(1)} %refs_0_.1), custom_call_target="tpu_custom_call" | custom-call | tf_op jit(solution)/shard_map/cond/branch_1_fun/partial_scores/pallas_call | solution.py:210
  73.8 0.5 collective-permute-start.12
  74.2 0.1 collective-permute-start.13
  74.3 3.0 %collective-permute-done.13.other_top_ref = f32[8,128]{1,0:T(8,128)S(1)} collective-permute-done((f32[8,128]{1,0:T(8,128)S(1)}, f32[8,128]{1,0:T(8,128)S(1)}, u32[]{:S(2)}, u32[]{:S(2)}) %collective-permute-start.13) | collective-permute-done | bytes 4128 | tf_op jit(solution)/shard_map/cond/branch_1_fun/ppermute | solution.py:560
  77.3 1.2 merge_scores.6
  78.5 0.5 collective-permute-start.14
  79.0 1.1 collective-permute-start.15
  80.1 1.1 collective-permute-start.16
  81.3 4.6 %collective-permute-done.14.refs_0_ = s16[2,25,16,128]{3,2,1,0:T(8,128)(2,1)S(1)} collective-permute-done((s16[2,25,16,128]{3,2,1,0:T(8,128)(2,1)S(1)}, s16[2,25,16,128]{3,2,1,0:T(8,128)(2,1)S(1)}, u32[]{:S(2)}, u32[]{:S(2)}) %collective-permute-start.14) | collective-permute-done | bytes 204832 | tf_op jit(solution)/shard_map/cond/branch_1_fun/ppermute | solution.py:560
  85.8 3.5 %collective-permute-done.15.refs_1_ = s16[2,25,16,128]{3,2,1,0:T(8,128)(2,1)S(1)} collective-permute-done((s16[2,25,16,128]{3,2,1,0:T(8,128)(2,1)S(1)}, s16[2,25,16,128]{3,2,1,0:T(8,128)(2,1)S(1)}, u32[]{:S(2)}, u32[]{:S(2)}) %collective-permute-start.15) | collective-permute-done | bytes 204832 | tf_op jit(solution)/shard_map/cond/branch_1_fun/ppermute | solution.py:560
  89.4 1.5 collective-permute-done.16.refs_2_
  90.9 0.5 half_scores.6
  91.5 0.6 collective-permute-start.17
  92.1 7.3 %collective-permute-done.17.refs_0_ = s16[25,16,128]{2,1,0:T(8,128)(2,1)S(1)} collective-permute-done((s16[25,16,128]{2,1,0:T(8,128)(2,1)S(1)}, s16[25,16,128]{2,1,0:T(8,128)(2,1)S(1)}, u32[]{:S(2)}, u32[]{:S(2)}) %collective-permute-start.17) | collective-permute-done | bytes 102432 | tf_op jit(solution)/shard_map/cond/branch_1_fun/ppermute | solution.py:560
  99.3 1.7 softmax_rows.6
  101.1 0.1 collective-permute-start.18
  101.1 6.5 %collective-permute-done.18 = bf16[1,25,16,128]{3,2,1,0:T(8,128)(2,1)S(1)} collective-permute-done((bf16[1,25,16,128]{3,2,1,0:T(8,128)(2,1)S(1)}, bf16[1,25,16,128]{3,2,1,0:T(8,128)(2,1)S(1)}, u32[]{:S(2)}, u32[]{:S(2)}) %collective-permute-start.18) | collective-permute-done | bytes 102432 | tf_op jit(solution)/shard_map/cond/branch_1_fun/ppermute | solution.py:560
  107.6 0.1 collective-permute-start.19
  107.7 0.9 collective-permute-start.20
  108.6 0.6 collective-permute-start.21
  109.3 4.5 %collective-permute-done.19 = bf16[2,25,16,128]{3,2,1,0:T(8,128)(2,1)S(1)} collective-permute-done((bf16[2,25,16,128]{3,2,1,0:T(8,128)(2,1)S(1)}, bf16[2,25,16,128]{3,2,1,0:T(8,128)(2,1)S(1)}, u32[]{:S(2)}, u32[]{:S(2)}) %collective-permute-start.19) | collective-permute-done | bytes 204832 | tf_op jit(solution)/shard_map/cond/branch_1_fun/ppermute | solution.py:560
  113.7 0.9 collective-permute-start.22
  114.8 4.1 %collective-permute-done.22 = bf16[2,25,16,128]{3,2,1,0:T(8,128)(2,1)S(1)} collective-permute-done((bf16[2,25,16,128]{3,2,1,0:T(8,128)(2,1)S(1)}, bf16[2,25,16,128]{3,2,1,0:T(8,128)(2,1)S(1)}, u32[]{:S(2)}, u32[]{:S(2)}) %collective-permute-start.22) | collective-permute-done | bytes 204832 | tf_op jit(solution)/shard_map/cond/branch_1_fun/ppermute | solution.py:560
  118.9 2.4 %collective-permute-start.23 = (bf16[8,25,16,128]{3,2,1,0:T(8,128)(2,1)S(1)}, bf16[8,25,16,128]{3,2,1,0:T(8,128)(2,1)S(1)}, u32[]{:S(2)}, u32[]{:S(2)}) collective-permute-start(bf16[8,25,16,128]{3,2,1,0:T(8,128)(2,1)S(1)} %constant_dynamic-update-slice_fusion.6.refs_0_), channel_id=1, source_target_pairs={{0,1},{1,0},{2,3},{3,2},{4,5},{5,4},{6,7},{7,6},{8,9},{9,8},{10,11... | collective-permute-start | bytes 2457608 | tf_op jit(solution)/shard_map/cond/branch_1_fun/ppermute | solution.py:560
  121.3 2.0 %collective-permute-done.23.refs_1_ = bf16[8,25,16,128]{3,2,1,0:T(8,128)(2,1)S(1)} collective-permute-done((bf16[8,25,16,128]{3,2,1,0:T(8,128)(2,1)S(1)}, bf16[8,25,16,128]{3,2,1,0:T(8,128)(2,1)S(1)}, u32[]{:S(2)}, u32[]{:S(2)}) %collective-permute-start.23) | collective-permute-done | bytes 819232 | tf_op jit(solution)/shard_map/cond/branch_1_fun/ppermute | solution.py:560
  123.3 9.1 %slice_grads.6 = (bf16[16,256,256]{2,1,0:T(8,128)(2,1)S(1)}, f32[1,128]{1,0:T(1,128)}) custom-call(s32[16,256]{1,0:T(8,128)S(1)} %get-tuple-element.20.own_ref, s32[5,16]{1,0:T(8,128)S(1)} %get-tuple-element.21.place_ref, bf16[2048,256]{1,0:T(8,128)(2,1)S(1)} %get-tuple-element.22.q_ref, bf16[2560,256]{1,0:T(8,128)(2,1)S(1)} %get-tuple-element.23.d_ref, ...), custom_call_target="tpu_custom_call" | custom-call | tf_op jit(solution)/shard_map/cond/branch_1_fun/slice_grads/pallas_call | solution.py:505
  132.6 52.1 %all_to_all.26.grad_ref = bf16[16,256,256]{2,1,0:T(8,128)(2,1)S(1)} all-to-all(bf16[16,256,256]{2,1,0:T(8,128)(2,1)S(1)} %get-tuple-element.88), channel_id=1, replica_groups=mesh['groups'=2,'pb'=16] {'pb'}, dimensions={0} | all-to-all | bytes 4194304 | tf_op jit(solution)/shard_map/all_to_all | solution.py:625
  184.6 3.3 %project_out.1 = f32[256,4096]{1,0:T(8,128)} custom-call(bf16[16,256,256]{2,1,0:T(8,128)(2,1)S(1)} %all_to_all.26.grad_ref, bf16[256,4096]{1,0:T(8,128)(2,1)S(1)} %copy-done, f32[256,128]{1,0:T(8,128)S(1)} %copy-done.1), custom_call_target="tpu_custom_call" | custom-call | tf_op jit(solution)/shard_map/project_out/pallas_call | solution.py:543
  (14 shorter events, 0.1 us)
Async XLA Ops:
  73.8 3.6 %collective-permute-start.12 = (f32[8,392,128]{2,1,0:T(8,128)S(1)}, f32[8,392,128]{2,1,0:T(8,128)S(1)}, u32[]{:S(2)}, u32[]{:S(2)}) collective-permute-start(f32[8,392,128]{2,1,0:T(8,128)S(1)} %get-tuple-element.25), channel_id=1, source_target_pairs={{0,1},{1,0},{2,3},{3,2},{4,5},{5,4},{6,7},{7,6},{8,9},{9,8},{10,11... | collective-permute-start | bytes 4816904 | tf_op jit(solution)/shard_map/cond/branch_1_fun/ppermute | solution.py:560
  74.2 3.1 %collective-permute-start.13 = (f32[8,128]{1,0:T(8,128)S(1)}, f32[8,128]{1,0:T(8,128)S(1)}, u32[]{:S(2)}, u32[]{:S(2)}) collective-permute-start(f32[8,128]{1,0:T(8,128)S(1)} %get-tuple-element.26.top_ref), channel_id=1, source_target_pairs={{0,1},{1,0},{2,3},{3,2},{4,5},{5,4},{6,7},{7,6},{8,9},{9,8},{10,11... | collective-permute-start | bytes 12296 | tf_op jit(solution)/shard_map/cond/branch_1_fun/ppermute | solution.py:560
  78.5 7.3 %collective-permute-start.14 = (s16[2,25,16,128]{3,2,1,0:T(8,128)(2,1)S(1)}, s16[2,25,16,128]{3,2,1,0:T(8,128)(2,1)S(1)}, u32[]{:S(2)}, u32[]{:S(2)}) collective-permute-start(s16[2,25,16,128]{3,2,1,0:T(8,128)(2,1)S(1)} %get-tuple-element.28), channel_id=1, source_target_pairs={{0,6},{1,7},{2,4},{3,5},{4,2},{5,3},{6,0},{7,1},{8,14},{9,15},{10,... | collective-permute-start | bytes 614408 | tf_op jit(solution)/shard_map/cond/branch_1_fun/ppermute | solution.py:560
  79.0 10.4 %collective-permute-start.15 = (s16[2,25,16,128]{3,2,1,0:T(8,128)(2,1)S(1)}, s16[2,25,16,128]{3,2,1,0:T(8,128)(2,1)S(1)}, u32[]{:S(2)}, u32[]{:S(2)}) collective-permute-start(s16[2,25,16,128]{3,2,1,0:T(8,128)(2,1)S(1)} %get-tuple-element.29), channel_id=1, source_target_pairs={{0,4},{1,5},{2,6},{3,7},{4,0},{5,1},{6,2},{7,3},{8,12},{9,13},{10,... | collective-permute-start | bytes 614408 | tf_op jit(solution)/shard_map/cond/branch_1_fun/ppermute | solution.py:560
  80.1 10.8 %collective-permute-start.16 = (s16[2,25,16,128]{3,2,1,0:T(8,128)(2,1)S(1)}, s16[2,25,16,128]{3,2,1,0:T(8,128)(2,1)S(1)}, u32[]{:S(2)}, u32[]{:S(2)}) collective-permute-start(s16[2,25,16,128]{3,2,1,0:T(8,128)(2,1)S(1)} %get-tuple-element.30), channel_id=1, source_target_pairs={{0,2},{1,3},{2,0},{3,1},{4,6},{5,7},{6,4},{7,5},{8,10},{9,11},{10,... | collective-permute-start | bytes 614408 | tf_op jit(solution)/shard_map/cond/branch_1_fun/ppermute | solution.py:560
  91.5 7.9 %collective-permute-start.17 = (s16[25,16,128]{2,1,0:T(8,128)(2,1)S(1)}, s16[25,16,128]{2,1,0:T(8,128)(2,1)S(1)}, u32[]{:S(2)}, u32[]{:S(2)}) collective-permute-start(s16[25,16,128]{2,1,0:T(8,128)(2,1)S(1)} %get-tuple-element.32), channel_id=1, source_target_pairs={{0,8},{1,9},{2,10},{3,11},{4,12},{5,13},{6,14},{7,15},{8,0},{9,1},... | collective-permute-start | bytes 307208 | tf_op jit(solution)/shard_map/cond/branch_1_fun/ppermute | solution.py:560
  101.1 6.5 %collective-permute-start.18 = (bf16[1,25,16,128]{3,2,1,0:T(8,128)(2,1)S(1)}, bf16[1,25,16,128]{3,2,1,0:T(8,128)(2,1)S(1)}, u32[]{:S(2)}, u32[]{:S(2)}) collective-permute-start(bf16[1,25,16,128]{3,2,1,0:T(8,128)(2,1)S(1)} %bitcast.30), channel_id=1, source_target_pairs={{0,8},{1,9},{2,10},{3,11},{4,12},{5,13},{6,14},{7,15},{8,0},{9,1},... | collective-permute-start | bytes 307208 | tf_op jit(solution)/shard_map/cond/branch_1_fun/ppermute | solution.py:560
  107.6 6.1 %collective-permute-start.19 = (bf16[2,25,16,128]{3,2,1,0:T(8,128)(2,1)S(1)}, bf16[2,25,16,128]{3,2,1,0:T(8,128)(2,1)S(1)}, u32[]{:S(2)}, u32[]{:S(2)}) collective-permute-start(bf16[2,25,16,128]{3,2,1,0:T(8,128)(2,1)S(1)} %pad_maximum_fusion.1), channel_id=1, source_target_pairs={{0,4},{1,5},{2,6},{3,7},{4,0},{5,1},{6,2},{7,3},{8,12},{9,13},{10,... | collective-permute-start | bytes 614408 | tf_op jit(solution)/shard_map/cond/branch_1_fun/ppermute | solution.py:560
  107.7 7.0 %collective-permute-start.20 = (bf16[1,25,16,128]{3,2,1,0:T(8,128)(2,1)S(1)}, bf16[1,25,16,128]{3,2,1,0:T(8,128)(2,1)S(1)}, u32[]{:S(2)}, u32[]{:S(2)}) collective-permute-start(bf16[1,25,16,128]{3,2,1,0:T(8,128)(2,1)S(1)} %bitcast.32), channel_id=1, source_target_pairs={{0,2},{1,3},{2,0},{3,1},{4,6},{5,7},{6,4},{7,5},{8,10},{9,11},{10,... | collective-permute-start | bytes 307208 | tf_op jit(solution)/shard_map/cond/branch_1_fun/ppermute | solution.py:560
  108.6 6.1 %collective-permute-start.21 = (bf16[1,25,16,128]{3,2,1,0:T(8,128)(2,1)S(1)}, bf16[1,25,16,128]{3,2,1,0:T(8,128)(2,1)S(1)}, u32[]{:S(2)}, u32[]{:S(2)}) collective-permute-start(bf16[1,25,16,128]{3,2,1,0:T(8,128)(2,1)S(1)} %collective-permute-done.18), channel_id=1, source_target_pairs={{0,2},{1,3},{2,0},{3,1},{4,6},{5,7},{6,4},{7,5},{8,10},{9,11},{10,... | collective-permute-start | bytes 307208 | tf_op jit(solution)/shard_map/cond/branch_1_fun/ppermute | solution.py:560
  113.7 5.1 %collective-permute-start.22 = (bf16[2,25,16,128]{3,2,1,0:T(8,128)(2,1)S(1)}, bf16[2,25,16,128]{3,2,1,0:T(8,128)(2,1)S(1)}, u32[]{:S(2)}, u32[]{:S(2)}) collective-permute-start(bf16[2,25,16,128]{3,2,1,0:T(8,128)(2,1)S(1)} %collective-permute-done.19), channel_id=1, source_target_pairs={{0,2},{1,3},{2,0},{3,1},{4,6},{5,7},{6,4},{7,5},{8,10},{9,11},{10,... | collective-permute-start | bytes 614408 | tf_op jit(solution)/shard_map/cond/branch_1_fun/ppermute | solution.py:560
  118.9 4.4 %collective-permute-start.23 = (bf16[8,25,16,128]{3,2,1,0:T(8,128)(2,1)S(1)}, bf16[8,25,16,128]{3,2,1,0:T(8,128)(2,1)S(1)}, u32[]{:S(2)}, u32[]{:S(2)}) collective-permute-start(bf16[8,25,16,128]{3,2,1,0:T(8,128)(2,1)S(1)} %constant_dynamic-update-slice_fusion.6.refs_0_), channel_id=1, source_target_pairs={{0,1},{1,0},{2,3},{3,2},{4,5},{5,4},{6,7},{7,6},{8,9},{9,8},{10,11... | collective-permute-start | bytes 2457608 | tf_op jit(solution)/shard_map/cond/branch_1_fun/ppermute | solution.py:560
  132.6 52.1 %copy-start = (bf16[256,4096]{1,0:T(8,128)(2,1)S(1)}, bf16[256,4096]{1,0:T(8,128)(2,1)}, u32[]{:S(2)}) copy-start(bf16[256,4096]{1,0:T(8,128)(2,1)} %get-tuple-element.89.normed_ref) | copy-start | bytes 6291460
  132.6 52.1 %copy-start.1 = (f32[256,128]{1,0:T(8,128)S(1)}, f32[256,128]{1,0:T(8,128)}, u32[]{:S(2)}) copy-start(f32[256,128]{1,0:T(8,128)} %get-tuple-element.90.inv_ref) | copy-start | bytes 393220

commit v4 on v3

--- a/solution.py
+++ b/solution.py
@@ -560,32 +560,24 @@
     return lax.ppermute(value, "pb", pairs)
 
 
-def swap_bits(devices):
-    bits = [1 << bit for bit in reversed(range(devices.bit_length() - 1))]
-    return bits[:-2], bits[-2], bits[-1]
+def near_hops(devices):
+    return [2 * hop for hop in reversed(range(1, devices // 4))]
 
 
 def swap_masks(devices):
-    far, side, last = swap_bits(devices)
-    held = [0]
-    for apart in far:
-        held = held + [mask ^ apart for mask in held]
-    held = held + [mask ^ side for mask in held]
-    return [held, [mask ^ last for mask in held]]
+    near = [0] + near_hops(devices)
+    held = near + [mask ^ (devices // 2) for mask in near]
+    return [held, [mask ^ 1 for mask in held]]
 
 
 def gather_all(value):
-    far, side, last = swap_bits(lax.axis_size("pb"))
-    held = value[None]
-    beside, latest = [], held
-    for apart in far:
-        arrived = swapped(held, apart)
-        beside.append(swapped(latest, side))
-        held = jnp.concatenate([held, arrived], axis=0)
-        latest = arrived
-    beside.append(swapped(latest, side))
-    held = jnp.concatenate([held] + beside, axis=0)
-    return [held, swapped(held, last)]
+    devices = lax.axis_size("pb")
+    own = value[None]
+    across = swapped(own, devices // 2)
+    held = [own] + [swapped(own, hop) for hop in near_hops(devices)]
+    held += [across] + [swapped(across, hop) for hop in near_hops(devices)]
+    held = jnp.concatenate(held, axis=0)
+    return [held, swapped(held, 1)]
 
 
 def middle(embedded, room, devices, pairs, window):

time: 188 us -> 183 us (0.973); the launches traced: 188 us -> 180 us
  waiting for transfers between devices: 36.8 us -> 26.7 us
  starting transfers between devices: 8.96 us -> 12 us
    ppermute x12 -> x14, waiting for transfers between devices: 36.8 us -> 26.7 us  [swapped(): return lax.ppermute(value, 'pb', pairs)]
    ppermute x12 -> x14, starting transfers between devices: 8.96 us -> 12 us  [swapped(): return lax.ppermute(value, 'pb', pairs)]
  transfers between devices with their start and end apart: 12 -> 14, of which waited for: 9 -> 12; matrix products, arithmetic and copies ran while one was open for 0% -> 0% of each run, Pallas kernels for 0% -> 0%
where the time goes in v4:
time: 183 us; the launch traced here: 180 us
  blocking collectives  110 us (60%)
  Pallas kernels  29.5 us (16%)
  waiting for transfers between devices  26.7 us (15%)
  starting transfers between devices  12 us (7%)
    all_to_all x1, blocking collectives, feature_plan(): lax.all_to_all(embedding, 'pb', split_axis=0, concat_axis=0, tiled=True)  58 us
    all_to_all x1, blocking collectives, feature_plan(): lax.all_to_all(grads, 'pb', split_axis=0, concat_axis=0, tiled=True)  51.8 us
    ppermute x14, waiting for transfers between devices, swapped(): return lax.ppermute(value, 'pb', pairs)  26.7 us
    ppermute x14, starting transfers between devices, swapped(): return lax.ppermute(value, 'pb', pairs)  12 us
    pallas_call x1, Pallas kernels, grad_call(): pl.pallas_call(functools.partial(grad_kernel, blocks, pairs, window), in_...  9.06 us
    pallas_call x1, Pallas kernels, score_call(): pl.pallas_call(functools.partial(score_kernel, blocks, pairs, window), in...  8.15 us
    pallas_call x1, Pallas kernels, norm_call(): pl.pallas_call(norm_kernel, in_specs=[whole, whole, whole, whole, pl.Bloc...  5.63 us
  transfers between devices with their start and end apart: 14, of which 12 were waited for; matrix products, arithmetic and copies ran while one was open for 0% of the time, Pallas kernels for 0%

profile of v4, /device:TPU:1, one launch (start us, length us, event | category | flops | bytes accessed | tf_op | source)
XLA Modules:
  0.0 180.3 jit_solution(6261479685963386103)
XLA Ops:
  0.6 5.6 %norm_rows.1 = (bf16[256,4096]{1,0:T(8,128)(2,1)}, f32[256,128]{1,0:T(8,128)}, bf16[16,264,256]{2,1,0:T(8,128)(2,1)}) custom-call(s32[1,256]{1,0:T(1,128)} %last_ref.1, bf16[256,4096]{1,0:T(8,128)(2,1)} %hidden_ref.1, bf16[4096]{0:T(1024)(128)(2,1)} %gain_ref.1, s32[2,128]{1,0:T(2,128)} %bitcast.41, s32[1,4]{1,0:T(1,128)} %negative_ref.1), custom_call_target="tpu_custom_call" | custom-call | tf_op jit(solution)/shard_map/norm_rows/pallas_call | solution.py:90
  6.3 58.0 %all_to_all.25 = bf16[16,264,256]{2,1,0:T(8,128)(2,1)S(1)} all-to-all(bf16[16,264,256]{2,1,0:T(8,128)(2,1)} %get-tuple-element.87), channel_id=1, replica_groups=mesh['groups'=2,'pb'=16] {'pb'}, dimensions={0} | all-to-all | bytes 4325376 | tf_op jit(solution)/shard_map/all_to_all | solution.py:604
  64.3 0.6 fusion
  65.6 59.7 %conditional.1 = (bf16[16,256,256]{2,1,0:T(8,128)(2,1)S(1)}, f32[1]{0:T(128)}) conditional(s32[]{:T(128)} %clamp.3, bf16[16,264,256]{2,1,0:T(8,128)(2,1)S(1)} %all_to_all.25, bf16[16,264,256]{2,1,0:T(8,128)(2,1)S(1)} %all_to_all.25, bf16[16,264,256]{2,1,0:T(8,128)(2,1)S(1)} %all_to_all.25, ...), branch_computations={%region_1.0_spmd, %region_2.0_spmd, %region_3.0_spmd, %region_4.0_... | conditional | bytes 28099136 | solution.py:609
  65.6 8.2 %partial_scores.5 = (bf16[2048,256]{1,0:T(8,128)(2,1)S(1)}, bf16[2560,256]{1,0:T(8,128)(2,1)S(1)}, f32[8,360,128]{2,1,0:T(8,128)S(1)}, f32[8,360,128]{2,1,0:T(8,...) custom-call(bf16[16,264,256]{2,1,0:T(8,128)(2,1)S(1)} %refs_0_), custom_call_target="tpu_custom_call" | custom-call | tf_op jit(solution)/shard_map/cond/branch_0_fun/partial_scores/pallas_call | solution.py:210
  73.8 0.5 collective-permute-start
  74.3 2.8 %collective-permute-done.1.other_top_ref = f32[8,128]{1,0:T(8,128)S(1)} collective-permute-done((f32[8,128]{1,0:T(8,128)S(1)}, f32[8,128]{1,0:T(8,128)S(1)}, u32[]{:S(2)}, u32[]{:S(2)}) %collective-permute-start.1) | collective-permute-done | bytes 4128 | tf_op jit(solution)/shard_map/cond/branch_0_fun/ppermute | solution.py:560
  77.1 1.1 merge_scores.5
  78.3 0.5 collective-permute-start.2
  78.7 1.1 collective-permute-start.3
  79.8 1.1 collective-permute-start.4
  81.0 4.2 %collective-permute-done.2.refs_0_ = s16[2,23,16,128]{3,2,1,0:T(8,128)(2,1)S(1)} collective-permute-done((s16[2,23,16,128]{3,2,1,0:T(8,128)(2,1)S(1)}, s16[2,23,16,128]{3,2,1,0:T(8,128)(2,1)S(1)}, u32[]{:S(2)}, u32[]{:S(2)}) %collective-permute-start.2) | collective-permute-done | bytes 188448 | tf_op jit(solution)/shard_map/cond/branch_0_fun/ppermute | solution.py:560
  85.2 3.2 %collective-permute-done.3.refs_1_ = s16[2,23,16,128]{3,2,1,0:T(8,128)(2,1)S(1)} collective-permute-done((s16[2,23,16,128]{3,2,1,0:T(8,128)(2,1)S(1)}, s16[2,23,16,128]{3,2,1,0:T(8,128)(2,1)S(1)}, u32[]{:S(2)}, u32[]{:S(2)}) %collective-permute-start.3) | collective-permute-done | bytes 188448 | tf_op jit(solution)/shard_map/cond/branch_0_fun/ppermute | solution.py:560
  88.4 1.5 collective-permute-done.4.refs_2_
  89.9 0.5 half_scores.5
  90.4 0.6 collective-permute-start.5
  91.1 6.9 %collective-permute-done.5.refs_0_ = s16[23,16,128]{2,1,0:T(8,128)(2,1)S(1)} collective-permute-done((s16[23,16,128]{2,1,0:T(8,128)(2,1)S(1)}, s16[23,16,128]{2,1,0:T(8,128)(2,1)S(1)}, u32[]{:S(2)}, u32[]{:S(2)}) %collective-permute-start.5) | collective-permute-done | bytes 94240 | tf_op jit(solution)/shard_map/cond/branch_0_fun/ppermute | solution.py:560
  97.9 1.7 softmax_rows.5
  99.8 1.8 collective-permute-start.9
  101.6 0.9 collective-permute-start.8
  102.5 1.8 collective-permute-done.9
  104.2 2.3 %collective-permute-start.10 = (bf16[1,23,16,128]{3,2,1,0:T(8,128)(2,1)S(1)}, bf16[1,23,16,128]{3,2,1,0:T(8,128)(2,1)S(1)}, u32[]{:S(2)}, u32[]{:S(2)}) collective-permute-start(bf16[1,23,16,128]{3,2,1,0:T(8,128)(2,1)S(1)} %collective-permute-done.9), channel_id=1, source_target_pairs={{0,6},{1,7},{2,4},{3,5},{4,2},{5,3},{6,0},{7,1},{8,14},{9,15},{10,... | collective-permute-start | bytes 282632 | tf_op jit(solution)/shard_map/cond/branch_0_fun/ppermute | solution.py:560
  106.5 0.6 collective-permute-done.6
  107.2 0.4 collective-permute-done.7
  107.6 2.5 %collective-permute-done.10 = bf16[1,23,16,128]{3,2,1,0:T(8,128)(2,1)S(1)} collective-permute-done((bf16[1,23,16,128]{3,2,1,0:T(8,128)(2,1)S(1)}, bf16[1,23,16,128]{3,2,1,0:T(8,128)(2,1)S(1)}, u32[]{:S(2)}, u32[]{:S(2)}) %collective-permute-start.10) | collective-permute-done | bytes 94240 | tf_op jit(solution)/shard_map/cond/branch_0_fun/ppermute | solution.py:560
  110.2 0.5 collective-permute-done.11
  110.7 0.4 collective-permute-done.12
  111.1 3.0 %collective-permute-start.13 = (bf16[8,23,16,128]{3,2,1,0:T(8,128)(2,1)S(1)}, bf16[8,23,16,128]{3,2,1,0:T(8,128)(2,1)S(1)}, u32[]{:S(2)}, u32[]{:S(2)}) collective-permute-start(bf16[8,23,16,128]{3,2,1,0:T(8,128)(2,1)S(1)} %constant_dynamic-update-slice_fusion.refs_0_), channel_id=1, source_target_pairs={{0,1},{1,0},{2,3},{3,2},{4,5},{5,4},{6,7},{7,6},{8,9},{9,8},{10,11... | collective-permute-start | bytes 2261000 | tf_op jit(solution)/shard_map/cond/branch_0_fun/ppermute | solution.py:560
  114.1 1.9 %collective-permute-done.13.refs_1_ = bf16[8,23,16,128]{3,2,1,0:T(8,128)(2,1)S(1)} collective-permute-done((bf16[8,23,16,128]{3,2,1,0:T(8,128)(2,1)S(1)}, bf16[8,23,16,128]{3,2,1,0:T(8,128)(2,1)S(1)}, u32[]{:S(2)}, u32[]{:S(2)}) %collective-permute-start.13) | collective-permute-done | bytes 753696 | tf_op jit(solution)/shard_map/cond/branch_0_fun/ppermute | solution.py:560
  116.0 9.1 %slice_grads.5 = (bf16[16,256,256]{2,1,0:T(8,128)(2,1)S(1)}, f32[1,128]{1,0:T(1,128)}) custom-call(s32[16,256]{1,0:T(8,128)S(1)} %get-tuple-element.5.own_ref, s32[5,16]{1,0:T(8,128)S(1)} %get-tuple-element.6.place_ref, bf16[2048,256]{1,0:T(8,128)(2,1)S(1)} %get-tuple-element.7.q_ref, bf16[2560,256]{1,0:T(8,128)(2,1)S(1)} %get-tuple-element.8.d_ref, ...), custom_call_target="tpu_custom_call" | custom-call | tf_op jit(solution)/shard_map/cond/branch_0_fun/slice_grads/pallas_call | solution.py:505
  125.3 51.8 %all_to_all.26.grad_ref = bf16[16,256,256]{2,1,0:T(8,128)(2,1)S(1)} all-to-all(bf16[16,256,256]{2,1,0:T(8,128)(2,1)S(1)} %get-tuple-element.88), channel_id=1, replica_groups=mesh['groups'=2,'pb'=16] {'pb'}, dimensions={0} | all-to-all | bytes 4194304 | tf_op jit(solution)/shard_map/all_to_all | solution.py:617
  177.1 3.3 %project_out.1 = f32[256,4096]{1,0:T(8,128)} custom-call(bf16[16,256,256]{2,1,0:T(8,128)(2,1)S(1)} %all_to_all.26.grad_ref, bf16[256,4096]{1,0:T(8,128)(2,1)S(1)} %copy-done, f32[256,128]{1,0:T(8,128)S(1)} %copy-done.1), custom_call_target="tpu_custom_call" | custom-call | tf_op jit(solution)/shard_map/project_out/pallas_call | solution.py:543
  (19 shorter events, 0.4 us)
Async XLA Ops:
  73.8 3.4 %collective-permute-start = (f32[8,360,128]{2,1,0:T(8,128)S(1)}, f32[8,360,128]{2,1,0:T(8,128)S(1)}, u32[]{:S(2)}, u32[]{:S(2)}) collective-permute-start(f32[8,360,128]{2,1,0:T(8,128)S(1)} %get-tuple-element.10), channel_id=1, source_target_pairs={{0,1},{1,0},{2,3},{3,2},{4,5},{5,4},{6,7},{7,6},{8,9},{9,8},{10,11... | collective-permute-start | bytes 4423688 | tf_op jit(solution)/shard_map/cond/branch_0_fun/ppermute | solution.py:560
  74.2 2.9 %collective-permute-start.1 = (f32[8,128]{1,0:T(8,128)S(1)}, f32[8,128]{1,0:T(8,128)S(1)}, u32[]{:S(2)}, u32[]{:S(2)}) collective-permute-start(f32[8,128]{1,0:T(8,128)S(1)} %get-tuple-element.11.top_ref), channel_id=1, source_target_pairs={{0,1},{1,0},{2,3},{3,2},{4,5},{5,4},{6,7},{7,6},{8,9},{9,8},{10,11... | collective-permute-start | bytes 12296 | tf_op jit(solution)/shard_map/cond/branch_0_fun/ppermute | solution.py:560
  78.3 6.9 %collective-permute-start.2 = (s16[2,23,16,128]{3,2,1,0:T(8,128)(2,1)S(1)}, s16[2,23,16,128]{3,2,1,0:T(8,128)(2,1)S(1)}, u32[]{:S(2)}, u32[]{:S(2)}) collective-permute-start(s16[2,23,16,128]{3,2,1,0:T(8,128)(2,1)S(1)} %get-tuple-element.13), channel_id=1, source_target_pairs={{0,6},{1,7},{2,4},{3,5},{4,2},{5,3},{6,0},{7,1},{8,14},{9,15},{10,... | collective-permute-start | bytes 565256 | tf_op jit(solution)/shard_map/cond/branch_0_fun/ppermute | solution.py:560
  78.7 9.6 %collective-permute-start.3 = (s16[2,23,16,128]{3,2,1,0:T(8,128)(2,1)S(1)}, s16[2,23,16,128]{3,2,1,0:T(8,128)(2,1)S(1)}, u32[]{:S(2)}, u32[]{:S(2)}) collective-permute-start(s16[2,23,16,128]{3,2,1,0:T(8,128)(2,1)S(1)} %get-tuple-element.14), channel_id=1, source_target_pairs={{0,4},{1,5},{2,6},{3,7},{4,0},{5,1},{6,2},{7,3},{8,12},{9,13},{10,... | collective-permute-start | bytes 565256 | tf_op jit(solution)/shard_map/cond/branch_0_fun/ppermute | solution.py:560
  79.8 10.1 %collective-permute-start.4 = (s16[2,23,16,128]{3,2,1,0:T(8,128)(2,1)S(1)}, s16[2,23,16,128]{3,2,1,0:T(8,128)(2,1)S(1)}, u32[]{:S(2)}, u32[]{:S(2)}) collective-permute-start(s16[2,23,16,128]{3,2,1,0:T(8,128)(2,1)S(1)} %get-tuple-element.15), channel_id=1, source_target_pairs={{0,2},{1,3},{2,0},{3,1},{4,6},{5,7},{6,4},{7,5},{8,10},{9,11},{10,... | collective-permute-start | bytes 565256 | tf_op jit(solution)/shard_map/cond/branch_0_fun/ppermute | solution.py:560
  90.4 7.5 %collective-permute-start.5 = (s16[23,16,128]{2,1,0:T(8,128)(2,1)S(1)}, s16[23,16,128]{2,1,0:T(8,128)(2,1)S(1)}, u32[]{:S(2)}, u32[]{:S(2)}) collective-permute-start(s16[23,16,128]{2,1,0:T(8,128)(2,1)S(1)} %get-tuple-element.17), channel_id=1, source_target_pairs={{0,8},{1,9},{2,10},{3,11},{4,12},{5,13},{6,14},{7,15},{8,0},{9,1},... | collective-permute-start | bytes 282632 | tf_op jit(solution)/shard_map/cond/branch_0_fun/ppermute | solution.py:560
  99.7 7.5 %collective-permute-start.6 = (bf16[1,23,16,128]{3,2,1,0:T(8,128)(2,1)S(1)}, bf16[1,23,16,128]{3,2,1,0:T(8,128)(2,1)S(1)}, u32[]{:S(2)}, u32[]{:S(2)}) collective-permute-start(bf16[1,23,16,128]{3,2,1,0:T(8,128)(2,1)S(1)} %bitcast.37), channel_id=1, source_target_pairs={{0,6},{1,7},{2,4},{3,5},{4,2},{5,3},{6,0},{7,1},{8,14},{9,15},{10,... | collective-permute-start | bytes 282632 | tf_op jit(solution)/shard_map/cond/branch_0_fun/ppermute | solution.py:560
  99.8 4.5 %collective-permute-start.9 = (bf16[1,23,16,128]{3,2,1,0:T(8,128)(2,1)S(1)}, bf16[1,23,16,128]{3,2,1,0:T(8,128)(2,1)S(1)}, u32[]{:S(2)}, u32[]{:S(2)}) collective-permute-start(bf16[1,23,16,128]{3,2,1,0:T(8,128)(2,1)S(1)} %bitcast.38), channel_id=1, source_target_pairs={{0,8},{1,9},{2,10},{3,11},{4,12},{5,13},{6,14},{7,15},{8,0},{9,1},... | collective-permute-start | bytes 282632 | tf_op jit(solution)/shard_map/cond/branch_0_fun/ppermute | solution.py:560
  101.5 6.0 %collective-permute-start.7 = (bf16[1,23,16,128]{3,2,1,0:T(8,128)(2,1)S(1)}, bf16[1,23,16,128]{3,2,1,0:T(8,128)(2,1)S(1)}, u32[]{:S(2)}, u32[]{:S(2)}) collective-permute-start(bf16[1,23,16,128]{3,2,1,0:T(8,128)(2,1)S(1)} %bitcast.39), channel_id=1, source_target_pairs={{0,4},{1,5},{2,6},{3,7},{4,0},{5,1},{6,2},{7,3},{8,12},{9,13},{10,... | collective-permute-start | bytes 282632 | tf_op jit(solution)/shard_map/cond/branch_0_fun/ppermute | solution.py:560
  101.6 6.0 %collective-permute-start.8 = (bf16[1,23,16,128]{3,2,1,0:T(8,128)(2,1)S(1)}, bf16[1,23,16,128]{3,2,1,0:T(8,128)(2,1)S(1)}, u32[]{:S(2)}, u32[]{:S(2)}) collective-permute-start(bf16[1,23,16,128]{3,2,1,0:T(8,128)(2,1)S(1)} %bitcast.40), channel_id=1, source_target_pairs={{0,2},{1,3},{2,0},{3,1},{4,6},{5,7},{6,4},{7,5},{8,10},{9,11},{10,... | collective-permute-start | bytes 282632 | tf_op jit(solution)/shard_map/cond/branch_0_fun/ppermute | solution.py:560
  104.2 5.9 %collective-permute-start.10 = (bf16[1,23,16,128]{3,2,1,0:T(8,128)(2,1)S(1)}, bf16[1,23,16,128]{3,2,1,0:T(8,128)(2,1)S(1)}, u32[]{:S(2)}, u32[]{:S(2)}) collective-permute-start(bf16[1,23,16,128]{3,2,1,0:T(8,128)(2,1)S(1)} %collective-permute-done.9), channel_id=1, source_target_pairs={{0,6},{1,7},{2,4},{3,5},{4,2},{5,3},{6,0},{7,1},{8,14},{9,15},{10,... | collective-permute-start | bytes 282632 | tf_op jit(solution)/shard_map/cond/branch_0_fun/ppermute | solution.py:560
  106.5 4.1 %collective-permute-start.11 = (bf16[1,23,16,128]{3,2,1,0:T(8,128)(2,1)S(1)}, bf16[1,23,16,128]{3,2,1,0:T(8,128)(2,1)S(1)}, u32[]{:S(2)}, u32[]{:S(2)}) collective-permute-start(bf16[1,23,16,128]{3,2,1,0:T(8,128)(2,1)S(1)} %collective-permute-done.9), channel_id=1, source_target_pairs={{0,4},{1,5},{2,6},{3,7},{4,0},{5,1},{6,2},{7,3},{8,12},{9,13},{10,... | collective-permute-start | bytes 282632 | tf_op jit(solution)/shard_map/cond/branch_0_fun/ppermute | solution.py:560
  107.2 4.0 %collective-permute-start.12 = (bf16[1,23,16,128]{3,2,1,0:T(8,128)(2,1)S(1)}, bf16[1,23,16,128]{3,2,1,0:T(8,128)(2,1)S(1)}, u32[]{:S(2)}, u32[]{:S(2)}) collective-permute-start(bf16[1,23,16,128]{3,2,1,0:T(8,128)(2,1)S(1)} %collective-permute-done.9), channel_id=1, source_target_pairs={{0,2},{1,3},{2,0},{3,1},{4,6},{5,7},{6,4},{7,5},{8,10},{9,11},{10,... | collective-permute-start | bytes 282632 | tf_op jit(solution)/shard_map/cond/branch_0_fun/ppermute | solution.py:560
  111.1 4.9 %collective-permute-start.13 = (bf16[8,23,16,128]{3,2,1,0:T(8,128)(2,1)S(1)}, bf16[8,23,16,128]{3,2,1,0:T(8,128)(2,1)S(1)}, u32[]{:S(2)}, u32[]{:S(2)}) collective-permute-start(bf16[8,23,16,128]{3,2,1,0:T(8,128)(2,1)S(1)} %constant_dynamic-update-slice_fusion.refs_0_), channel_id=1, source_target_pairs={{0,1},{1,0},{2,3},{3,2},{4,5},{5,4},{6,7},{7,6},{8,9},{9,8},{10,11... | collective-permute-start | bytes 2261000 | tf_op jit(solution)/shard_map/cond/branch_0_fun/ppermute | solution.py:560
  125.3 51.8 %copy-start = (bf16[256,4096]{1,0:T(8,128)(2,1)S(1)}, bf16[256,4096]{1,0:T(8,128)(2,1)}, u32[]{:S(2)}) copy-start(bf16[256,4096]{1,0:T(8,128)(2,1)} %get-tuple-element.89.normed_ref) | copy-start | bytes 6291460
  125.3 51.8 %copy-start.1 = (f32[256,128]{1,0:T(8,128)S(1)}, f32[256,128]{1,0:T(8,128)}, u32[]{:S(2)}) copy-start(f32[256,128]{1,0:T(8,128)} %get-tuple-element.90.inv_ref) | copy-start | bytes 393220

commit v5 on v4

--- a/solution.py
+++ b/solution.py
@@ -246,9 +246,9 @@
     return jnp.max(jnp.max(values, axis=1, keepdims=True), axis=0, keepdims=True)
 
 
-def merge_kernel(mine_ref, other_ref, top_ref, other_top_ref, own_ref, *code_refs):
-    _, rows, pairs = own_ref.shape
-    steps = code_refs[0].shape[1] - 1
+def merge_kernel(mine_ref, other_ref, top_ref, other_top_ref, own_ref, over_ref, *code_refs):
+    rows, pairs = own_ref.shape
+    steps = code_refs[0].shape[0] - 1
     fine = rows // steps // 2
     chip = lax.axis_index("pb") // 2
     across = mine_ref.shape[0] // 2
@@ -256,20 +256,23 @@
     bound = jnp.ceil(top * bound_steps) + 1.0
     scale = code_steps * bound_steps / bound
     sent_bound = jnp.broadcast_to(bound, (2 * fine, pairs)).astype(jnp.int32).astype(jnp.int16)
-    for which in range(2):
-        target = chip ^ (which * across)
-        own_ref[which] = mine_ref[target, :rows] + other_ref[target, :rows]
-        for hop, code_ref in enumerate(code_refs):
-            near = target ^ (hop + 1)
+    near = len(code_refs) // 2
+    for target, sum_ref, refs in (
+        (chip ^ across, over_ref, code_refs[:near]),
+        (chip, own_ref, code_refs[near:]),
+    ):
+        sum_ref[...] = mine_ref[target, :rows] + other_ref[target, :rows]
+        for hop, code_ref in enumerate(refs):
+            whose = target ^ (hop + 1)
 
             def encode(step, carry):
                 there = pl.ds(pl.multiple_of(step * 2 * fine, 2 * fine), 2 * fine)
-                values = mine_ref[near, there, :] + other_ref[near, there, :]
-                code_ref[which, step] = coded(values, scale)
+                values = mine_ref[whose, there, :] + other_ref[whose, there, :]
+                code_ref[step] = coded(values, scale)
                 return carry
 
             lax.fori_loop(0, steps, encode, 0)
-            code_ref[which, steps] = sent_bound
+            code_ref[steps] = sent_bound
 
 
 def merge_call(mine, other, top, other_top, blocks):
@@ -277,32 +280,30 @@
     fine = pairs // blocks
     rows = rows - fine
     whole = pl.BlockSpec(memory_space=pltpu.VMEM)
-    codes = jax.ShapeDtypeStruct((2, rows // (2 * fine) + 1, 2 * fine, pairs), jnp.int16)
+    codes = jax.ShapeDtypeStruct((rows // (2 * fine) + 1, 2 * fine, pairs), jnp.int16)
     near = chips // 2 - 1
     return pl.pallas_call(
         merge_kernel,
         in_specs=[whole] * 4,
-        out_specs=[whole] * (near + 1),
-        out_shape=[jax.ShapeDtypeStruct((2, rows, pairs), jnp.float32)] + [codes] * near,
+        out_specs=[whole] * (2 * near + 2),
+        out_shape=[jax.ShapeDtypeStruct((rows, pairs), jnp.float32)] * 2 + [codes] * (2 * near),
         compiler_params=pltpu.CompilerParams(vmem_limit_bytes=12 * mebibyte),
         name="merge_scores",
     )(mine, other, top, other_top)
 
 
-def half_kernel(own_ref, *refs):
-    near_refs, (sum_ref, code_ref, sums) = refs[:-3], refs[-3:]
+def half_kernel(over_ref, *refs):
+    near_refs, (code_ref, sums) = refs[:-2], refs[-2:]
     steps, deep, pairs = code_ref.shape
     steps = steps - 1
     unit = 1.0 / (code_steps * bound_steps)
-    scales = [decoded(ref[0, steps], unit) for ref in near_refs]
+    scales = [decoded(ref[steps], unit) for ref in near_refs]
 
     def add(step, top):
         there = pl.ds(pl.multiple_of(step * deep, deep), deep)
-        here, over = own_ref[0, there, :], own_ref[1, there, :]
+        over = over_ref[there, :]
         for ref, scale in zip(near_refs, scales):
-            here = here + decoded(ref[0, step], scale)
-            over = over + decoded(ref[1, step], scale)
-        sum_ref[there, :] = here
+            over = over + decoded(ref[step], scale)
         sums[there, :] = over
         return jnp.maximum(top, jnp.abs(over))
 
@@ -319,21 +320,17 @@
     code_ref[steps] = jnp.broadcast_to(bound, (deep, pairs)).astype(jnp.int32).astype(jnp.int16)
 
 
-def half_call(own, near):
-    _, rows, pairs = own.shape
+def half_call(over, near):
     whole = pl.BlockSpec(memory_space=pltpu.VMEM)
     return pl.pallas_call(
         half_kernel,
         in_specs=[whole] * (1 + len(near)),
-        out_specs=[whole, whole],
-        out_shape=[
-            jax.ShapeDtypeStruct((rows, pairs), jnp.float32),
-            jax.ShapeDtypeStruct(near[0].shape[1:], jnp.int16),
-        ],
-        scratch_shapes=[pltpu.VMEM((rows, pairs), jnp.float32)],
+        out_specs=whole,
+        out_shape=jax.ShapeDtypeStruct(near[0].shape, jnp.int16),
+        scratch_shapes=[pltpu.VMEM(over.shape, jnp.float32)],
         compiler_params=pltpu.CompilerParams(vmem_limit_bytes=8 * mebibyte),
         name="half_scores",
-    )(own, *near)
+    )(over, *near)
 
 
 def softmax_kernel(blocks, window, place_ref, own_ref, *refs):
@@ -584,10 +581,12 @@
     queries, documents, mine, other, top, own, place = score_call(
         embedded, room, devices, pairs, window
     )
-    own_scores, *codes = merge_call(mine, swapped(other, 1), top, swapped(top, 1), devices)
-    near = [swapped(codes[hop], 2 * (hop + 1)) for hop in reversed(range(len(codes)))]
-    own_scores, over = half_call(own_scores, near)
-    codes = [swapped(over, devices // 2)]
+    own_scores, over, *codes = merge_call(mine, swapped(other, 1), top, swapped(top, 1), devices)
+    hops = near_hops(devices)
+    half = len(hops)
+    far = [swapped(codes[hop // 2 - 1], hop) for hop in hops]
+    near = [swapped(codes[half + hop // 2 - 1], hop) for hop in hops]
+    codes = near + [swapped(half_call(over, far), devices // 2)]
     parts = gather_all(softmax_call(place, own_scores, codes, devices, window))
     grads, loss = grad_call(own, place, parts, queries, documents, devices, pairs, window)
     return grads, loss[0, :1]

time: 183 us -> 179 us (0.978); the launches traced: 180 us -> 179 us
  waiting for transfers between devices: 26.7 us -> 20.8 us
  starting transfers between devices: 12 us -> 16 us
    ppermute x14 -> x17, waiting for transfers between devices: 26.7 us -> 20.8 us  [swapped(): return lax.ppermute(value, 'pb', pairs)]
    ppermute x14 -> x17, starting transfers between devices: 12 us -> 16 us  [swapped(): return lax.ppermute(value, 'pb', pairs)]
  transfers between devices with their start and end apart: 14 -> 17, of which waited for: 12 -> 12; matrix products, arithmetic and copies ran while one was open for 0% -> 0% of each run, Pallas kernels for 0% -> 0%
where the time goes in v5:
time: 179 us
  blocking collectives  110 us (61%)
  Pallas kernels  29.7 us (17%)
  waiting for transfers between devices  20.8 us (12%)
  starting transfers between devices  16 us (9%)
    all_to_all x1, blocking collectives, feature_plan(): lax.all_to_all(embedding, 'pb', split_axis=0, concat_axis=0, tiled=True)  58 us
    all_to_all x1, blocking collectives, feature_plan(): lax.all_to_all(grads, 'pb', split_axis=0, concat_axis=0, tiled=True)  51.8 us
    ppermute x17, waiting for transfers between devices, swapped(): return lax.ppermute(value, 'pb', pairs)  20.8 us
    ppermute x17, starting transfers between devices, swapped(): return lax.ppermute(value, 'pb', pairs)  16 us
    pallas_call x1, Pallas kernels, grad_call(): pl.pallas_call(functools.partial(grad_kernel, blocks, pairs, window), in_...  9.1 us
    pallas_call x1, Pallas kernels, score_call(): pl.pallas_call(functools.partial(score_kernel, blocks, pairs, window), in...  8.15 us
    pallas_call x1, Pallas kernels, norm_call(): pl.pallas_call(norm_kernel, in_specs=[whole, whole, whole, whole, pl.Bloc...  5.63 us
  transfers between devices with their start and end apart: 17, of which 12 were waited for; matrix products, arithmetic and copies ran while one was open for 0% of the time, Pallas kernels for 0%

profile of v5, /device:TPU:1, one launch (start us, length us, event | category | flops | bytes accessed | tf_op | source)
XLA Modules:
  0.0 178.7 jit_solution(5460757854179533402)
XLA Ops:
  0.6 5.6 %norm_rows.1 = (bf16[256,4096]{1,0:T(8,128)(2,1)}, f32[256,128]{1,0:T(8,128)}, bf16[16,264,256]{2,1,0:T(8,128)(2,1)}) custom-call(s32[1,256]{1,0:T(1,128)} %last_ref.1, bf16[256,4096]{1,0:T(8,128)(2,1)} %hidden_ref.1, bf16[4096]{0:T(1024)(128)(2,1)} %gain_ref.1, s32[2,128]{1,0:T(2,128)} %bitcast.41, s32[1,4]{1,0:T(1,128)} %negative_ref.1), custom_call_target="tpu_custom_call" | custom-call | tf_op jit(solution)/shard_map/norm_rows/pallas_call | solution.py:90
  6.3 58.0 %all_to_all.25 = bf16[16,264,256]{2,1,0:T(8,128)(2,1)S(1)} all-to-all(bf16[16,264,256]{2,1,0:T(8,128)(2,1)} %get-tuple-element.97), channel_id=1, replica_groups=mesh['groups'=2,'pb'=16] {'pb'}, dimensions={0} | all-to-all | bytes 4325376 | tf_op jit(solution)/shard_map/all_to_all | solution.py:603
  64.3 0.6 fusion
  65.6 58.0 %conditional.1 = (bf16[16,256,256]{2,1,0:T(8,128)(2,1)S(1)}, f32[1]{0:T(128)}) conditional(s32[]{:T(128)} %clamp.3, bf16[16,264,256]{2,1,0:T(8,128)(2,1)S(1)} %all_to_all.25, bf16[16,264,256]{2,1,0:T(8,128)(2,1)S(1)} %all_to_all.25, bf16[16,264,256]{2,1,0:T(8,128)(2,1)S(1)} %all_to_all.25, ...), branch_computations={%region_1.0_spmd, %region_2.0_spmd, %region_3.0_spmd, %region_4.0_... | conditional | bytes 28099256 | solution.py:608
  65.6 8.1 %partial_scores.6 = (bf16[2048,256]{1,0:T(8,128)(2,1)S(1)}, bf16[2560,256]{1,0:T(8,128)(2,1)S(1)}, f32[8,392,128]{2,1,0:T(8,128)S(1)}, f32[8,392,128]{2,1,0:T(8,...) custom-call(bf16[16,264,256]{2,1,0:T(8,128)(2,1)S(1)} %refs_0_.1), custom_call_target="tpu_custom_call" | custom-call | tf_op jit(solution)/shard_map/cond/branch_1_fun/partial_scores/pallas_call | solution.py:210
  74.3 3.0 %collective-permute-done.18.other_top_ref = f32[8,128]{1,0:T(8,128)S(1)} collective-permute-done((f32[8,128]{1,0:T(8,128)S(1)}, f32[8,128]{1,0:T(8,128)S(1)}, u32[]{:S(2)}, u32[]{:S(2)}) %collective-permute-start.18) | collective-permute-done | bytes 4128 | tf_op jit(solution)/shard_map/cond/branch_1_fun/ppermute | solution.py:557
  77.3 1.2 merge_scores.6
  78.6 0.5 collective-permute-start.22
  79.0 1.1 collective-permute-start.23
  80.1 1.1 collective-permute-start.24
  81.7 1.1 collective-permute-start.20
  82.8 0.8 collective-permute-done.22.refs_0_
  84.0 1.0 collective-permute-done.23.refs_1_
  85.0 1.9 %collective-permute-done.24.refs_2_ = s16[25,16,128]{2,1,0:T(8,128)(2,1)S(1)} collective-permute-done((s16[25,16,128]{2,1,0:T(8,128)(2,1)S(1)}, s16[25,16,128]{2,1,0:T(8,128)(2,1)S(1)}, u32[]{:S(2)}, u32[]{:S(2)}) %collective-permute-start.24) | collective-permute-done | bytes 102432 | tf_op jit(solution)/shard_map/cond/branch_1_fun/ppermute | solution.py:557
  86.8 0.5 half_scores.6
  87.3 0.7 collective-permute-start.25
  88.0 1.3 collective-permute-done.20.refs_1_
  89.4 1.2 collective-permute-done.21.refs_2_
  90.6 2.3 %collective-permute-done.25.refs_3_ = s16[25,16,128]{2,1,0:T(8,128)(2,1)S(1)} collective-permute-done((s16[25,16,128]{2,1,0:T(8,128)(2,1)S(1)}, s16[25,16,128]{2,1,0:T(8,128)(2,1)S(1)}, u32[]{:S(2)}, u32[]{:S(2)}) %collective-permute-start.25) | collective-permute-done | bytes 102432 | tf_op jit(solution)/shard_map/cond/branch_1_fun/ppermute | solution.py:557
  92.9 1.8 %softmax_rows.6 = bf16[25,16,128]{2,1,0:T(8,128)(2,1)S(1)} custom-call(s32[5,16]{1,0:T(8,128)S(1)} %get-tuple-element.23.place_ref, f32[384,128]{1,0:T(8,128)S(1)} %get-tuple-element.29.own_ref, s16[25,16,128]{2,1,0:T(8,128)(2,1)S(1)} %collective-permute-done.19.refs_0_, s16[25,16,128]{2,1,0:T(8,128)(2,1)S(1)} %collective-permute-done.20.refs_1_, ...), custom_call_target="tpu_custom_call" | custom-call | tf_op jit(solution)/shard_map/cond/branch_1_fun/softmax_rows/pallas_call | solution.py:398
  95.2 1.3 collective-permute-start.27
  96.5 1.0 collective-permute-start.28
  97.5 2.9 %collective-permute-done.29 = bf16[1,25,16,128]{3,2,1,0:T(8,128)(2,1)S(1)} collective-permute-done((bf16[1,25,16,128]{3,2,1,0:T(8,128)(2,1)S(1)}, bf16[1,25,16,128]{3,2,1,0:T(8,128)(2,1)S(1)}, u32[]{:S(2)}, u32[]{:S(2)}) %collective-permute-start.29) | collective-permute-done | bytes 102432 | tf_op jit(solution)/shard_map/cond/branch_1_fun/ppermute | solution.py:557
  100.3 1.4 collective-permute-start.30
  101.7 1.3 collective-permute-start.32
  103.1 2.8 %collective-permute-done.30 = bf16[1,25,16,128]{3,2,1,0:T(8,128)(2,1)S(1)} collective-permute-done((bf16[1,25,16,128]{3,2,1,0:T(8,128)(2,1)S(1)}, bf16[1,25,16,128]{3,2,1,0:T(8,128)(2,1)S(1)}, u32[]{:S(2)}, u32[]{:S(2)}) %collective-permute-start.30) | collective-permute-done | bytes 102432 | tf_op jit(solution)/shard_map/cond/branch_1_fun/ppermute | solution.py:557
  105.9 1.3 collective-permute-done.31
  107.6 4.7 %collective-permute-start.33 = (bf16[8,25,16,128]{3,2,1,0:T(8,128)(2,1)S(1)}, bf16[8,25,16,128]{3,2,1,0:T(8,128)(2,1)S(1)}, u32[]{:S(2)}, u32[]{:S(2)}) collective-permute-start(bf16[8,25,16,128]{3,2,1,0:T(8,128)(2,1)S(1)} %constant_dynamic-update-slice_fusion.8.refs_0_), channel_id=1, source_target_pairs={{0,1},{1,0},{2,3},{3,2},{4,5},{5,4},{6,7},{7,6},{8,9},{9,8},{10,11... | collective-permute-start | bytes 2457608 | tf_op jit(solution)/shard_map/cond/branch_1_fun/ppermute | solution.py:557
  112.4 2.0 %collective-permute-done.33.refs_1_ = bf16[8,25,16,128]{3,2,1,0:T(8,128)(2,1)S(1)} collective-permute-done((bf16[8,25,16,128]{3,2,1,0:T(8,128)(2,1)S(1)}, bf16[8,25,16,128]{3,2,1,0:T(8,128)(2,1)S(1)}, u32[]{:S(2)}, u32[]{:S(2)}) %collective-permute-start.33) | collective-permute-done | bytes 819232 | tf_op jit(solution)/shard_map/cond/branch_1_fun/ppermute | solution.py:557
  114.3 9.1 %slice_grads.6 = (bf16[16,256,256]{2,1,0:T(8,128)(2,1)S(1)}, f32[1,128]{1,0:T(1,128)}) custom-call(s32[16,256]{1,0:T(8,128)S(1)} %get-tuple-element.22.own_ref, s32[5,16]{1,0:T(8,128)S(1)} %get-tuple-element.23.place_ref, bf16[2048,256]{1,0:T(8,128)(2,1)S(1)} %get-tuple-element.24.q_ref, bf16[2560,256]{1,0:T(8,128)(2,1)S(1)} %get-tuple-element.25.d_ref, ...), custom_call_target="tpu_custom_call" | custom-call | tf_op jit(solution)/shard_map/cond/branch_1_fun/slice_grads/pallas_call | solution.py:502
  123.6 51.8 %all_to_all.26.grad_ref = bf16[16,256,256]{2,1,0:T(8,128)(2,1)S(1)} all-to-all(bf16[16,256,256]{2,1,0:T(8,128)(2,1)S(1)} %get-tuple-element.98), channel_id=1, replica_groups=mesh['groups'=2,'pb'=16] {'pb'}, dimensions={0} | all-to-all | bytes 4194304 | tf_op jit(solution)/shard_map/all_to_all | solution.py:616
  175.4 3.3 %project_out.1 = f32[256,4096]{1,0:T(8,128)} custom-call(bf16[16,256,256]{2,1,0:T(8,128)(2,1)S(1)} %all_to_all.26.grad_ref, bf16[256,4096]{1,0:T(8,128)(2,1)S(1)} %copy-done, f32[256,128]{1,0:T(8,128)S(1)} %copy-done.1), custom_call_target="tpu_custom_call" | custom-call | tf_op jit(solution)/shard_map/project_out/pallas_call | solution.py:540
  (25 shorter events, 2.2 us)
Async XLA Ops:
  73.8 3.6 %collective-permute-start.17 = (f32[8,392,128]{2,1,0:T(8,128)S(1)}, f32[8,392,128]{2,1,0:T(8,128)S(1)}, u32[]{:S(2)}, u32[]{:S(2)}) collective-permute-start(f32[8,392,128]{2,1,0:T(8,128)S(1)} %get-tuple-element.27), channel_id=1, source_target_pairs={{0,1},{1,0},{2,3},{3,2},{4,5},{5,4},{6,7},{7,6},{8,9},{9,8},{10,11... | collective-permute-start | bytes 4816904 | tf_op jit(solution)/shard_map/cond/branch_1_fun/ppermute | solution.py:557
  74.2 3.1 %collective-permute-start.18 = (f32[8,128]{1,0:T(8,128)S(1)}, f32[8,128]{1,0:T(8,128)S(1)}, u32[]{:S(2)}, u32[]{:S(2)}) collective-permute-start(f32[8,128]{1,0:T(8,128)S(1)} %get-tuple-element.28.top_ref), channel_id=1, source_target_pairs={{0,1},{1,0},{2,3},{3,2},{4,5},{5,4},{6,7},{7,6},{8,9},{9,8},{10,11... | collective-permute-start | bytes 12296 | tf_op jit(solution)/shard_map/cond/branch_1_fun/ppermute | solution.py:557
  78.6 5.1 %collective-permute-start.22 = (s16[25,16,128]{2,1,0:T(8,128)(2,1)S(1)}, s16[25,16,128]{2,1,0:T(8,128)(2,1)S(1)}, u32[]{:S(2)}, u32[]{:S(2)}) collective-permute-start(s16[25,16,128]{2,1,0:T(8,128)(2,1)S(1)} %get-tuple-element.34), channel_id=1, source_target_pairs={{0,6},{1,7},{2,4},{3,5},{4,2},{5,3},{6,0},{7,1},{8,14},{9,15},{10,... | collective-permute-start | bytes 307208 | tf_op jit(solution)/shard_map/cond/branch_1_fun/ppermute | solution.py:557
  79.0 5.9 %collective-permute-start.23 = (s16[25,16,128]{2,1,0:T(8,128)(2,1)S(1)}, s16[25,16,128]{2,1,0:T(8,128)(2,1)S(1)}, u32[]{:S(2)}, u32[]{:S(2)}) collective-permute-start(s16[25,16,128]{2,1,0:T(8,128)(2,1)S(1)} %get-tuple-element.35), channel_id=1, source_target_pairs={{0,4},{1,5},{2,6},{3,7},{4,0},{5,1},{6,2},{7,3},{8,12},{9,13},{10,... | collective-permute-start | bytes 307208 | tf_op jit(solution)/shard_map/cond/branch_1_fun/ppermute | solution.py:557
  80.1 6.7 %collective-permute-start.24 = (s16[25,16,128]{2,1,0:T(8,128)(2,1)S(1)}, s16[25,16,128]{2,1,0:T(8,128)(2,1)S(1)}, u32[]{:S(2)}, u32[]{:S(2)}) collective-permute-start(s16[25,16,128]{2,1,0:T(8,128)(2,1)S(1)} %get-tuple-element.36), channel_id=1, source_target_pairs={{0,2},{1,3},{2,0},{3,1},{4,6},{5,7},{6,4},{7,5},{8,10},{9,11},{10,... | collective-permute-start | bytes 307208 | tf_op jit(solution)/shard_map/cond/branch_1_fun/ppermute | solution.py:557
  81.3 6.7 %collective-permute-start.19 = (s16[25,16,128]{2,1,0:T(8,128)(2,1)S(1)}, s16[25,16,128]{2,1,0:T(8,128)(2,1)S(1)}, u32[]{:S(2)}, u32[]{:S(2)}) collective-permute-start(s16[25,16,128]{2,1,0:T(8,128)(2,1)S(1)} %get-tuple-element.30), channel_id=1, source_target_pairs={{0,6},{1,7},{2,4},{3,5},{4,2},{5,3},{6,0},{7,1},{8,14},{9,15},{10,... | collective-permute-start | bytes 307208 | tf_op jit(solution)/shard_map/cond/branch_1_fun/ppermute | solution.py:557
  81.7 7.7 %collective-permute-start.20 = (s16[25,16,128]{2,1,0:T(8,128)(2,1)S(1)}, s16[25,16,128]{2,1,0:T(8,128)(2,1)S(1)}, u32[]{:S(2)}, u32[]{:S(2)}) collective-permute-start(s16[25,16,128]{2,1,0:T(8,128)(2,1)S(1)} %get-tuple-element.31), channel_id=1, source_target_pairs={{0,4},{1,5},{2,6},{3,7},{4,0},{5,1},{6,2},{7,3},{8,12},{9,13},{10,... | collective-permute-start | bytes 307208 | tf_op jit(solution)/shard_map/cond/branch_1_fun/ppermute | solution.py:557
  83.6 6.9 %collective-permute-start.21 = (s16[25,16,128]{2,1,0:T(8,128)(2,1)S(1)}, s16[25,16,128]{2,1,0:T(8,128)(2,1)S(1)}, u32[]{:S(2)}, u32[]{:S(2)}) collective-permute-start(s16[25,16,128]{2,1,0:T(8,128)(2,1)S(1)} %get-tuple-element.32), channel_id=1, source_target_pairs={{0,2},{1,3},{2,0},{3,1},{4,6},{5,7},{6,4},{7,5},{8,10},{9,11},{10,... | collective-permute-start | bytes 307208 | tf_op jit(solution)/shard_map/cond/branch_1_fun/ppermute | solution.py:557
  87.3 5.6 %collective-permute-start.25 = (s16[25,16,128]{2,1,0:T(8,128)(2,1)S(1)}, s16[25,16,128]{2,1,0:T(8,128)(2,1)S(1)}, u32[]{:S(2)}, u32[]{:S(2)}) collective-permute-start(s16[25,16,128]{2,1,0:T(8,128)(2,1)S(1)} %half_scores.6), channel_id=1, source_target_pairs={{0,8},{1,9},{2,10},{3,11},{4,12},{5,13},{6,14},{7,15},{8,0},{9,1},... | collective-permute-start | bytes 307208 | tf_op jit(solution)/shard_map/cond/branch_1_fun/ppermute | solution.py:557
  94.7 7.0 %collective-permute-start.26 = (bf16[1,25,16,128]{3,2,1,0:T(8,128)(2,1)S(1)}, bf16[1,25,16,128]{3,2,1,0:T(8,128)(2,1)S(1)}, u32[]{:S(2)}, u32[]{:S(2)}) collective-permute-start(bf16[1,25,16,128]{3,2,1,0:T(8,128)(2,1)S(1)} %bitcast.33), channel_id=1, source_target_pairs={{0,6},{1,7},{2,4},{3,5},{4,2},{5,3},{6,0},{7,1},{8,14},{9,15},{10,... | collective-permute-start | bytes 307208 | tf_op jit(solution)/shard_map/cond/branch_1_fun/ppermute | solution.py:557
  94.8 5.6 %collective-permute-start.29 = (bf16[1,25,16,128]{3,2,1,0:T(8,128)(2,1)S(1)}, bf16[1,25,16,128]{3,2,1,0:T(8,128)(2,1)S(1)}, u32[]{:S(2)}, u32[]{:S(2)}) collective-permute-start(bf16[1,25,16,128]{3,2,1,0:T(8,128)(2,1)S(1)} %bitcast.34), channel_id=1, source_target_pairs={{0,8},{1,9},{2,10},{3,11},{4,12},{5,13},{6,14},{7,15},{8,0},{9,1},... | collective-permute-start | bytes 307208 | tf_op jit(solution)/shard_map/cond/branch_1_fun/ppermute | solution.py:557
  95.2 7.8 %collective-permute-start.27 = (bf16[1,25,16,128]{3,2,1,0:T(8,128)(2,1)S(1)}, bf16[1,25,16,128]{3,2,1,0:T(8,128)(2,1)S(1)}, u32[]{:S(2)}, u32[]{:S(2)}) collective-permute-start(bf16[1,25,16,128]{3,2,1,0:T(8,128)(2,1)S(1)} %bitcast.35), channel_id=1, source_target_pairs={{0,4},{1,5},{2,6},{3,7},{4,0},{5,1},{6,2},{7,3},{8,12},{9,13},{10,... | collective-permute-start | bytes 307208 | tf_op jit(solution)/shard_map/cond/branch_1_fun/ppermute | solution.py:557
  96.5 6.5 %collective-permute-start.28 = (bf16[1,25,16,128]{3,2,1,0:T(8,128)(2,1)S(1)}, bf16[1,25,16,128]{3,2,1,0:T(8,128)(2,1)S(1)}, u32[]{:S(2)}, u32[]{:S(2)}) collective-permute-start(bf16[1,25,16,128]{3,2,1,0:T(8,128)(2,1)S(1)} %bitcast.36), channel_id=1, source_target_pairs={{0,2},{1,3},{2,0},{3,1},{4,6},{5,7},{6,4},{7,5},{8,10},{9,11},{10,... | collective-permute-start | bytes 307208 | tf_op jit(solution)/shard_map/cond/branch_1_fun/ppermute | solution.py:557
  100.3 5.6 %collective-permute-start.30 = (bf16[1,25,16,128]{3,2,1,0:T(8,128)(2,1)S(1)}, bf16[1,25,16,128]{3,2,1,0:T(8,128)(2,1)S(1)}, u32[]{:S(2)}, u32[]{:S(2)}) collective-permute-start(bf16[1,25,16,128]{3,2,1,0:T(8,128)(2,1)S(1)} %collective-permute-done.29), channel_id=1, source_target_pairs={{0,6},{1,7},{2,4},{3,5},{4,2},{5,3},{6,0},{7,1},{8,14},{9,15},{10,... | collective-permute-start | bytes 307208 | tf_op jit(solution)/shard_map/cond/branch_1_fun/ppermute | solution.py:557
  101.7 5.6 %collective-permute-start.31 = (bf16[1,25,16,128]{3,2,1,0:T(8,128)(2,1)S(1)}, bf16[1,25,16,128]{3,2,1,0:T(8,128)(2,1)S(1)}, u32[]{:S(2)}, u32[]{:S(2)}) collective-permute-start(bf16[1,25,16,128]{3,2,1,0:T(8,128)(2,1)S(1)} %collective-permute-done.29), channel_id=1, source_target_pairs={{0,4},{1,5},{2,6},{3,7},{4,0},{5,1},{6,2},{7,3},{8,12},{9,13},{10,... | collective-permute-start | bytes 307208 | tf_op jit(solution)/shard_map/cond/branch_1_fun/ppermute | solution.py:557
  101.7 5.9 %collective-permute-start.32 = (bf16[1,25,16,128]{3,2,1,0:T(8,128)(2,1)S(1)}, bf16[1,25,16,128]{3,2,1,0:T(8,128)(2,1)S(1)}, u32[]{:S(2)}, u32[]{:S(2)}) collective-permute-start(bf16[1,25,16,128]{3,2,1,0:T(8,128)(2,1)S(1)} %collective-permute-done.29), channel_id=1, source_target_pairs={{0,2},{1,3},{2,0},{3,1},{4,6},{5,7},{6,4},{7,5},{8,10},{9,11},{10,... | collective-permute-start | bytes 307208 | tf_op jit(solution)/shard_map/cond/branch_1_fun/ppermute | solution.py:557
  107.6 6.7 %collective-permute-start.33 = (bf16[8,25,16,128]{3,2,1,0:T(8,128)(2,1)S(1)}, bf16[8,25,16,128]{3,2,1,0:T(8,128)(2,1)S(1)}, u32[]{:S(2)}, u32[]{:S(2)}) collective-permute-start(bf16[8,25,16,128]{3,2,1,0:T(8,128)(2,1)S(1)} %constant_dynamic-update-slice_fusion.8.refs_0_), channel_id=1, source_target_pairs={{0,1},{1,0},{2,3},{3,2},{4,5},{5,4},{6,7},{7,6},{8,9},{9,8},{10,11... | collective-permute-start | bytes 2457608 | tf_op jit(solution)/shard_map/cond/branch_1_fun/ppermute | solution.py:557
  123.6 51.8 %copy-start = (bf16[256,4096]{1,0:T(8,128)(2,1)S(1)}, bf16[256,4096]{1,0:T(8,128)(2,1)}, u32[]{:S(2)}) copy-start(bf16[256,4096]{1,0:T(8,128)(2,1)} %get-tuple-element.99.normed_ref) | copy-start | bytes 6291460
  123.6 51.8 %copy-start.1 = (f32[256,128]{1,0:T(8,128)S(1)}, f32[256,128]{1,0:T(8,128)}, u32[]{:S(2)}) copy-start(f32[256,128]{1,0:T(8,128)} %get-tuple-element.100.inv_ref) | copy-start | bytes 393220

commit v6 on v5

--- a/solution.py
+++ b/solution.py
@@ -563,18 +563,19 @@
 
 def swap_masks(devices):
     near = [0] + near_hops(devices)
-    held = near + [mask ^ (devices // 2) for mask in near]
-    return [held, [mask ^ 1 for mask in held]]
+    held = [near, [mask ^ (devices // 2) for mask in near]]
+    return held + [[mask ^ 1 for mask in part] for part in held]
 
 
 def gather_all(value):
     devices = lax.axis_size("pb")
     own = value[None]
     across = swapped(own, devices // 2)
-    held = [own] + [swapped(own, hop) for hop in near_hops(devices)]
-    held += [across] + [swapped(across, hop) for hop in near_hops(devices)]
-    held = jnp.concatenate(held, axis=0)
-    return [held, swapped(held, 1)]
+    held = [
+        jnp.concatenate([part] + [swapped(part, hop) for hop in near_hops(devices)], axis=0)
+        for part in (own, across)
+    ]
+    return held + [swapped(part, 1) for part in held]
 
 
 def middle(embedded, room, devices, pairs, window):

time: 179 us -> 182 us (1.017)
  starting transfers between devices: 16 us -> 19.8 us
    ppermute x17 -> x18, starting transfers between devices: 16 us -> 19.8 us  [swapped(): return lax.ppermute(value, 'pb', pairs)]
    ppermute x17 -> x18, waiting for transfers between devices: 20.8 us -> 20.8 us  [swapped(): return lax.ppermute(value, 'pb', pairs)]
  transfers between devices with their start and end apart: 17 -> 18, of which waited for: 12 -> 14; matrix products, arithmetic and copies ran while one was open for 0% -> 0% of each run, Pallas kernels for 0% -> 0%
where the time goes in v6:
time: 182 us
  blocking collectives  109 us (60%)
  Pallas kernels  29.9 us (16%)
  waiting for transfers between devices  20.8 us (11%)
  starting transfers between devices  19.8 us (11%)
    all_to_all x1, blocking collectives, feature_plan(): lax.all_to_all(embedding, 'pb', split_axis=0, concat_axis=0, tiled=True)  58 us
    all_to_all x1, blocking collectives, feature_plan(): lax.all_to_all(grads, 'pb', split_axis=0, concat_axis=0, tiled=True)  51.1 us
    ppermute x18, waiting for transfers between devices, swapped(): return lax.ppermute(value, 'pb', pairs)  20.8 us
    ppermute x18, starting transfers between devices, swapped(): return lax.ppermute(value, 'pb', pairs)  19.8 us
    pallas_call x1, Pallas kernels, grad_call(): pl.pallas_call(functools.partial(grad_kernel, blocks, pairs, window), in_...  9.16 us
    pallas_call x1, Pallas kernels, score_call(): pl.pallas_call(functools.partial(score_kernel, blocks, pairs, window), in...  8.15 us
    pallas_call x1, Pallas kernels, norm_call(): pl.pallas_call(norm_kernel, in_specs=[whole, whole, whole, whole, pl.Bloc...  5.63 us
  transfers between devices with their start and end apart: 18, of which 14 were waited for; matrix products, arithmetic and copies ran while one was open for 0% of the time, Pallas kernels for 0%

profile of v6, /device:TPU:1, one launch (start us, length us, event | category | flops | bytes accessed | tf_op | source)
XLA Modules:
  0.0 182.0 jit_solution(10639133762049196352)
XLA Ops:
  0.6 5.6 %norm_rows.1 = (bf16[256,4096]{1,0:T(8,128)(2,1)}, f32[256,128]{1,0:T(8,128)}, bf16[16,264,256]{2,1,0:T(8,128)(2,1)}) custom-call(s32[1,256]{1,0:T(1,128)} %last_ref.1, bf16[256,4096]{1,0:T(8,128)(2,1)} %hidden_ref.1, bf16[4096]{0:T(1024)(128)(2,1)} %gain_ref.1, s32[2,128]{1,0:T(2,128)} %bitcast.41, s32[1,4]{1,0:T(1,128)} %negative_ref.1), custom_call_target="tpu_custom_call" | custom-call | tf_op jit(solution)/shard_map/norm_rows/pallas_call | solution.py:90
  6.3 58.0 %all_to_all.25 = bf16[16,264,256]{2,1,0:T(8,128)(2,1)S(1)} all-to-all(bf16[16,264,256]{2,1,0:T(8,128)(2,1)} %get-tuple-element.97), channel_id=1, replica_groups=mesh['groups'=2,'pb'=16] {'pb'}, dimensions={0} | all-to-all | bytes 4325376 | tf_op jit(solution)/shard_map/all_to_all | solution.py:604
  64.3 0.6 fusion
  65.6 62.0 %conditional.1 = (bf16[16,256,256]{2,1,0:T(8,128)(2,1)S(1)}, f32[1]{0:T(128)}) conditional(s32[]{:T(128)} %clamp.3, bf16[16,264,256]{2,1,0:T(8,128)(2,1)S(1)} %all_to_all.25, bf16[16,264,256]{2,1,0:T(8,128)(2,1)S(1)} %all_to_all.25, bf16[16,264,256]{2,1,0:T(8,128)(2,1)S(1)} %all_to_all.25, ...), branch_computations={%region_1.0_spmd, %region_2.0_spmd, %region_3.0_spmd, %region_4.0_... | conditional | flops 1007616 | bytes 28099296 | solution.py:609
  65.8 8.1 %partial_scores.7 = (bf16[2048,256]{1,0:T(8,128)(2,1)S(1)}, bf16[2560,256]{1,0:T(8,128)(2,1)S(1)}, f32[8,424,128]{2,1,0:T(8,128)S(1)}, f32[8,424,128]{2,1,0:T(8,...) custom-call(bf16[16,264,256]{2,1,0:T(8,128)(2,1)S(1)} %refs_0_.2), custom_call_target="tpu_custom_call" | custom-call | tf_op jit(solution)/shard_map/cond/branch_2_fun/partial_scores/pallas_call | solution.py:210
  74.5 3.2 %collective-permute-done.37.other_top_ref = f32[8,128]{1,0:T(8,128)S(1)} collective-permute-done((f32[8,128]{1,0:T(8,128)S(1)}, f32[8,128]{1,0:T(8,128)S(1)}, u32[]{:S(2)}, u32[]{:S(2)}) %collective-permute-start.37) | collective-permute-done | bytes 4128 | tf_op jit(solution)/shard_map/cond/branch_2_fun/ppermute | solution.py:557
  77.7 1.3 merge_scores.7
  79.5 1.1 collective-permute-start.42
  80.6 1.1 collective-permute-start.43
  82.2 1.1 collective-permute-start.39
  83.3 1.0 collective-permute-done.41.refs_0_
  84.6 1.2 collective-permute-done.42.refs_1_
  85.8 2.0 %collective-permute-done.43.refs_2_ = s16[27,16,128]{2,1,0:T(8,128)(2,1)S(1)} collective-permute-done((s16[27,16,128]{2,1,0:T(8,128)(2,1)S(1)}, s16[27,16,128]{2,1,0:T(8,128)(2,1)S(1)}, u32[]{:S(2)}, u32[]{:S(2)}) %collective-permute-start.43) | collective-permute-done | bytes 110624 | tf_op jit(solution)/shard_map/cond/branch_2_fun/ppermute | solution.py:557
  88.3 0.7 collective-permute-start.44
  89.1 1.5 collective-permute-done.39.refs_1_
  90.5 1.4 collective-permute-done.40.refs_2_
  91.9 2.2 %collective-permute-done.44.refs_3_ = s16[27,16,128]{2,1,0:T(8,128)(2,1)S(1)} collective-permute-done((s16[27,16,128]{2,1,0:T(8,128)(2,1)S(1)}, s16[27,16,128]{2,1,0:T(8,128)(2,1)S(1)}, u32[]{:S(2)}, u32[]{:S(2)}) %collective-permute-start.44) | collective-permute-done | bytes 110624 | tf_op jit(solution)/shard_map/cond/branch_2_fun/ppermute | solution.py:557
  94.1 1.8 %softmax_rows.7 = bf16[27,16,128]{2,1,0:T(8,128)(2,1)S(1)} custom-call(s32[5,16]{1,0:T(8,128)S(1)} %get-tuple-element.40.place_ref, f32[416,128]{1,0:T(8,128)S(1)} %get-tuple-element.46.own_ref, s16[27,16,128]{2,1,0:T(8,128)(2,1)S(1)} %collective-permute-done.38.refs_0_, s16[27,16,128]{2,1,0:T(8,128)(2,1)S(1)} %collective-permute-done.39.refs_1_, ...), custom_call_target="tpu_custom_call" | custom-call | tf_op jit(solution)/shard_map/cond/branch_2_fun/softmax_rows/pallas_call | solution.py:398
  96.1 2.6 %collective-permute-start.45 = (bf16[1,27,16,128]{3,2,1,0:T(8,128)(2,1)S(1)}, bf16[1,27,16,128]{3,2,1,0:T(8,128)(2,1)S(1)}, u32[]{:S(2)}, u32[]{:S(2)}) collective-permute-start(bf16[1,27,16,128]{3,2,1,0:T(8,128)(2,1)S(1)} %bitcast.28), channel_id=1, source_target_pairs={{0,6},{1,7},{2,4},{3,5},{4,2},{5,3},{6,0},{7,1},{8,14},{9,15},{10,... | collective-permute-start | bytes 331784 | tf_op jit(solution)/shard_map/cond/branch_2_fun/ppermute | solution.py:557
  98.6 0.9 collective-permute-done.47
  99.6 2.3 %collective-permute-done.45 = bf16[1,27,16,128]{3,2,1,0:T(8,128)(2,1)S(1)} collective-permute-done((bf16[1,27,16,128]{3,2,1,0:T(8,128)(2,1)S(1)}, bf16[1,27,16,128]{3,2,1,0:T(8,128)(2,1)S(1)}, u32[]{:S(2)}, u32[]{:S(2)}) %collective-permute-start.45) | collective-permute-done | bytes 110624 | tf_op jit(solution)/shard_map/cond/branch_2_fun/ppermute | solution.py:557
  102.0 5.2 %collective-permute-start.52 = (bf16[4,27,16,128]{3,2,1,0:T(8,128)(2,1)S(1)}, bf16[4,27,16,128]{3,2,1,0:T(8,128)(2,1)S(1)}, u32[]{:S(2)}, u32[]{:S(2)}) collective-permute-start(bf16[4,27,16,128]{3,2,1,0:T(8,128)(2,1)S(1)} %pad_maximum_fusion.2.refs_0_), channel_id=1, source_target_pairs={{0,1},{1,0},{2,3},{3,2},{4,5},{5,4},{6,7},{7,6},{8,9},{9,8},{10,11... | collective-permute-start | bytes 1327112 | tf_op jit(solution)/shard_map/cond/branch_2_fun/ppermute | solution.py:557
  107.2 0.9 collective-permute-start.49
  108.1 1.5 collective-permute-start.50
  109.9 1.8 %collective-permute-done.49 = bf16[1,27,16,128]{3,2,1,0:T(8,128)(2,1)S(1)} collective-permute-done((bf16[1,27,16,128]{3,2,1,0:T(8,128)(2,1)S(1)}, bf16[1,27,16,128]{3,2,1,0:T(8,128)(2,1)S(1)}, u32[]{:S(2)}, u32[]{:S(2)}) %collective-permute-start.49) | collective-permute-done | bytes 110624 | tf_op jit(solution)/shard_map/cond/branch_2_fun/ppermute | solution.py:557
  111.7 1.2 collective-permute-done.50
  113.0 0.6 collective-permute-done.51
  113.5 3.5 %collective-permute-start.53 = (bf16[4,27,16,128]{3,2,1,0:T(8,128)(2,1)S(1)}, bf16[4,27,16,128]{3,2,1,0:T(8,128)(2,1)S(1)}, u32[]{:S(2)}, u32[]{:S(2)}) collective-permute-start(bf16[4,27,16,128]{3,2,1,0:T(8,128)(2,1)S(1)} %constant_dynamic-update-slice_fusion.8.refs_1_), channel_id=1, source_target_pairs={{0,1},{1,0},{2,3},{3,2},{4,5},{5,4},{6,7},{7,6},{8,9},{9,8},{10,11... | collective-permute-start | bytes 1327112 | tf_op jit(solution)/shard_map/cond/branch_2_fun/ppermute | solution.py:557
  117.0 1.4 collective-permute-done.53.refs_3_
  118.4 9.2 %slice_grads.7 = (bf16[16,256,256]{2,1,0:T(8,128)(2,1)S(1)}, f32[1,128]{1,0:T(1,128)}) custom-call(s32[16,256]{1,0:T(8,128)S(1)} %get-tuple-element.39.own_ref, s32[5,16]{1,0:T(8,128)S(1)} %get-tuple-element.40.place_ref, bf16[2048,256]{1,0:T(8,128)(2,1)S(1)} %get-tuple-element.41.q_ref, bf16[2560,256]{1,0:T(8,128)(2,1)S(1)} %get-tuple-element.42.d_ref, ...), custom_call_target="tpu_custom_call" | custom-call | tf_op jit(solution)/shard_map/cond/branch_2_fun/slice_grads/pallas_call | solution.py:502
  127.6 51.1 %all_to_all.26.grad_ref = bf16[16,256,256]{2,1,0:T(8,128)(2,1)S(1)} all-to-all(bf16[16,256,256]{2,1,0:T(8,128)(2,1)S(1)} %get-tuple-element.98), channel_id=1, replica_groups=mesh['groups'=2,'pb'=16] {'pb'}, dimensions={0} | all-to-all | bytes 4194304 | tf_op jit(solution)/shard_map/all_to_all | solution.py:617
  178.7 3.3 %project_out.1 = f32[256,4096]{1,0:T(8,128)} custom-call(bf16[16,256,256]{2,1,0:T(8,128)(2,1)S(1)} %all_to_all.26.grad_ref, bf16[256,4096]{1,0:T(8,128)(2,1)S(1)} %copy-done, f32[256,128]{1,0:T(8,128)S(1)} %copy-done.1), custom_call_target="tpu_custom_call" | custom-call | tf_op jit(solution)/shard_map/project_out/pallas_call | solution.py:540
  (24 shorter events, 2.9 us)
Async XLA Ops:
  74.0 3.8 %collective-permute-start.36 = (f32[8,424,128]{2,1,0:T(8,128)S(1)}, f32[8,424,128]{2,1,0:T(8,128)S(1)}, u32[]{:S(2)}, u32[]{:S(2)}) collective-permute-start(f32[8,424,128]{2,1,0:T(8,128)S(1)} %get-tuple-element.44), channel_id=1, source_target_pairs={{0,1},{1,0},{2,3},{3,2},{4,5},{5,4},{6,7},{7,6},{8,9},{9,8},{10,11... | collective-permute-start | bytes 5210120 | tf_op jit(solution)/shard_map/cond/branch_2_fun/ppermute | solution.py:557
  74.4 3.3 %collective-permute-start.37 = (f32[8,128]{1,0:T(8,128)S(1)}, f32[8,128]{1,0:T(8,128)S(1)}, u32[]{:S(2)}, u32[]{:S(2)}) collective-permute-start(f32[8,128]{1,0:T(8,128)S(1)} %get-tuple-element.45.top_ref), channel_id=1, source_target_pairs={{0,1},{1,0},{2,3},{3,2},{4,5},{5,4},{6,7},{7,6},{8,9},{9,8},{10,11... | collective-permute-start | bytes 12296 | tf_op jit(solution)/shard_map/cond/branch_2_fun/ppermute | solution.py:557
  79.0 5.2 %collective-permute-start.41 = (s16[27,16,128]{2,1,0:T(8,128)(2,1)S(1)}, s16[27,16,128]{2,1,0:T(8,128)(2,1)S(1)}, u32[]{:S(2)}, u32[]{:S(2)}) collective-permute-start(s16[27,16,128]{2,1,0:T(8,128)(2,1)S(1)} %get-tuple-element.51), channel_id=1, source_target_pairs={{0,6},{1,7},{2,4},{3,5},{4,2},{5,3},{6,0},{7,1},{8,14},{9,15},{10,... | collective-permute-start | bytes 331784 | tf_op jit(solution)/shard_map/cond/branch_2_fun/ppermute | solution.py:557
  79.5 6.3 %collective-permute-start.42 = (s16[27,16,128]{2,1,0:T(8,128)(2,1)S(1)}, s16[27,16,128]{2,1,0:T(8,128)(2,1)S(1)}, u32[]{:S(2)}, u32[]{:S(2)}) collective-permute-start(s16[27,16,128]{2,1,0:T(8,128)(2,1)S(1)} %get-tuple-element.52), channel_id=1, source_target_pairs={{0,4},{1,5},{2,6},{3,7},{4,0},{5,1},{6,2},{7,3},{8,12},{9,13},{10,... | collective-permute-start | bytes 331784 | tf_op jit(solution)/shard_map/cond/branch_2_fun/ppermute | solution.py:557
  80.6 7.2 %collective-permute-start.43 = (s16[27,16,128]{2,1,0:T(8,128)(2,1)S(1)}, s16[27,16,128]{2,1,0:T(8,128)(2,1)S(1)}, u32[]{:S(2)}, u32[]{:S(2)}) collective-permute-start(s16[27,16,128]{2,1,0:T(8,128)(2,1)S(1)} %get-tuple-element.53), channel_id=1, source_target_pairs={{0,2},{1,3},{2,0},{3,1},{4,6},{5,7},{6,4},{7,5},{8,10},{9,11},{10,... | collective-permute-start | bytes 331784 | tf_op jit(solution)/shard_map/cond/branch_2_fun/ppermute | solution.py:557
  81.8 7.3 %collective-permute-start.38 = (s16[27,16,128]{2,1,0:T(8,128)(2,1)S(1)}, s16[27,16,128]{2,1,0:T(8,128)(2,1)S(1)}, u32[]{:S(2)}, u32[]{:S(2)}) collective-permute-start(s16[27,16,128]{2,1,0:T(8,128)(2,1)S(1)} %get-tuple-element.47), channel_id=1, source_target_pairs={{0,6},{1,7},{2,4},{3,5},{4,2},{5,3},{6,0},{7,1},{8,14},{9,15},{10,... | collective-permute-start | bytes 331784 | tf_op jit(solution)/shard_map/cond/branch_2_fun/ppermute | solution.py:557
  82.2 8.4 %collective-permute-start.39 = (s16[27,16,128]{2,1,0:T(8,128)(2,1)S(1)}, s16[27,16,128]{2,1,0:T(8,128)(2,1)S(1)}, u32[]{:S(2)}, u32[]{:S(2)}) collective-permute-start(s16[27,16,128]{2,1,0:T(8,128)(2,1)S(1)} %get-tuple-element.48), channel_id=1, source_target_pairs={{0,4},{1,5},{2,6},{3,7},{4,0},{5,1},{6,2},{7,3},{8,12},{9,13},{10,... | collective-permute-start | bytes 331784 | tf_op jit(solution)/shard_map/cond/branch_2_fun/ppermute | solution.py:557
  84.3 7.6 %collective-permute-start.40 = (s16[27,16,128]{2,1,0:T(8,128)(2,1)S(1)}, s16[27,16,128]{2,1,0:T(8,128)(2,1)S(1)}, u32[]{:S(2)}, u32[]{:S(2)}) collective-permute-start(s16[27,16,128]{2,1,0:T(8,128)(2,1)S(1)} %get-tuple-element.49), channel_id=1, source_target_pairs={{0,2},{1,3},{2,0},{3,1},{4,6},{5,7},{6,4},{7,5},{8,10},{9,11},{10,... | collective-permute-start | bytes 331784 | tf_op jit(solution)/shard_map/cond/branch_2_fun/ppermute | solution.py:557
  88.3 5.7 %collective-permute-start.44 = (s16[27,16,128]{2,1,0:T(8,128)(2,1)S(1)}, s16[27,16,128]{2,1,0:T(8,128)(2,1)S(1)}, u32[]{:S(2)}, u32[]{:S(2)}) collective-permute-start(s16[27,16,128]{2,1,0:T(8,128)(2,1)S(1)} %half_scores.7), channel_id=1, source_target_pairs={{0,8},{1,9},{2,10},{3,11},{4,12},{5,13},{6,14},{7,15},{8,0},{9,1},... | collective-permute-start | bytes 331784 | tf_op jit(solution)/shard_map/cond/branch_2_fun/ppermute | solution.py:557
  95.9 3.7 %collective-permute-start.47 = (bf16[1,27,16,128]{3,2,1,0:T(8,128)(2,1)S(1)}, bf16[1,27,16,128]{3,2,1,0:T(8,128)(2,1)S(1)}, u32[]{:S(2)}, u32[]{:S(2)}) collective-permute-start(bf16[1,27,16,128]{3,2,1,0:T(8,128)(2,1)S(1)} %bitcast.26), channel_id=1, source_target_pairs={{0,2},{1,3},{2,0},{3,1},{4,6},{5,7},{6,4},{7,5},{8,10},{9,11},{10,... | collective-permute-start | bytes 331784 | tf_op jit(solution)/shard_map/cond/branch_2_fun/ppermute | solution.py:557
  96.0 3.7 %collective-permute-start.46 = (bf16[1,27,16,128]{3,2,1,0:T(8,128)(2,1)S(1)}, bf16[1,27,16,128]{3,2,1,0:T(8,128)(2,1)S(1)}, u32[]{:S(2)}, u32[]{:S(2)}) collective-permute-start(bf16[1,27,16,128]{3,2,1,0:T(8,128)(2,1)S(1)} %bitcast.27), channel_id=1, source_target_pairs={{0,4},{1,5},{2,6},{3,7},{4,0},{5,1},{6,2},{7,3},{8,12},{9,13},{10,... | collective-permute-start | bytes 331784 | tf_op jit(solution)/shard_map/cond/branch_2_fun/ppermute | solution.py:557
  96.1 5.9 %collective-permute-start.45 = (bf16[1,27,16,128]{3,2,1,0:T(8,128)(2,1)S(1)}, bf16[1,27,16,128]{3,2,1,0:T(8,128)(2,1)S(1)}, u32[]{:S(2)}, u32[]{:S(2)}) collective-permute-start(bf16[1,27,16,128]{3,2,1,0:T(8,128)(2,1)S(1)} %bitcast.28), channel_id=1, source_target_pairs={{0,6},{1,7},{2,4},{3,5},{4,2},{5,3},{6,0},{7,1},{8,14},{9,15},{10,... | collective-permute-start | bytes 331784 | tf_op jit(solution)/shard_map/cond/branch_2_fun/ppermute | solution.py:557
  98.6 8.6 %collective-permute-start.48 = (bf16[1,27,16,128]{3,2,1,0:T(8,128)(2,1)S(1)}, bf16[1,27,16,128]{3,2,1,0:T(8,128)(2,1)S(1)}, u32[]{:S(2)}, u32[]{:S(2)}) collective-permute-start(bf16[1,27,16,128]{3,2,1,0:T(8,128)(2,1)S(1)} %bitcast.29), channel_id=1, source_target_pairs={{0,8},{1,9},{2,10},{3,11},{4,12},{5,13},{6,14},{7,15},{8,0},{9,1},... | collective-permute-start | bytes 331784 | tf_op jit(solution)/shard_map/cond/branch_2_fun/ppermute | solution.py:557
  102.0 15.0 %collective-permute-start.52 = (bf16[4,27,16,128]{3,2,1,0:T(8,128)(2,1)S(1)}, bf16[4,27,16,128]{3,2,1,0:T(8,128)(2,1)S(1)}, u32[]{:S(2)}, u32[]{:S(2)}) collective-permute-start(bf16[4,27,16,128]{3,2,1,0:T(8,128)(2,1)S(1)} %pad_maximum_fusion.2.refs_0_), channel_id=1, source_target_pairs={{0,1},{1,0},{2,3},{3,2},{4,5},{5,4},{6,7},{7,6},{8,9},{9,8},{10,11... | collective-permute-start | bytes 1327112 | tf_op jit(solution)/shard_map/cond/branch_2_fun/ppermute | solution.py:557
  107.2 4.5 %collective-permute-start.49 = (bf16[1,27,16,128]{3,2,1,0:T(8,128)(2,1)S(1)}, bf16[1,27,16,128]{3,2,1,0:T(8,128)(2,1)S(1)}, u32[]{:S(2)}, u32[]{:S(2)}) collective-permute-start(bf16[1,27,16,128]{3,2,1,0:T(8,128)(2,1)S(1)} %collective-permute-done.48), channel_id=1, source_target_pairs={{0,6},{1,7},{2,4},{3,5},{4,2},{5,3},{6,0},{7,1},{8,14},{9,15},{10,... | collective-permute-start | bytes 331784 | tf_op jit(solution)/shard_map/cond/branch_2_fun/ppermute | solution.py:557
  108.1 4.8 %collective-permute-start.50 = (bf16[1,27,16,128]{3,2,1,0:T(8,128)(2,1)S(1)}, bf16[1,27,16,128]{3,2,1,0:T(8,128)(2,1)S(1)}, u32[]{:S(2)}, u32[]{:S(2)}) collective-permute-start(bf16[1,27,16,128]{3,2,1,0:T(8,128)(2,1)S(1)} %collective-permute-done.48), channel_id=1, source_target_pairs={{0,4},{1,5},{2,6},{3,7},{4,0},{5,1},{6,2},{7,3},{8,12},{9,13},{10,... | collective-permute-start | bytes 331784 | tf_op jit(solution)/shard_map/cond/branch_2_fun/ppermute | solution.py:557
  109.6 3.9 %collective-permute-start.51 = (bf16[1,27,16,128]{3,2,1,0:T(8,128)(2,1)S(1)}, bf16[1,27,16,128]{3,2,1,0:T(8,128)(2,1)S(1)}, u32[]{:S(2)}, u32[]{:S(2)}) collective-permute-start(bf16[1,27,16,128]{3,2,1,0:T(8,128)(2,1)S(1)} %collective-permute-done.48), channel_id=1, source_target_pairs={{0,2},{1,3},{2,0},{3,1},{4,6},{5,7},{6,4},{7,5},{8,10},{9,11},{10,... | collective-permute-start | bytes 331784 | tf_op jit(solution)/shard_map/cond/branch_2_fun/ppermute | solution.py:557
  113.5 4.9 %collective-permute-start.53 = (bf16[4,27,16,128]{3,2,1,0:T(8,128)(2,1)S(1)}, bf16[4,27,16,128]{3,2,1,0:T(8,128)(2,1)S(1)}, u32[]{:S(2)}, u32[]{:S(2)}) collective-permute-start(bf16[4,27,16,128]{3,2,1,0:T(8,128)(2,1)S(1)} %constant_dynamic-update-slice_fusion.8.refs_1_), channel_id=1, source_target_pairs={{0,1},{1,0},{2,3},{3,2},{4,5},{5,4},{6,7},{7,6},{8,9},{9,8},{10,11... | collective-permute-start | bytes 1327112 | tf_op jit(solution)/shard_map/cond/branch_2_fun/ppermute | solution.py:557
  127.6 51.1 %copy-start = (bf16[256,4096]{1,0:T(8,128)(2,1)S(1)}, bf16[256,4096]{1,0:T(8,128)(2,1)}, u32[]{:S(2)}) copy-start(bf16[256,4096]{1,0:T(8,128)(2,1)} %get-tuple-element.99.normed_ref) | copy-start | bytes 6291460
  127.6 51.1 %copy-start.1 = (f32[256,128]{1,0:T(8,128)S(1)}, f32[256,128]{1,0:T(8,128)}, u32[]{:S(2)}) copy-start(f32[256,128]{1,0:T(8,128)} %get-tuple-element.100.inv_ref) | copy-start | bytes 393220
